TPU v7x, 32 devices: a whole 2x2x4 slice. The times are simulated.
32 devices in a mesh: dp: 4 (over y, x), edge: 8 (over z, core).
Axes of the slice: x: 2, y: 2, z: 4, core: 2. Of those that a mesh axis runs over, the one named last changes fastest.
Arguments:
- nodes: bfloat16 [4096, 512], P(('dp', 'edge')), parts along dimension 0, may hold values from -6 to 6
- edges: bfloat16 [4096, 9984], P(('dp', 'edge')), parts along dimension 0, may hold values from -6 to 6
- nbr_owner: int32 [4096, 52, 1], P(('dp', 'edge')), parts along dimension 0, may hold values from 0 to 7; in each aligned block of 6656 rows (0 to 6655, 6656 to 13311, ..., all dimensions but the last counted through in order) at most 1664 rows name the same one
- nbr_slot: int32 [4096, 52], P(('dp', 'edge')), parts along dimension 0, may hold values from 0 to 127
- edge_mask: int32 [4096, 52], P(('dp', 'edge')), parts along dimension 0, may hold values 0 or 1
- w_msg1: bfloat16 [1216, 512], replicated, may hold values from -0.15625 to 0.15625
- w_msg2: bfloat16 [512, 512], replicated, may hold values from -0.25 to 0.25
- w_msg3: bfloat16 [512, 512], replicated, may hold values from -1.25 to 1.25
- gain_one: float32 [512], replicated, may hold values from 0.1 to 1.9
- offset_one: float32 [512], replicated, may hold values from -3 to 3
- w_ffn1: bfloat16 [512, 2048], replicated, may hold values from -0.25 to 0.25
- w_ffn2: bfloat16 [2048, 512], replicated, may hold values from -0.125 to 0.125
- gain_two: float32 [512], replicated, may hold values from 0.1 to 1.9
- offset_two: float32 [512], replicated, may hold values from -3 to 3
- w_edge1: bfloat16 [1216, 192], replicated, may hold values from -0.15625 to 0.15625
- w_edge2: bfloat16 [192, 192], replicated, may hold values from -0.4375 to 0.4375
- w_edge3: bfloat16 [192, 192], replicated, may hold values from -0.4375 to 0.4375
- gain_three: float32 [192], replicated, may hold values from 0.1 to 1.9
- offset_three: float32 [192], replicated, may hold values from -3 to 3
- node_cotangent: bfloat16 [4096, 512], P(('dp', 'edge')), parts along dimension 0, may hold values from -6 to 6
- edge_cotangent: bfloat16 [4096, 9984], P(('dp', 'edge')), parts along dimension 0, may hold values from -6 to 6
Outputs:
- node_out: bfloat16 [4096, 512], P(('dp', 'edge')), parts along dimension 0
- edge_out: bfloat16 [4096, 9984], P(('dp', 'edge')), parts along dimension 0
- grad_nodes: float32 [4096, 512], P(('dp', 'edge')), parts along dimension 0
- grad_edges: float32 [4096, 9984], P(('dp', 'edge')), parts along dimension 0
- grad_w_msg1: float32 [4864, 512], P('dp'), parts along dimension 0
- grad_w_msg2: float32 [2048, 512], P('dp'), parts along dimension 0
- grad_w_msg3: float32 [2048, 512], P('dp'), parts along dimension 0
- grad_gain_one: float32 [2048], P('dp'), parts along dimension 0
- grad_offset_one: float32 [2048], P('dp'), parts along dimension 0
- grad_w_ffn1: float32 [2048, 2048], P('dp'), parts along dimension 0
- grad_w_ffn2: float32 [8192, 512], P('dp'), parts along dimension 0
- grad_gain_two: float32 [2048], P('dp'), parts along dimension 0
- grad_offset_two: float32 [2048], P('dp'), parts along dimension 0
- grad_w_edge1: float32 [4864, 192], P('dp'), parts along dimension 0
- grad_w_edge2: float32 [768, 192], P('dp'), parts along dimension 0
- grad_w_edge3: float32 [768, 192], P('dp'), parts along dimension 0
- grad_gain_three: float32 [768], P('dp'), parts along dimension 0
- grad_offset_three: float32 [768], P('dp'), parts along dimension 0
There are 4 independent parts, one for each index of `dp`. A program takes and returns all parts, laid end to end along the dimension named above; an argument that names none is the same for every part. Nothing has to cross between parts.
Inputs may be any that keep to these rules, and one draw needn't show every extreme that they name: `nbr_owner`: among the 6656 edges of one device (aligned blocks of rows), no value is named by more than 1664 edges, a bound that some block reaches.
All inputs are finite; a program needn't handle non-finite values. No bound on the sum of `edge_mask` on one device may be relied on, other than what follows from the above.
Results may differ from a plain program's by a relative error of at most 0.017.
Values may be sent and summed in bfloat16 or wider, within the bound.
A program may use at most 512 MiB of HBM per device.

v0:
```python
import jax
import jax.numpy as jnp
from jax import lax
from jax.sharding import PartitionSpec as P


def gelu_act(values):
    return jax.nn.gelu(values, approximate=True)


def gelu_back(values, upstream):
    return jax.vjp(gelu_act, values)[1](upstream)[0]


def product(left, right):
    return jnp.dot(left, right, preferred_element_type=jnp.float32)


def product_tn(left, right):
    return lax.dot_general(
        left, right, (((0,), (0,)), ((), ())), preferred_element_type=jnp.float32
    )


def product_nt(left, right):
    return lax.dot_general(
        left, right, (((1,), (1,)), ((), ())), preferred_element_type=jnp.float32
    )


def exact_sum(selector, values):
    return jnp.dot(
        selector, values, precision=lax.Precision.HIGHEST, preferred_element_type=jnp.float32
    )


def norm_forward(values, scale_gain, offset):
    average = jnp.mean(values, axis=-1, keepdims=True)
    centred = values - average
    variance = jnp.mean(centred * centred, axis=-1, keepdims=True)
    inverse = lax.rsqrt(variance + 1e-05)
    normal = centred * inverse
    return (normal * scale_gain + offset, normal, inverse)


def norm_backward(upstream, normal, inverse, scale_gain):
    grad_gain = jnp.sum(upstream * normal, axis=0)
    grad_offset = jnp.sum(upstream, axis=0)
    scaled = upstream * scale_gain
    centred = scaled - jnp.mean(scaled, axis=-1, keepdims=True)
    grad_values = inverse * (centred - normal * jnp.mean(scaled * normal, axis=-1, keepdims=True))
    return (grad_values, grad_gain, grad_offset)


def message_hidden(joined, w_msg1, w_msg2):
    pre_one = product(joined, w_msg1)
    act_one = gelu_act(pre_one).astype(jnp.bfloat16)
    pre_two = product(act_one, w_msg2)
    act_two = gelu_act(pre_two).astype(jnp.bfloat16)
    return (pre_one, act_one, pre_two, act_two)


def body(
    nodes,
    edges,
    nbr_owner,
    nbr_slot,
    edge_mask,
    w_msg1,
    w_msg2,
    w_msg3,
    gain_one,
    offset_one,
    w_ffn1,
    w_ffn2,
    gain_two,
    offset_two,
    w_edge1,
    w_edge2,
    w_edge3,
    gain_three,
    offset_three,
    node_cotangent,
    edge_cotangent,
):
    peer_count = lax.axis_size("edge")
    row_count = nodes.shape[0]
    node_width = nodes.shape[1]
    channels = w_edge2.shape[0]
    fanout = nbr_slot.shape[1]
    edge_count = row_count * fanout
    capacity = 2 * edge_count // peer_count
    slot_count = peer_count * capacity
    owner_flat = nbr_owner.reshape(edge_count)
    local_flat = nbr_slot.reshape(edge_count)
    live_flat = edge_mask.reshape(edge_count)
    peer_ids = jnp.arange(peer_count, dtype=jnp.int32)
    owner_hits = (owner_flat[:, None] == peer_ids[None, :]).astype(jnp.int32)
    ranked = jnp.cumsum(owner_hits, axis=0) - 1
    rank_flat = jnp.sum(ranked * owner_hits, axis=1)
    position = owner_flat * capacity + rank_flat
    edge_ids = jnp.arange(edge_count, dtype=jnp.int32)
    slot_edge = jnp.full((slot_count,), -1, jnp.int32).at[position].set(edge_ids)
    filled = slot_edge >= 0
    slot_safe = jnp.maximum(slot_edge, 0)
    slot_source = slot_safe // fanout
    code_flat = local_flat + row_count * (1 - live_flat)
    slot_code = jnp.where(filled, code_flat[slot_safe], -1)
    edge_rows = edges.reshape(edge_count, channels)
    slot_edges = jnp.where(filled[:, None], edge_rows[slot_safe], jnp.zeros((), jnp.bfloat16))
    send_edges = slot_edges.reshape(peer_count, capacity * channels)
    send_code = slot_code.reshape(peer_count, capacity)
    slot_nodes = jnp.where(filled[:, None], nodes[slot_source], jnp.zeros((), jnp.bfloat16))
    got_nodes, got_edges, got_code = (
        lax.all_to_all(
            slot_nodes.reshape(peer_count, capacity, node_width),
            "edge",
            split_axis=0,
            concat_axis=0,
            tiled=True,
        ),
        lax.all_to_all(send_edges, "edge", split_axis=0, concat_axis=0, tiled=True),
        lax.all_to_all(send_code, "edge", split_axis=0, concat_axis=0, tiled=True),
    )
    recv_nodes = got_nodes.reshape(slot_count, node_width)
    recv_edges = got_edges.reshape(slot_count, channels)
    recv_code = got_code.reshape(slot_count)
    node_ids = jnp.arange(row_count, dtype=jnp.int32)
    occupied = recv_code >= 0
    live_slot = occupied & (recv_code < row_count)
    target_local = jnp.where(occupied, recv_code % row_count, 0)
    pick_all = ((node_ids[:, None] == target_local[None, :]) & occupied[None, :]).astype(
        jnp.bfloat16
    )
    pick_live = ((node_ids[:, None] == target_local[None, :]) & live_slot[None, :]).astype(
        jnp.float32
    )
    dest_nodes = nodes[target_local]
    joined = jnp.concatenate([recv_nodes, dest_nodes, recv_edges], axis=1)
    act_two = message_hidden(joined, w_msg1, w_msg2)[3]
    message = product(act_two, w_msg3)
    divisor = 1.0 + jnp.sum(pick_live, axis=1)
    summed = exact_sum(pick_live, message)
    node_in = nodes.astype(jnp.float32)
    normed_one, normal_one, inverse_one = norm_forward(
        node_in + summed / divisor[:, None], gain_one, offset_one
    )
    normed_low = normed_one.astype(jnp.bfloat16)
    ffn_pre = product(normed_low, w_ffn1)
    ffn_act = gelu_act(ffn_pre).astype(jnp.bfloat16)
    node_new, normal_two, inverse_two = norm_forward(
        normed_one + product(ffn_act, w_ffn2), gain_two, offset_two
    )
    node_low = node_new.astype(jnp.bfloat16)
    back_rows = jnp.where(occupied[:, None], node_low[target_local], jnp.zeros((), jnp.bfloat16))
    returned = lax.all_to_all(
        back_rows.reshape(peer_count, capacity, node_width),
        "edge",
        split_axis=0,
        concat_axis=0,
        tiled=True,
    )
    far_nodes = returned.reshape(slot_count, node_width)[position]
    near_nodes = jnp.repeat(node_low, fanout, axis=0)
    edge_join = jnp.concatenate([near_nodes, far_nodes, edge_rows], axis=1)
    edge_pre1 = product(edge_join, w_edge1)
    hidden_one = gelu_act(edge_pre1).astype(jnp.bfloat16)
    edge_pre2 = product(hidden_one, w_edge2)
    hidden_two = gelu_act(edge_pre2).astype(jnp.bfloat16)
    edge_new, normal_three, inverse_three = norm_forward(
        edge_rows.astype(jnp.float32) + product(hidden_two, w_edge3), gain_three, offset_three
    )
    edge_upstream = edge_cotangent.reshape(edge_count, channels).astype(jnp.float32)
    grad_three, grad_gain_three, grad_offset_three = norm_backward(
        edge_upstream, normal_three, inverse_three, gain_three
    )
    grad_low3 = grad_three.astype(jnp.bfloat16)
    grad_w_edge3 = product_tn(hidden_two, grad_low3)
    grad_low2 = gelu_back(edge_pre2, product_nt(grad_low3, w_edge3)).astype(jnp.bfloat16)
    grad_w_edge2 = product_tn(hidden_one, grad_low2)
    grad_low1 = gelu_back(edge_pre1, product_nt(grad_low2, w_edge2)).astype(jnp.bfloat16)
    grad_w_edge1 = product_tn(edge_join, grad_low1)
    grad_edge_join = product_nt(grad_low1, w_edge1)
    grad_near = jnp.sum(
        grad_edge_join[:, :node_width].reshape(row_count, fanout, node_width), axis=1
    )
    grad_far = grad_edge_join[:, node_width : 2 * node_width].astype(jnp.bfloat16)
    grad_edge_rows = grad_three + grad_edge_join[:, 2 * node_width :]
    far_slots = jnp.where(filled[:, None], grad_far[slot_safe], jnp.zeros((), jnp.bfloat16))
    far_back = lax.all_to_all(
        far_slots.reshape(peer_count, capacity, node_width),
        "edge",
        split_axis=0,
        concat_axis=0,
        tiled=True,
    )
    far_mine = product(pick_all, far_back.reshape(slot_count, node_width))
    grad_node_new = node_cotangent.astype(jnp.float32) + grad_near + far_mine
    grad_two, grad_gain_two, grad_offset_two = norm_backward(
        grad_node_new, normal_two, inverse_two, gain_two
    )
    grad_resid = grad_two.astype(jnp.bfloat16)
    grad_w_ffn2 = product_tn(ffn_act, grad_resid)
    grad_ffn = gelu_back(ffn_pre, product_nt(grad_resid, w_ffn2)).astype(jnp.bfloat16)
    grad_w_ffn1 = product_tn(normed_low, grad_ffn)
    grad_normed = grad_two + product_nt(grad_ffn, w_ffn1)
    grad_one, grad_gain_one, grad_offset_one = norm_backward(
        grad_normed, normal_one, inverse_one, gain_one
    )
    grad_mean = grad_one / divisor[:, None]
    grad_message = jnp.where(live_slot[:, None], grad_mean[target_local], 0.0).astype(jnp.bfloat16)
    pre_one, act_one, pre_two, act_two = message_hidden(joined, w_msg1, w_msg2)
    grad_w_msg3 = product_tn(act_two, grad_message)
    grad_upper = gelu_back(pre_two, product_nt(grad_message, w_msg3)).astype(jnp.bfloat16)
    grad_w_msg2 = product_tn(act_one, grad_upper)
    grad_lower = gelu_back(pre_one, product_nt(grad_upper, w_msg2)).astype(jnp.bfloat16)
    grad_w_msg1 = product_tn(joined, grad_lower)
    grad_joined = product_nt(grad_lower, w_msg1)
    grad_node_rows = grad_one + exact_sum(pick_live, grad_joined[:, node_width : 2 * node_width])
    source_low = grad_joined[:, :node_width].astype(jnp.bfloat16)
    edge_grads = (
        grad_joined[:, 2 * node_width :]
        .astype(jnp.bfloat16)
        .reshape(peer_count, capacity * channels)
    )
    back_source, back_edges = (
        lax.all_to_all(
            source_low.reshape(peer_count, capacity, node_width),
            "edge",
            split_axis=0,
            concat_axis=0,
            tiled=True,
        ),
        lax.all_to_all(edge_grads, "edge", split_axis=0, concat_axis=0, tiled=True),
    )
    source_per_edge = back_source.reshape(slot_count, node_width)[position].astype(jnp.float32)
    grad_node_rows = grad_node_rows + jnp.sum(
        source_per_edge.reshape(row_count, fanout, node_width), axis=1
    )
    grad_edge_rows = grad_edge_rows + back_edges.reshape(slot_count, channels)[position].astype(
        jnp.float32
    )
    totals = lax.psum(
        (
            grad_w_msg1,
            grad_w_msg2,
            grad_w_msg3,
            grad_gain_one,
            grad_offset_one,
            grad_w_ffn1,
            grad_w_ffn2,
            grad_gain_two,
            grad_offset_two,
            grad_w_edge1,
            grad_w_edge2,
            grad_w_edge3,
            grad_gain_three,
            grad_offset_three,
        ),
        "edge",
    )
    edge_out = edge_new.astype(jnp.bfloat16).reshape(row_count, fanout * channels)
    return (
        node_low,
        edge_out,
        grad_node_rows,
        grad_edge_rows.reshape(row_count, fanout * channels),
        totals[0],
        totals[1],
        totals[2],
        totals[3],
        totals[4],
        totals[5],
        totals[6],
        totals[7],
        totals[8],
        totals[9],
        totals[10],
        totals[11],
        totals[12],
        totals[13],
    )


def solution(mesh):
    return jax.shard_map(
        body,
        mesh=mesh,
        in_specs=(
            P(("dp", "edge"), None),
            P(("dp", "edge"), None),
            P(("dp", "edge"), None, None),
            P(("dp", "edge"), None),
            P(("dp", "edge"), None),
            P(),
            P(),
            P(),
            P(),
            P(),
            P(),
            P(),
            P(),
            P(),
            P(),
            P(),
            P(),
            P(),
            P(),
            P(("dp", "edge"), None),
            P(("dp", "edge"), None),
        ),
        out_specs=(
            P(("dp", "edge"), None),
            P(("dp", "edge"), None),
            P(("dp", "edge"), None),
            P(("dp", "edge"), None),
            P("dp", None),
            P("dp", None),
            P("dp", None),
            P("dp"),
            P("dp"),
            P("dp", None),
            P("dp", None),
            P("dp"),
            P("dp"),
            P("dp", None),
            P("dp", None),
            P("dp", None),
            P("dp"),
            P("dp"),
        ),
        check_vma=False,
    )
```

profile of v0, /device:TPU:0, one launch (start us, length us, event | category | flops | bytes accessed | tf_op | source)
XLA Modules:
  0.0 2750.9 jit_solution(6221552783280286426)
XLA Ops:
  13.7 24.9 scatter_custom_fusion
  38.7 73.7 %gather_fusion = s32[13312]{0:T(1024)S(1)} fusion(s32[6656]{0:T(1024)S(1)} %add.241, s32[13312]{0:T(1024)S(1)} %get-tuple-element.50), kind=kCustom, calls=%fused_computation | custom fusion | bytes 159744 | tf_op jit(solution)/shard_map/gather | solution.py:108
  148.8 52.3 %gather_fusion.3 = bf16[13312,192]{1,0:T(8,128)(2,1)} fusion(bf16[6656,192]{1,0:T(8,128)(2,1)} %reshape.395, s32[13312]{0:T(1024)S(1)} %get-tuple-element.50), kind=kCustom, calls=%fused_computation.3 | custom fusion | bytes 10276864 | tf_op jit(solution)/shard_map/gather | solution.py:110
  250.4 54.2 %gather_fusion.1 = bf16[13312,512]{1,0:T(8,128)(2,1)} fusion(bf16[128,512]{1,0:T(8,128)(2,1)S(1)} %copy-done.2, s32[13312]{0:T(1024)S(1)} %get-tuple-element.49), kind=kCustom, calls=%fused_computation.1 | custom fusion | bytes 27316224 | tf_op jit(solution)/shard_map/gather | solution.py:113
  318.1 46.1 %all-to-all-done.2 = bf16[8,2,159744]{2,1,0:T(2,128)(2,1)} async-done(((bf16[8,2,159744]{2,1,0:T(2,128)(2,1)}), bf16[8,2,159744]{2,1,0:T(2,128)(2,1)}, u32[]{:S(2)}, u32[]{:S(2)}) %all-to-all-start.2) | async-done | bytes 5111840 | tf_op jit(solution)/shard_map/all_to_all | solution.py:122
  370.3 54.2 %gather_fusion.2 = bf16[13312,512]{1,0:T(8,128)(2,1)} fusion(bf16[128,512]{1,0:T(8,128)(2,1)S(1)} %copy-done.2, s32[13312]{0:T(1024)S(1)} %broadcast_clamp_fusion), kind=kCustom, calls=%fused_computation.2 | custom fusion | bytes 27316224 | tf_op jit(solution)/shard_map/gather | solution.py:138
  436.7 109.6 %reduce.2 = bf16[8,319488]{1,0:T(8,128)(2,1)} reduce(bf16[8,1,319488]{2,1,0:T(2,128)(2,1)} %reshape.515, bf16[]{:T(256)} %constant.99), dimensions={1}, to_apply=%all_to_all.31.reduce_sub_computation | reduce | bytes 10223618 | tf_op jit(solution)/shard_map/all_to_all | solution.py:122
  564.1 102.1 %all-to-all-done.1 = bf16[8,1664,512]{2,1,0:T(8,128)(2,1)} async-done(((bf16[8,1664,512]{2,1,0:T(8,128)(2,1)}), bf16[8,1664,512]{2,1,0:T(8,128)(2,1)}, u32[]{:S(2)}, u32[]{:S(2)}) %all-to-all-start.1) | async-done | bytes 13631520 | tf_op jit(solution)/shard_map/all_to_all | solution.py:115
  666.3 33.3 %multiply_convert_fusion.1 = (bf16[13312,512]{1,0:T(8,128)(2,1)}, f32[13312,512]{1,0:T(8,128)}) fusion(bf16[1216,512]{1,0:T(8,128)(2,1)S(1)} %copy-done.27, bf16[13312,192]{1,0:T(8,128)(2,1)} %reshape.396, bf16[13312,512]{1,0:T(8,128)(2,1)} %gather_fusion.2, bf16[13312,512]{1,0:T(8,128)(2,1)} %bitcast.4), kind=kOutput, calls=%fused_computation.34 | convolution fusion | flops 16734355456 | bytes 74514432 | tf_op jit(solution)/shard_map/dot_general | solution.py:16
  757.6 54.2 %gather_fusion.4 = bf16[13312,512]{1,0:T(8,128)(2,1)} fusion(bf16[128,512]{1,0:T(8,128)(2,1)S(1)} %add_convert_fusion.1, s32[13312]{0:T(1024)S(1)} %broadcast_clamp_fusion), kind=kCustom, calls=%fused_computation.4 | custom fusion | bytes 27316224 | tf_op jit(solution)/shard_map/gather | solution.py:155
  869.8 257.6 %all-to-all-done.3 = bf16[8,1664,512]{2,1,0:T(8,128)(2,1)} async-done(((bf16[8,1664,512]{2,1,0:T(8,128)(2,1)}), bf16[8,1664,512]{2,1,0:T(8,128)(2,1)}, u32[]{:S(2)}, u32[]{:S(2)}) %all-to-all-start.3) | async-done | bytes 13631520 | tf_op jit(solution)/shard_map/all_to_all | solution.py:156
  1127.4 26.3 gather_fusion.5
  1225.6 58.3 %gather_fusion.6 = bf16[13312,512]{1,0:T(8,128)(2,1)} fusion(bf16[6656,512]{1,0:T(8,128)(2,1)} %copy.103, s32[13312]{0:T(1024)S(1)} %copy-done.32), kind=kCustom, calls=%fused_computation.6 | custom fusion | bytes 27316224 | tf_op jit(solution)/shard_map/gather | solution.py:189
  1351.3 247.9 %all-to-all-done.4 = bf16[8,1664,512]{2,1,0:T(8,128)(2,1)} async-done(((bf16[8,1664,512]{2,1,0:T(8,128)(2,1)}), bf16[8,1664,512]{2,1,0:T(8,128)(2,1)}, u32[]{:S(2)}, u32[]{:S(2)}) %all-to-all-start.4) | async-done | bytes 13631520 | tf_op jit(solution)/shard_map/all_to_all | solution.py:190
  1610.8 54.2 %gather_fusion.7 = bf16[13312,512]{1,0:T(8,128)(2,1)} fusion(bf16[128,512]{1,0:T(8,128)(2,1)S(1)} %broadcast_divide_fusion, s32[13312]{0:T(1024)S(1)} %copy-done.34), kind=kCustom, calls=%fused_computation.7 | custom fusion | bytes 27316224 | tf_op jit(solution)/shard_map/gather | solution.py:211
  1665.0 30.8 %fusion.13 = bf16[13312,512]{1,0:T(8,128)(2,1)} fusion(f32[13312,512]{1,0:T(8,128)} %get-tuple-element.54, bf16[512,512]{1,0:T(8,128)(2,1)S(1)} %copy-done.40, bf16[13312,512]{1,0:T(8,128)(2,1)} %gather_fusion.7, pred[13312]{0:T(1024)(128)(4,1)S(1)} %copy-done.47), kind=kOutput, calls=%fused_computation.29 | convolution fusion | flops 7122452480 | bytes 55063552 | tf_op jit(solution)/shard_map/dot_general | solution.py:26
  1695.8 30.6 %fusion.6 = bf16[13312,512]{1,0:T(8,128)(2,1)} fusion(f32[13312,512]{1,0:T(8,128)} %get-tuple-element.52, bf16[13312,512]{1,0:T(8,128)(2,1)} %fusion.13, bf16[512,512]{1,0:T(8,128)(2,1)S(1)} %copy-done.89), kind=kOutput, calls=%fused_computation.22 | convolution fusion | flops 7115636736 | bytes 55050240 | tf_op jit(solution)/shard_map/dot_general | solution.py:26
  1726.4 38.6 %fusion.108 = (bf16[13312,1216]{0,1:T(8,128)(2,1)}, f32[13312,1216]{0,1:T(8,128)}) fusion(bf16[13312,512]{1,0:T(8,128)(2,1)} %fusion.6, bf16[1216,512]{1,0:T(8,128)(2,1)S(1)} %copy-done.28), kind=kOutput, calls=%fused_computation.191 | convolution fusion | flops 16592076800 | bytes 112001024 | tf_op jit(solution)/shard_map/dot_general | solution.py:26
  1790.7 110.4 %reduce.7 = bf16[8,319488]{1,0:T(8,128)(2,1)} reduce(bf16[8,1,319488]{2,1,0:T(2,128)(2,1)} %all_to_all.37, bf16[]{:T(256)} %broadcast.517), dimensions={1}, to_apply=%all_to_all.37.reduce_sub_computation | reduce | bytes 10223618 | tf_op jit(solution)/shard_map/all_to_all | solution.py:234
  1928.0 100.9 %all-to-all-done.6 = bf16[8,2,159744]{2,1,0:T(2,128)(2,1)} async-done(((bf16[8,2,159744]{2,1,0:T(2,128)(2,1)}), bf16[8,2,159744]{2,1,0:T(2,128)(2,1)}, u32[]{:S(2)}, u32[]{:S(2)}) %all-to-all-start.6) | async-done | bytes 5111840 | tf_op jit(solution)/shard_map/all_to_all | solution.py:234
  2088.1 33.2 %fusion.16 = f32[1216,512]{1,0:T(8,128)} fusion(bf16[13312,512]{1,0:T(8,128)(2,1)} %fusion.6, bf16[13312,192]{1,0:T(8,128)(2,1)S(1)} %bitcast.90, bf16[13312,512]{1,0:T(8,128)(2,1)} %gather_fusion.2, bf16[13312,512]{1,0:T(8,128)(2,1)} %bitcast.4), kind=kOutput, calls=%fused_computation.35 | convolution fusion | flops 16673013760 | bytes 48496640 | tf_op jit(solution)/shard_map/dot_general | solution.py:20
  2136.8 325.6 %all-reduce = (f32[512]{0:T(512)}, f32[512]{0:T(512)}, f32[512]{0:T(512)}, f32[512]{0:T(512)}, f32[192]{0:T(256)}, /*index=5*/f32[192]{0:T(256)}) all-reduce(f32[512]{0:T(512)S(1)} %copy-done.69, f32[512]{0:T(512)S(1)} %copy-done.70, f32[512]{0:T(512)S(1)} %copy-done.78, ...), channel_id=1, replica_groups=mesh['dp'=4,'edge'=8] {'edge'}, use_global_device_ids=true, to_apply=%region_23.24 | all-reduce | flops 2432 | bytes 19456 | tf_op jit(solution)/shard_map/psum | solution.py:243
  2472.0 109.8 %reduce.3 = bf16[8,319488]{1,0:T(8,128)(2,1)} reduce(bf16[8,1,319488]{2,1,0:T(2,128)(2,1)} %reshape.517, bf16[]{:T(256)} %constant.99), dimensions={1}, to_apply=%all_to_all.36.reduce_sub_computation | reduce | bytes 10223618 | tf_op jit(solution)/shard_map/all_to_all | solution.py:234
  2665.0 26.3 gather_fusion.8
  (344 shorter events, 680.4 us)
Async XLA Ops:
  7.2 747.8 %copy-start = (bf16[512,2048]{1,0:T(8,128)(2,1)S(1)}, bf16[512,2048]{1,0:T(8,128)(2,1)}, u32[]{:S(2)}) copy-start(bf16[512,2048]{1,0:T(8,128)(2,1)} %param.31) | copy-start | bytes 6291460
  38.7 110.1 %copy-start.31 = (s32[13312]{0:T(1024)}, s32[13312]{0:T(1024)S(1)}, u32[]{:S(2)}) copy-start(s32[13312]{0:T(1024)S(1)} %get-tuple-element.50) | copy-start | bytes 159748
  113.0 132.2 %all-to-all-start = ((s32[8,1,1664]{2,1,0:T(1,128)}), s32[8,1,1664]{2,1,0:T(1,128)S(1)}, u32[]{:S(2)}, u32[]{:S(2)}) async-start(s32[8,1,1664]{2,1,0:T(1,128)} %bitcast.1), calls=%async_computation | async-start | bytes 106496 | tf_op jit(solution)/shard_map/all_to_all | solution.py:123
  119.6 185.0 %copy-start.44 = (pred[8,1664]{1,0:T(8,128)(4,1)}, pred[8,1664]{1,0:T(8,128)(4,1)S(1)}, u32[]{:S(2)}) copy-start(pred[8,1664]{1,0:T(8,128)(4,1)S(1)} %broadcast_in_dim.59) | copy-start | bytes 39940
  245.2 119.0 %all-to-all-start.2 = ((bf16[8,2,159744]{2,1,0:T(2,128)(2,1)}), bf16[8,2,159744]{2,1,0:T(2,128)(2,1)}, u32[]{:S(2)}, u32[]{:S(2)}) async-start(bf16[8,2,159744]{2,1,0:T(2,128)(2,1)} %reshape.514), calls=%async_computation.2 | async-start | bytes 10223616 | tf_op jit(solution)/shard_map/all_to_all | solution.py:122
  364.2 302.1 %all-to-all-start.1 = ((bf16[8,1664,512]{2,1,0:T(8,128)(2,1)}), bf16[8,1664,512]{2,1,0:T(8,128)(2,1)}, u32[]{:S(2)}, u32[]{:S(2)}) async-start(bf16[8,1664,512]{2,1,0:T(8,128)(2,1)} %broadcast_select_fusion.2), calls=%async_computation.1 | async-start | bytes 27262976 | tf_op jit(solution)/shard_map/all_to_all | solution.py:115
  370.3 387.2 %copy-start.33 = (s32[13312]{0:T(1024)}, s32[13312]{0:T(1024)S(1)}, u32[]{:S(2)}) copy-start(s32[13312]{0:T(1024)S(1)} %broadcast_clamp_fusion) | copy-start | bytes 159748
  425.1 315.3 %copy-start.46 = (pred[13312]{0:T(1024)(128)(4,1)}, pred[13312]{0:T(1024)(128)(4,1)S(1)}, u32[]{:S(2)}) copy-start(pred[13312]{0:T(1024)(128)(4,1)S(1)} %get-tuple-element.48) | copy-start | bytes 39940
  426.4 314.1 %copy-start.80 = (f32[128]{0:T(128)}, f32[128]{0:T(128)S(1)}, u32[]{:S(2)}) copy-start(f32[128]{0:T(128)S(1)} %broadcast_add_fusion) | copy-start | bytes 1540
  553.3 113.0 %copy-start.27 = (bf16[1216,512]{1,0:T(8,128)(2,1)S(1)}, bf16[1216,512]{1,0:T(8,128)(2,1)}, u32[]{:S(2)}) copy-start(bf16[1216,512]{1,0:T(8,128)(2,1)} %param.26) | copy-start | bytes 3735556
  757.6 92.0 %copy-start.3 = (bf16[128,512]{1,0:T(8,128)(2,1)}, bf16[128,512]{1,0:T(8,128)(2,1)S(1)}, u32[]{:S(2)}) copy-start(bf16[128,512]{1,0:T(8,128)(2,1)S(1)} %add_convert_fusion.1) | copy-start | bytes 393220
  825.4 302.1 %all-to-all-start.3 = ((bf16[8,1664,512]{2,1,0:T(8,128)(2,1)}), bf16[8,1664,512]{2,1,0:T(8,128)(2,1)}, u32[]{:S(2)}, u32[]{:S(2)}) async-start(bf16[8,1664,512]{2,1,0:T(8,128)(2,1)} %broadcast_select_fusion), calls=%async_computation.3 | async-start | bytes 27262976 | tf_op jit(solution)/shard_map/all_to_all | solution.py:156
  849.6 277.9 %copy-start.42 = (s32[7168]{0:T(1024)}, s32[7168]{0:T(1024)S(1)}, u32[]{:S(2)}) copy-start(s32[7168]{0:T(1024)S(1)} %pad_clamp_fusion) | copy-start | bytes 86020
  1297.6 301.7 %all-to-all-start.4 = ((bf16[8,1664,512]{2,1,0:T(8,128)(2,1)}), bf16[8,1664,512]{2,1,0:T(8,128)(2,1)}, u32[]{:S(2)}, u32[]{:S(2)}) async-start(bf16[8,1664,512]{2,1,0:T(8,128)(2,1)} %broadcast_select_fusion.1), calls=%async_computation.4 | async-start | bytes 27262976 | tf_op jit(solution)/shard_map/all_to_all | solution.py:190
  1343.4 255.8 %copy-start.22 = (f32[128,512]{1,0:T(8,128)S(1)}, f32[128,512]{1,0:T(8,128)}, u32[]{:S(2)}) copy-start(f32[128,512]{1,0:T(8,128)} %copy-done.21) | copy-start | bytes 786436
  1343.4 255.8 %copy-start.37 = (s32[13312]{0:T(1024)S(1)}, s32[13312]{0:T(1024)}, u32[]{:S(2)}) copy-start(s32[13312]{0:T(1024)} %copy-done.35) | copy-start | bytes 159748
  1343.4 255.8 %copy-start.61 = (pred[13312]{0:T(1024)(128)(4,1)S(1)}, pred[13312]{0:T(1024)(128)(4,1)}, u32[]{:S(2)}) copy-start(pred[13312]{0:T(1024)(128)(4,1)} %get-tuple-element.47) | copy-start | bytes 39940
  1343.4 255.9 %copy-start.66 = (f32[512]{0:T(512)S(1)}, f32[512]{0:T(512)}, u32[]{:S(2)}) copy-start(f32[512]{0:T(512)} %param.33) | copy-start | bytes 6148
  1343.4 255.9 %copy-start.72 = (f32[128]{0:T(128)S(1)}, f32[128]{0:T(128)}, u32[]{:S(2)}) copy-start(f32[128]{0:T(128)} %copy-done.71) | copy-start | bytes 1540
  1343.5 255.9 %copy-start.77 = (f32[128]{0:T(128)S(1)}, f32[128]{0:T(128)}, u32[]{:S(2)}) copy-start(f32[128]{0:T(128)} %copy-done.76) | copy-start | bytes 1540
  1343.5 255.9 %copy-start.90 = (bf16[128,512]{1,0:T(8,128)(2,1)S(1)}, bf16[128,512]{1,0:T(8,128)(2,1)}, u32[]{:S(2)}) copy-start(bf16[128,512]{1,0:T(8,128)(2,1)} %param.40) | copy-start | bytes 393220
  1910.6 118.3 %all-to-all-start.6 = ((bf16[8,2,159744]{2,1,0:T(2,128)(2,1)}), bf16[8,2,159744]{2,1,0:T(2,128)(2,1)}, u32[]{:S(2)}, u32[]{:S(2)}) async-start(bf16[8,2,159744]{2,1,0:T(2,128)(2,1)} %reshape.516), calls=%async_computation.6 | async-start | bytes 10223616 | tf_op jit(solution)/shard_map/all_to_all | solution.py:234
  2028.9 618.0 %all-to-all-start.5 = ((bf16[8,1664,512]{1,2,0:T(8,128)(2,1)}), bf16[8,1664,512]{1,2,0:T(8,128)(2,1)}, u32[]{:S(2)}, u32[]{:S(2)}) async-start(bf16[8,1664,512]{1,2,0:T(8,128)(2,1)} %bitcast.80), calls=%async_computation.5 | async-start | bytes 27262976 | tf_op jit(solution)/shard_map/all_to_all | solution.py:227
  2034.4 696.1 %all-reduce.4.cloned.1.call-start = ((), (), s32[]{:S(2)}) async-start(), calls=%async_computation.7 | async-start | bytes 28704768 | tf_op jit(solution)/shard_map/psum | solution.py:243
  (85 other events, 988.4 us)
Sparse Core Ops, SparseCore 0:
  2121.5 490.8 all-reduce.3
where the time goes:
time: 2760 us; the launch traced here: 2750 us
  local copies, waits for them, and re-layouts  849 us (31%)
  waiting for transfers between devices  755 us (27%)
  other arithmetic  427 us (15%)
  matrix products  340 us (12%)
  blocking collectives  326 us (12%)
  starting transfers between devices  39 us (1%)
    psum x1, blocking collectives, body(): lax.psum((grad_w_msg1, grad_w_msg2, grad_w_msg3, grad_gain_one, grad_offs...  326 us
    all_to_all x1, waiting for transfers between devices, body(): lax.all_to_all(back_rows.reshape(peer_count, capacity, node_width), 'edge...  258 us
    all_to_all x1, waiting for transfers between devices, body(): lax.all_to_all(far_slots.reshape(peer_count, capacity, node_width), 'edge...  248 us
    all_to_all x2, other arithmetic, body(): lax.all_to_all(edge_grads, 'edge', split_axis=0, concat_axis=0, tiled=True)  220 us
    unnamed x223, local copies, waits for them, and re-layouts  123 us
    dot_general x8, matrix products, product_nt(): lax.dot_general(left, right, (((1,), (1,)), ((), ())), preferred_element_...  123 us
    all_to_all x1, other arithmetic, body(): lax.all_to_all(send_edges, 'edge', split_axis=0, concat_axis=0, tiled=True)  110 us
    all_to_all x1, waiting for transfers between devices, body(): lax.all_to_all(slot_nodes.reshape(peer_count, capacity, node_width), 'edg...  102 us
  transfers between devices with their start and end apart: 8, of which 5 were waited for; matrix products, arithmetic and copies ran while one was open for 31% of the time, Pallas kernels for 0%

commit v1 on v0

v1 whole, which is shorter than its diff:
```python
import functools

import jax
import jax.numpy as jnp
from jax import lax
from jax.experimental import pallas as pl
from jax.experimental.pallas import tpu as pltpu
from jax.sharding import PartitionSpec as P

BF = jnp.bfloat16
F32 = jnp.float32
I32 = jnp.int32
MESH = pl.DeviceIdType.MESH
MIB = 1024 * 1024
LANES = 128
GROUP = 4
TABLE = 1024
EPS = 1e-05
ROOT = 0.7978845608028654
CUBE = 0.044715 * ROOT


def dot(a, b):
    return jnp.dot(a, b, preferred_element_type=F32)


def dot_tn(a, b):
    return lax.dot_general(a, b, (((0,), (0,)), ((), ())), preferred_element_type=F32)


def dot_nt(a, b):
    return lax.dot_general(a, b, (((1,), (1,)), ((), ())), preferred_element_type=F32)


def gelu_pair(v):
    z = v * v
    q = 0.5 + 0.5 * jnp.tanh(v * (ROOT + CUBE * z))
    act = v * q
    slope = q + (act - act * q) * (2.0 * ROOT + 6.0 * CUBE * z)
    return act, slope


def row_mean(v):
    return jnp.mean(v, axis=-1, keepdims=True)


def lane_column(ref, k):
    rows = ref.shape[0]
    return jnp.broadcast_to(pltpu.roll(ref[...], LANES - k, axis=1)[:, 0:1], (rows, LANES))


def pick_rows(target, width):
    lane = lax.broadcasted_iota(I32, target.shape, 1)
    return jnp.concatenate(
        [(target == lane + LANES * c).astype(F32).astype(BF) for c in range(width // LANES)],
        axis=1,
    )


def pick_cols(target, width):
    edges = target.shape[1]
    sub = lax.broadcasted_iota(I32, (width, edges), 0)
    return (jnp.broadcast_to(target, (width, edges)) == sub).astype(F32).astype(BF)


def gather_table(targets, table):
    count = table.shape[0]
    if count <= TABLE:
        hot = jnp.concatenate([pick_rows(t, count) for t in targets], axis=0)
        return dot(hot, table[...])

    def step(c, total):
        base = c * TABLE
        hot = jnp.concatenate([pick_rows(t - base, TABLE) for t in targets], axis=0)
        return total + dot(hot, table[pl.ds(pl.multiple_of(base, TABLE), TABLE), :])

    rows = sum(t.shape[0] for t in targets)
    return lax.fori_loop(0, count // TABLE, step, jnp.zeros((rows, table.shape[1]), F32))


def add_by_target(target, values, total):
    count = total.shape[0]
    if count <= TABLE:
        total[...] += dot(pick_cols(target, count), values)
        return

    def step(c, carry):
        base = c * TABLE
        part = pl.ds(pl.multiple_of(base, TABLE), TABLE)
        total[part, :] += dot(pick_cols(target - base, TABLE), values)
        return carry

    lax.fori_loop(0, count // TABLE, step, 0)


def by_chunks(count, step):
    if count <= TABLE:
        step(pl.ds(0, count))
        return

    def one(c, carry):
        step(pl.ds(pl.multiple_of(c * TABLE, TABLE), TABLE))
        return carry

    lax.fori_loop(0, count // TABLE, one, 0)


def remote(src, dst, send, recv, peer):
    return pltpu.make_async_remote_copy(
        src_ref=src,
        dst_ref=dst,
        send_sem=send,
        recv_sem=recv,
        device_id={"edge": peer},
        device_id_type=MESH,
    )


def greet(peers):
    barrier = pltpu.get_barrier_semaphore()
    for peer in peers:
        pl.semaphore_signal(barrier, inc=1, device_id={"edge": peer}, device_id_type=MESH)
    pl.semaphore_wait(barrier, len(peers))


def block(ref, index, rows):
    return ref.at[pl.ds(pl.multiple_of(index * rows, rows), rows)]


class Place:
    def __init__(self, n):
        self.me = lax.axis_index("edge")
        self.chips = n // 2
        self.chip = self.me // 2
        self.core = lax.rem(self.me, 2)
        self.sibling = self.chip * 2 + 1 - self.core
        self.mates = [self.at(d) for d in range(1, self.chips)]

    def at(self, d):
        return lax.rem(self.chip + d + self.chips, self.chips) * 2 + self.core


def gather_start(place, x, out, send, recv):
    rows, chips = x.shape[0], place.chips
    far = []
    for d in range(1, chips):
        far.append(
            remote(x, block(out, place.me, rows), send.at[d], recv.at[d], place.mates[d - 1])
        )
    near = remote(x, block(out, place.me, rows), send.at[0], recv.at[0], place.sibling)
    for copy in far:
        copy.start()
    near.start()
    return far, near


def gather_finish(place, handles, x, out, send, recv):
    far, near = handles
    rows, chips = x.shape[0], place.chips
    passed = []
    for d in range(1, chips):
        far[d - 1].wait_recv()
        got = block(out, place.at(-d), rows)
        copy = remote(got, got, send.at[chips + d], recv.at[chips + d], place.sibling)
        copy.start()
        passed.append(copy)
    near.wait()
    for copy in passed:
        copy.wait()
    for copy in far:
        copy.wait_send()


def scatter_sum(place, x, pair_buf, send_buf, far_buf, send, recv):
    chips, rows = place.chips, pair_buf.shape[1]
    pairs = []
    for d in range(chips):
        theirs = lax.rem(place.chip + d, chips) * 2 + 1 - place.core
        pairs.append(
            remote(block(x, theirs, rows), pair_buf.at[d], send.at[d], recv.at[d], place.sibling)
        )
    for d in range(1, chips):
        pairs[d].start()
    pairs[0].start()
    far = []
    for d in range(1, chips):
        pairs[d].wait_recv()
        mine = x[pl.ds(pl.multiple_of(place.at(d) * rows, rows), rows), :]
        send_buf[d] = (mine.astype(F32) + pair_buf[d].astype(F32)).astype(BF)
        copy = remote(
            send_buf.at[d], far_buf.at[d], send.at[chips + d], recv.at[chips + d], place.at(d)
        )
        copy.start()
        far.append(copy)
    pairs[0].wait_recv()
    own = x[pl.ds(pl.multiple_of(place.me * rows, rows), rows), :]
    total = own.astype(F32) + pair_buf[0].astype(F32)
    for d in range(1, chips):
        far[d - 1].wait_recv()
        total = total + far_buf[d].astype(F32)
    for d in range(chips):
        pairs[d].wait_send()
    for copy in far:
        copy.wait_send()
    return total


def comm_scratch(n, rows, width):
    return [pltpu.VMEM((n // 2, rows, width), BF)] * 3


def sems(count):
    return [pltpu.SemaphoreType.DMA((count,))] * 2


def remote_params(cid):
    return pltpu.CompilerParams(
        collective_id=cid, has_side_effects=True, vmem_limit_bytes=60 * MIB
    )


LOCAL = pltpu.CompilerParams(vmem_limit_bytes=62 * MIB)
WHOLE = pl.BlockSpec(memory_space=pltpu.VMEM)


def start_kernel(
    n, K, nodes, owner, slot, live, nodes_all, tcol, lcol, trow, count,
    orow, lrow, scol, hist, got, send, recv, hsend, hrecv, own_sem,
):
    place = Place(n)
    rows = nodes.shape[0]
    others = [lax.rem(place.me + d, n) for d in range(1, n)]
    greet(others)
    handles = gather_start(place, nodes, nodes_all, send, recv)
    own = pltpu.make_async_copy(nodes, block(nodes_all, place.me, rows), own_sem.at[0])
    own.start()
    spare = jnp.zeros((rows, LANES - K), I32)
    own_wide = jnp.concatenate([owner[...], spare], axis=1)
    slot_wide = jnp.concatenate([slot[...], spare], axis=1)
    live_wide = jnp.concatenate([live[...], spare], axis=1).astype(F32)
    target = own_wide * rows + slot_wide
    tcol[...] = target
    lcol[...] = live_wide
    scol[...] = slot_wide
    trow[...] = jnp.transpose(target)
    orow[...] = jnp.transpose(own_wide)
    lrow[...] = jnp.transpose(live_wide)

    def tally(g, total):
        ks = [g * GROUP + j for j in range(GROUP)]
        hot = jnp.concatenate([pick_rows(lane_column(scol, k), LANES) for k in ks], axis=0)
        owners = jnp.concatenate([orow[pl.ds(k, 1), :] for k in ks], axis=1)
        lives = jnp.concatenate([lrow[pl.ds(k, 1), :] for k in ks], axis=1)
        sub = lax.broadcasted_iota(I32, (n, GROUP * rows), 0)
        who = jnp.where(
            jnp.broadcast_to(owners, sub.shape) == sub, jnp.broadcast_to(lives, sub.shape), 0.0
        )
        return total + dot(who.astype(BF), hot)

    totals = lax.fori_loop(0, K // GROUP, tally, jnp.zeros((n, LANES), F32))
    for e in range(n):
        hist[e] = jnp.broadcast_to(totals[e : e + 1, :], (8, LANES))
    copies = []
    for d in range(1, n):
        copy = remote(
            hist.at[others[d - 1]], got.at[d], hsend.at[d], hrecv.at[d], others[d - 1]
        )
        copy.start()
        copies.append(copy)
    total = hist[place.me]
    for copy in copies:
        copy.wait_recv()
    for d in range(1, n):
        total = total + got[d]
    count[...] = total
    own.wait()
    gather_finish(place, handles, nodes, nodes_all, send, recv)
    for copy in copies:
        copy.wait_send()


def start_call(n, nodes, owner, slot, live):
    rows, D = nodes.shape
    K = slot.shape[1]
    shape = jax.ShapeDtypeStruct
    return pl.pallas_call(
        functools.partial(start_kernel, n, K),
        in_specs=[WHOLE] * 4,
        out_specs=[WHOLE] * 5,
        out_shape=[
            shape((n * rows, D), BF),
            shape((rows, LANES), I32),
            shape((rows, LANES), F32),
            shape((LANES, rows), I32),
            shape((8, LANES), F32),
        ],
        scratch_shapes=[
            pltpu.VMEM((LANES, rows), I32),
            pltpu.VMEM((LANES, rows), F32),
            pltpu.VMEM((rows, LANES), I32),
            pltpu.VMEM((n, 8, LANES), F32),
            pltpu.VMEM((n, 8, LANES), F32),
            *sems(n),
            *sems(n),
            pltpu.SemaphoreType.DMA((1,)),
        ],
        compiler_params=remote_params(0),
    )(nodes, owner, slot, live)


def slab_pairs(slab, C):
    pairs = slab.shape[1] // (2 * C)
    even = [slab[:, 2 * C * m : 2 * C * m + 256] for m in range(pairs)]
    odd = [slab[:, 2 * C * m + 2 * C - 256 : 2 * C * m + 2 * C] for m in range(pairs)]
    return jnp.concatenate(even, axis=0), jnp.concatenate(odd, axis=0)


def interleave(even, odd, rows):
    parts = []
    for m in range(even.shape[0] // rows):
        parts += [even[m * rows : (m + 1) * rows], odd[m * rows : (m + 1) * rows]]
    return jnp.concatenate(parts, axis=0)


def split_tiles(values, rows):
    count = values.shape[0] // rows
    pick = lambda first: jnp.concatenate(
        [values[k * rows : (k + 1) * rows] for k in range(first, count, 2)], axis=0
    )
    return pick(0), pick(1)


def join_slab(even, odd, rows, C):
    parts = []
    for m in range(even.shape[0] // rows):
        a = even[m * rows : (m + 1) * rows]
        b = odd[m * rows : (m + 1) * rows]
        parts += [a[:, :LANES], a[:, LANES:] + b[:, :LANES], b[:, LANES:]]
    return jnp.concatenate(parts, axis=1)


def message_kernel(
    tiles, C, tcol, lcol, trow, nodes_all, nodes, w1, w2, edges,
    act1, slope1, slope2, summed, p_all, p_own, w_own, total, pre1, pre2,
):
    i = pl.program_id(0)
    rows, D = nodes.shape
    count = nodes_all.shape[0]

    @pl.when(i == 0)
    def _():
        def project(part):
            p_all[part, :] = dot(nodes_all[part, :], w1[D : 2 * D, :]).astype(BF)

        by_chunks(count, project)
        p_own[...] = dot(nodes[...], w1[:D, :])
        w_own[...] = jnp.zeros_like(w_own)
        w_own[0, :C, :] = w1[2 * D :, :]
        w_own[1, 256 - C :, :] = w1[2 * D :, :]
        total[...] = jnp.zeros_like(total)
        pre1[...] = jnp.zeros_like(pre1)
        pre2[...] = jnp.zeros_like(pre2)

    last = jnp.clip(i - 2, 0, tiles - 1)
    ks = [last * GROUP + j for j in range(GROUP)]
    act, slope = gelu_pair(pre2[...])
    live = jnp.concatenate(
        [jnp.concatenate([lane_column(lcol, k)] * (D // LANES), axis=1) for k in ks], axis=0
    )
    slope2[...] = (slope * live).astype(BF)
    live = live * jnp.where(i >= 2, 1.0, 0.0)
    act = (act * live).astype(BF)
    target = jnp.concatenate([trow[pl.ds(k, 1), :] for k in ks], axis=1)
    add_by_target(target, act, total)

    act, slope = gelu_pair(pre1[...])
    act = act.astype(BF)
    act1[...] = act
    slope1[...] = slope.astype(BF)
    pre2[...] = dot(act, w2[...])

    now = jnp.minimum(i, tiles - 1)
    targets = [lane_column(tcol, now * GROUP + j) for j in range(GROUP)]
    even, odd = slab_pairs(edges[...], C)
    base = p_own[...]
    own = interleave(dot(even, w_own[0]), dot(odd, w_own[1]), rows)
    pre1[...] = gather_table(targets, p_all) + own + jnp.concatenate([base] * GROUP, axis=0)

    @pl.when(i == tiles + 1)
    def _():
        summed[...] = total[...].astype(BF)


def full(x):
    return pl.BlockSpec(
        x.shape, lambda g: (0,) * x.ndim, pipeline_mode=pl.Buffered(buffer_count=1)
    )


def message_call(C, tcol, lcol, trow, nodes_all, nodes, w1, w2, edges):
    rows, D = nodes.shape
    count = nodes_all.shape[0]
    K = edges.shape[1] // C
    tiles = K // GROUP
    size = GROUP * rows
    shape = jax.ShapeDtypeStruct
    lag = lambda d: pl.BlockSpec((size, D), lambda g: (jnp.clip(g - d, 0, tiles - 1), 0))
    return pl.pallas_call(
        functools.partial(message_kernel, tiles, C),
        grid=(tiles + 2,),
        in_specs=[full(x) for x in (tcol, lcol, trow, nodes_all, nodes, w1, w2)]
        + [pl.BlockSpec((rows, GROUP * C), lambda g: (0, jnp.minimum(g, tiles - 1)))],
        out_specs=[lag(1), lag(1), lag(2), pl.BlockSpec((count, D), lambda g: (0, 0))],
        out_shape=[shape((K * rows, D), BF)] * 3 + [shape((count, D), BF)],
        scratch_shapes=[
            pltpu.VMEM((count, D), BF),
            pltpu.VMEM((rows, D), F32),
            pltpu.VMEM((2, 256, D), BF),
            pltpu.VMEM((count, D), F32),
            pltpu.VMEM((size, D), F32),
            pltpu.VMEM((size, D), F32),
        ],
        compiler_params=LOCAL,
    )(tcol, lcol, trow, nodes_all, nodes, w1, w2, edges)


def column_of(row):
    return jnp.transpose(jnp.broadcast_to(row, (LANES, row.shape[1])))


def spread(column, width):
    return jnp.concatenate([column] * (width // LANES), axis=1)


def norm_parts(values):
    centred = values - row_mean(values)
    inverse = lax.rsqrt(row_mean(centred * centred) + EPS)
    return centred * inverse, inverse


def node_kernel(
    n, C, summed, count, nodes, w3, g1, o1, wf1, wf2, g2, o2, we1,
    node_out, far_all, near, low_out, n1_out, n2_out, inv_out, act_out, slope_out, sum_out,
    pair_buf, send_buf, far_buf, q_own, send, recv, gsend, grecv, own_sem,
):
    place = Place(n)
    rows, D = nodes.shape
    greet([place.sibling] + place.mates)
    total = scatter_sum(place, summed, pair_buf, send_buf, far_buf, send, recv).astype(BF)
    sum_out[...] = total
    divisor = 1.0 + column_of(count[0:1, :])
    inv_out[2] = divisor
    resid = nodes[...].astype(F32) + dot(total, w3[...]) / spread(divisor, D)
    n1, inv1 = norm_parts(resid)
    n1_out[...] = n1
    inv_out[0] = jnp.broadcast_to(inv1, (rows, LANES))
    normed = n1 * g1[...] + o1[...]
    low = normed.astype(BF)
    low_out[...] = low
    act, slope = gelu_pair(dot(low, wf1[...]))
    act = act.astype(BF)
    act_out[...] = act
    slope_out[...] = slope.astype(BF)
    n2, inv2 = norm_parts(normed + dot(act, wf2[...]))
    n2_out[...] = n2
    inv_out[1] = jnp.broadcast_to(inv2, (rows, LANES))
    node_low = (n2 * g2[...] + o2[...]).astype(BF)
    node_out[...] = node_low
    pad = jnp.zeros((rows, 256 - C), F32)
    far = dot(node_low, we1[D : 2 * D, :])
    q_own[...] = jnp.concatenate([far, pad], axis=1).astype(BF)
    handles = gather_start(place, q_own, far_all, gsend, grecv)
    own = pltpu.make_async_copy(q_own, block(far_all, place.me, rows), own_sem.at[0])
    own.start()
    near[...] = jnp.concatenate([dot(node_low, we1[:D, :]), pad], axis=1)
    own.wait()
    gather_finish(place, handles, q_own, far_all, gsend, grecv)


def node_call(n, C, summed, count, nodes, w3, g1, o1, wf1, wf2, g2, o2, we1):
    rows, D = nodes.shape
    FF = wf1.shape[1]
    shape = jax.ShapeDtypeStruct
    return pl.pallas_call(
        functools.partial(node_kernel, n, C),
        in_specs=[WHOLE] * 11,
        out_specs=[WHOLE] * 10,
        out_shape=[
            shape((rows, D), BF),
            shape((n * rows, 256), BF),
            shape((rows, 256), F32),
            shape((rows, D), BF),
            shape((rows, D), F32),
            shape((rows, D), F32),
            shape((3, rows, LANES), F32),
            shape((rows, FF), BF),
            shape((rows, FF), BF),
            shape((rows, D), BF),
        ],
        scratch_shapes=[
            *comm_scratch(n, rows, D),
            pltpu.VMEM((rows, 256), BF),
            *sems(n),
            *sems(n),
            pltpu.SemaphoreType.DMA((1,)),
        ],
        compiler_params=remote_params(1),
    )(summed, count, nodes, w3, g1, o1, wf1, wf2, g2, o2, we1)


def edge_kernel(
    tiles, C, tcol, trow, far_all, near, we1, we2, we3, gain, offset, edges, cot,
    edge_out, partial, far_sum, near_sum, dw1, dw2, dw3, dgain,
    w1o, w2p, w3o, w1t, w2t, w3t, gains, total, a1, a2, a3, ag,
):
    g = pl.program_id(0)
    rows = near.shape[0]
    D2 = we1.shape[0] - C
    gap = 256 - C

    @pl.when(g == 0)
    def _():
        for ref in (w1o, w2p, w3o, w1t, w2t, w3t, gains, total, a1, a2, a3, ag, near_sum):
            ref[...] = jnp.zeros_like(ref)
        own = we1[D2:, :]
        w1o[0, :C, :C] = own
        w1o[1, gap:, :C] = own
        w2p[:C, :C] = we2[...]
        w3o[0, :C, :C] = we3[...]
        w3o[1, :C, :] = jnp.concatenate([jnp.zeros((C, gap), F32), we3[...].astype(F32)], axis=1).astype(BF)
        for s in range(2):
            w1t[s] = jnp.transpose(w1o[s].astype(F32)).astype(BF)
            w3t[s] = jnp.transpose(w3o[s].astype(F32)).astype(BF)
        w2t[...] = jnp.transpose(w2p[...].astype(F32)).astype(BF)
        zero = jnp.zeros((1, gap), F32)
        gains[0, 0:1] = jnp.concatenate([gain[...], zero], axis=1)
        gains[0, 1:2] = jnp.concatenate([offset[...], zero], axis=1)
        gains[1, 0:1] = jnp.concatenate([zero, gain[...]], axis=1)
        gains[1, 1:2] = jnp.concatenate([zero, offset[...]], axis=1)

    ks = [g * GROUP + j for j in range(GROUP)]
    slabs = slab_pairs(edges[...], C)
    cots = slab_pairs(cot[...], C)
    half = slabs[0].shape[0]
    own = interleave(dot(slabs[0], w1o[0]), dot(slabs[1], w1o[1]), rows)
    base = near[...]
    pre1 = gather_table([lane_column(tcol, k) for k in ks], far_all)
    pre1 = pre1 + own + jnp.concatenate([base] * GROUP, axis=0)
    h1, s1 = gelu_pair(pre1)
    h1 = h1.astype(BF)
    h2, s2 = gelu_pair(dot(h1, w2p[...]))
    h2 = h2.astype(BF)
    h2s = split_tiles(h2, rows)
    lane = lax.broadcasted_iota(I32, (half, 256), 1)
    outs, thirds, lows = [], [], []
    for s in range(2):
        inside = (lane < C) if s == 0 else (lane >= gap)
        keep = lambda v: jnp.where(inside, v, 0.0)
        mean = lambda v: jnp.sum(v, axis=-1, keepdims=True) * (1.0 / C)
        value = keep(slabs[s].astype(F32)) + dot(h2s[s], w3o[s])
        centred = keep(value - mean(value))
        inverse = lax.rsqrt(mean(centred * centred) + EPS)
        normal = centred * inverse
        outs.append(normal * gains[s, 0:1] + gains[s, 1:2])
        upstream = keep(cots[s].astype(F32))
        moved = upstream * normal
        for r in range(half // rows):
            part = slice(r * rows, (r + 1) * rows)
            ag[s, 0] += moved[part]
            ag[s, 1] += upstream[part]
        scaled = upstream * gains[s, 0:1]
        third = inverse * (scaled - mean(scaled) - normal * mean(scaled * normal))
        third = keep(third)
        thirds.append(third)
        low = third.astype(BF)
        lows.append(low)
        a3[s] += dot_tn(h2s[s], low)
    edge_out[...] = join_slab(outs[0], outs[1], rows, C).astype(BF)
    low2 = interleave(dot(lows[0], w3t[0]), dot(lows[1], w3t[1]), rows)
    low2 = (low2 * s2).astype(BF)
    a2[...] += dot_tn(h1, low2)
    low1 = (dot(low2, w2t[...]) * s1).astype(BF)
    low1s = split_tiles(low1, rows)
    for s in range(2):
        a1[s] += dot_tn(low1s[s], slabs[s])
        thirds[s] = thirds[s] + dot(low1s[s], w1t[s])
    partial[...] = join_slab(thirds[0], thirds[1], rows, C)
    wide = low1.astype(F32)
    acc = wide[:rows]
    for j in range(1, GROUP):
        acc = acc + wide[j * rows : (j + 1) * rows]
    near_sum[...] += acc
    target = jnp.concatenate([trow[pl.ds(k, 1), :] for k in ks], axis=1)
    add_by_target(target, low1, total)

    @pl.when(g == tiles - 1)
    def _():
        far_sum[...] = total[...].astype(BF)
        dw1[...] = (jnp.transpose(a1[0])[:C,:] + jnp.transpose(a1[1])[gap:,:])
        dw2[...] = a2[...]
        shifted = a3[1][:, gap:]
        dw3[...] = a3[0] + jnp.concatenate([shifted, jnp.zeros((256, gap), F32)], axis=1)
        for r in range(2):
            even = jnp.sum(ag[0, r], axis=0, keepdims=True)
            odd = jnp.sum(ag[1, r], axis=0, keepdims=True)
            row = even + jnp.concatenate([odd[:, gap:], jnp.zeros((1, gap), F32)], axis=1)
            dgain[r * 8 : r * 8 + 8, :] = jnp.broadcast_to(row, (8, 256))


def edge_call(C, tcol, trow, far_all, near, we1, we2, we3, gain, offset, edges, cot):
    rows = near.shape[0]
    count = far_all.shape[0]
    K = edges.shape[1] // C
    tiles = K // GROUP
    shape = jax.ShapeDtypeStruct
    slab = pl.BlockSpec((rows, GROUP * C), lambda g: (0, g))
    fixed = lambda *s: pl.BlockSpec(s, lambda g: (0,) * len(s))
    return pl.pallas_call(
        functools.partial(edge_kernel, tiles, C),
        grid=(tiles,),
        in_specs=[full(x) for x in (tcol, trow, far_all, near, we1, we2, we3, gain, offset)]
        + [slab, slab],
        out_specs=[
            slab, slab, fixed(count, 256), fixed(rows, 256),
            fixed(C, 256), fixed(256, 256), fixed(256, 256), fixed(16, 256),
        ],
        out_shape=[
            shape((rows, K * C), BF),
            shape((rows, K * C), F32),
            shape((count, 256), BF),
            shape((rows, 256), F32),
            shape((C, 256), F32),
            shape((256, 256), F32),
            shape((256, 256), F32),
            shape((16, 256), F32),
        ],
        scratch_shapes=[
            pltpu.VMEM((2, 256, 256), BF),
            pltpu.VMEM((256, 256), BF),
            pltpu.VMEM((2, 256, 256), BF),
            pltpu.VMEM((2, 256, 256), BF),
            pltpu.VMEM((256, 256), BF),
            pltpu.VMEM((2, 256, 256), BF),
            pltpu.VMEM((2, 8, 256), F32),
            pltpu.VMEM((count, 256), F32),
            pltpu.VMEM((2, 256, 256), F32),
            pltpu.VMEM((256, 256), F32),
            pltpu.VMEM((2, 256, 256), F32),
            pltpu.VMEM((2, 2, rows, 256), F32),
        ],
        compiler_params=LOCAL,
    )(tcol, trow, far_all, near, we1, we2, we3, gain, offset, edges, cot)


def norm_back(upstream, normal, inverse, gain):
    scaled = upstream * gain
    return inverse * (scaled - row_mean(scaled) - normal * row_mean(scaled * normal))


def node_back_kernel(
    n, C, far_sum, near_sum, cot, node_low, n1, n2, inv, act, slope, low, summed,
    w3, g1, wf1, wf2, g2, we1,
    grad_one, vw_all, resid_out, dgain, dw3, dwe_near, dwe_far,
    pair_buf, send_buf, far_buf, v_own, send, recv, gsend, grecv, own_sem,
):
    place = Place(n)
    rows, D = cot.shape
    greet([place.sibling] + place.mates)
    far = scatter_sum(place, far_sum, pair_buf, send_buf, far_buf, send, recv)
    far = far.astype(BF)[:, :C]
    near = near_sum[...].astype(BF)[:, :C]
    grad = cot[...].astype(F32) + dot_nt(near, we1[:D, :]) + dot_nt(far, we1[D : 2 * D, :])
    two = norm_back(grad, n2[...], inv[1][:, 0:1], g2[...])
    dgain[16:24, :] = jnp.broadcast_to(jnp.sum(grad * n2[...], axis=0, keepdims=True), (8, D))
    dgain[24:32, :] = jnp.broadcast_to(jnp.sum(grad, axis=0, keepdims=True), (8, D))
    resid = two.astype(BF)
    resid_out[...] = resid
    inner = (dot_nt(resid, wf2[...]) * slope[...].astype(F32)).astype(BF)
    grad = two + dot_nt(inner, wf1[...])
    one = norm_back(grad, n1[...], inv[0][:, 0:1], g1[...])
    dgain[0:8, :] = jnp.broadcast_to(jnp.sum(grad * n1[...], axis=0, keepdims=True), (8, D))
    dgain[8:16, :] = jnp.broadcast_to(jnp.sum(grad, axis=0, keepdims=True), (8, D))
    grad_one[...] = one
    upper = (one / spread(inv[2], D)).astype(BF)
    v_own[...] = dot_nt(upper, w3[...]).astype(BF)
    handles = gather_start(place, v_own, vw_all, gsend, grecv)
    own = pltpu.make_async_copy(v_own, block(vw_all, place.me, rows), own_sem.at[0])
    own.start()
    dw3[...] = dot_tn(summed[...], upper)
    dwe_near[...] = dot_tn(node_low[...], near)
    dwe_far[...] = dot_tn(node_low[...], far)
    own.wait()
    gather_finish(place, handles, v_own, vw_all, gsend, grecv)


def node_back_call(n, C, *args):
    cot, wf1 = args[2], args[13]
    rows, D = cot.shape
    shape = jax.ShapeDtypeStruct
    return pl.pallas_call(
        functools.partial(node_back_kernel, n, C),
        in_specs=[WHOLE] * len(args),
        out_specs=[WHOLE] * 7,
        out_shape=[
            shape((rows, D), F32),
            shape((n * rows, D), BF),
            shape((rows, D), BF),
            shape((32, D), F32),
            shape((D, D), F32),
            shape((D, C), F32),
            shape((D, C), F32),
        ],
        scratch_shapes=[
            *comm_scratch(n, rows, 256),
            pltpu.VMEM((rows, D), BF),
            *sems(n),
            *sems(n),
            pltpu.SemaphoreType.DMA((1,)),
        ],
        compiler_params=remote_params(2),
    )(*args)


def message_back_kernel(
    tiles, C, tcol, trow, nodes, vw, w1, w2,
    act1, slope1, slope2, edges, partial,
    grad_edges, dw1, dw2, target_sum, source_sum,
    w2t, w_own, w_own_t, total, a2, ae,
):
    g = pl.program_id(0)
    rows, D = nodes.shape
    gap = 256 - C

    @pl.when(g == 0)
    def _():
        for ref in (w_own, total, a2, ae, source_sum):
            ref[...] = jnp.zeros_like(ref)
        w_own[0, :C, :] = w1[2 * D :, :]
        w_own[1, gap:, :] = w1[2 * D :, :]
        for s in range(2):
            w_own_t[s] = jnp.transpose(w_own[s].astype(F32)).astype(BF)
        w2t[...] = jnp.transpose(w2[...].astype(F32)).astype(BF)

    ks = [g * GROUP + j for j in range(GROUP)]
    up = gather_table([lane_column(tcol, k) for k in ks], vw)
    upper = (up * slope2[...].astype(F32)).astype(BF)
    a2[...] += dot_tn(act1[...], upper)
    lower = (dot(upper, w2t[...]) * slope1[...].astype(F32)).astype(BF)
    wide = lower.astype(F32)
    acc = wide[:rows]
    for j in range(1, GROUP):
        acc = acc + wide[j * rows : (j + 1) * rows]
    source_sum[...] += acc
    target = jnp.concatenate([trow[pl.ds(k, 1), :] for k in ks], axis=1)
    add_by_target(target, lower, total)
    slabs = slab_pairs(edges[...], C)
    lowers = split_tiles(lower, rows)
    own = []
    for s in range(2):
        ae[s] += dot_tn(slabs[s], lowers[s])
        own.append(dot(lowers[s], w_own_t[s]))
    grad_edges[...] = partial[...] + join_slab(own[0], own[1], rows, C)

    @pl.when(g == tiles - 1)
    def _():
        target_sum[...] = total[...].astype(BF)
        dw2[...] = a2[...].astype(BF)
        dw1[:D, :] = dot_tn(nodes[...], source_sum[...].astype(BF)).astype(BF)
        dw1[D:, :] = (ae[0][:C, :] + ae[1][gap:, :]).astype(BF)


def message_back_call(C, tcol, trow, nodes, vw, w1, w2, act1, slope1, slope2, edges, partial):
    rows, D = nodes.shape
    count = vw.shape[0]
    K = edges.shape[1] // C
    tiles = K // GROUP
    size = GROUP * rows
    shape = jax.ShapeDtypeStruct
    slab = pl.BlockSpec((rows, GROUP * C), lambda g: (0, g))
    tile = pl.BlockSpec((size, D), lambda g: (g, 0))
    fixed = lambda *s: pl.BlockSpec(
        s, lambda g: (0,) * len(s), pipeline_mode=pl.Buffered(buffer_count=1)
    )
    return pl.pallas_call(
        functools.partial(message_back_kernel, tiles, C),
        grid=(tiles,),
        in_specs=[full(x) for x in (tcol, trow, nodes, vw, w1, w2)]
        + [tile, tile, tile, slab, slab],
        out_specs=[slab, fixed(D + C, D), fixed(D, D), fixed(count, D), fixed(rows, D)],
        out_shape=[
            shape((rows, K * C), F32),
            shape((D + C, D), BF),
            shape((D, D), BF),
            shape((count, D), BF),
            shape((rows, D), F32),
        ],
        scratch_shapes=[
            pltpu.VMEM((D, D), BF),
            pltpu.VMEM((2, 256, D), BF),
            pltpu.VMEM((2, D, 256), BF),
            pltpu.VMEM((count, D), F32),
            pltpu.VMEM((D, D), F32),
            pltpu.VMEM((2, 256, D), F32),
        ],
        compiler_params=LOCAL,
    )(tcol, trow, nodes, vw, w1, w2, act1, slope1, slope2, edges, partial)


def feed_kernel(low, resid, wf1, wf2, dwf1, dwf2):
    @pl.when(pl.program_id(1) == 0)
    def _():
        dwf1[...] = jnp.zeros_like(dwf1)
        dwf2[...] = jnp.zeros_like(dwf2)

    act, slope = gelu_pair(dot(low[...], wf1[...]))
    dwf2[...] += dot_tn(act.astype(BF), resid[...])
    inner = (dot_nt(resid[...], wf2[...]) * slope).astype(BF)
    dwf1[...] += dot_tn(low[...], inner)


def feed_call(both, wf1, wf2):
    count = both.shape[0]
    D, FF = wf1.shape
    step, rows = min(FF, 512), min(count, TABLE)
    shape = jax.ShapeDtypeStruct
    return pl.pallas_call(
        feed_kernel,
        grid=(FF // step, count // rows),
        in_specs=[
            pl.BlockSpec((rows, D), lambda f, r: (r, 0)),
            pl.BlockSpec((rows, D), lambda f, r: (r, 1)),
            pl.BlockSpec((D, step), lambda f, r: (0, f)),
            pl.BlockSpec((step, D), lambda f, r: (f, 0)),
        ],
        out_specs=[
            pl.BlockSpec((D, step), lambda f, r: (0, f)),
            pl.BlockSpec((step, D), lambda f, r: (f, 0)),
        ],
        out_shape=[shape((D, FF), F32), shape((FF, D), F32)],
        compiler_params=LOCAL,
    )(both, both, wf1, wf2)


def total_kernel(n, pieces, lag, x, out, pair_buf, low_buf, high_buf, send_buf, send, recv):
    place = Place(n)
    chips, c, q = place.chips, place.chip, place.core
    root = chips // 2 - 1 + q
    right = jnp.minimum(c + 1, chips - 1) * 2 + q
    left = jnp.maximum(c - 1, 0) * 2 + q
    half = x.shape[0] // 2
    rows = half // pieces
    barrier = pltpu.get_barrier_semaphore()

    def hello(peer):
        pl.semaphore_signal(barrier, inc=1, device_id={"edge": peer}, device_id_type=MESH)

    hello(place.sibling)
    pl.when(c > 0)(lambda: hello(left))
    pl.when(c < chips - 1)(lambda: hello(right))
    inner = jnp.where((c > 0) & (c < chips - 1), 1, 0)
    pl.semaphore_wait(barrier, 2 + inner)

    def part(which, p):
        return pl.ds(pl.multiple_of(which * half + p * rows, rows), rows)

    def local(p):
        return pl.ds(p * rows, rows)

    def link(src, dst, p, sent, got, peer):
        return remote(src, dst, send.at[sent * pieces + p], recv.at[got * pieces + p], peer)

    def pair(p):
        return link(x.at[part(1 - q, p)], pair_buf.at[local(p)], p, 0, 0, place.sibling)

    def up(p):
        return link(send_buf.at[local(p)], low_buf.at[local(p)], p, 1, 1, right)

    def down(p):
        return link(send_buf.at[local(p)], high_buf.at[local(p)], p, 2, 2, left)

    def out_left(p):
        return link(out.at[part(q, p)], out.at[part(q, p)], p, 3, 3, left)

    def out_right(p):
        return link(out.at[part(q, p)], out.at[part(q, p)], p, 5, 3, right)

    def across(p):
        return link(out.at[part(q, p)], out.at[part(q, p)], p, 4, 4, place.sibling)

    for p in range(pieces):
        pair(p).start()

    def reduce(p):
        pair(p).wait_recv()
        here = local(p)
        mine = lambda: x[part(q, p), :].astype(F32) + pair_buf[here, :].astype(F32)

        def from_left():
            def first():
                send_buf[here, :] = mine().astype(BF)

            def inner():
                up(p).wait_recv()
                send_buf[here, :] = (mine() + low_buf[here, :].astype(F32)).astype(BF)

            pl.when(c == 0)(first)
            pl.when(c > 0)(inner)
            up(p).start()

        def from_right():
            def first():
                send_buf[here, :] = mine().astype(BF)

            def inner():
                down(p).wait_recv()
                send_buf[here, :] = (mine() + high_buf[here, :].astype(F32)).astype(BF)

            pl.when(c == chips - 1)(first)
            pl.when(c < chips - 1)(inner)
            down(p).start()

        def at_root():
            up(p).wait_recv()
            down(p).wait_recv()
            total = mine() + low_buf[here, :].astype(F32) + high_buf[here, :].astype(F32)
            out[part(q, p), :] = total.astype(BF)
            out_left(p).start()
            out_right(p).start()
            across(p).start()

        pl.when(c < root)(from_left)
        pl.when(c > root)(from_right)
        pl.when(c == root)(at_root)

    def spread_out(p):
        def leftward():
            out_left(p).wait_recv()
            pl.when(c > 0)(lambda: out_left(p).start())
            across(p).start()

        def rightward():
            out_right(p).wait_recv()
            pl.when(c < chips - 1)(lambda: out_right(p).start())
            across(p).start()

        pl.when(c < root)(leftward)
        pl.when(c > root)(rightward)

    for s in range(pieces + lag):
        if s < pieces:
            reduce(s)
        if s >= lag:
            spread_out(s - lag)
    for p in range(pieces):
        across(p).wait_recv()
    for p in range(pieces):
        pair(p).wait_send()
        across(p).wait_send()
        pl.when(c < root)(lambda: up(p).wait_send())
        pl.when(c > root)(lambda: down(p).wait_send())
        pl.when((c <= root) & (c > 0))(lambda: out_left(p).wait_send())
        pl.when((c >= root) & (c < chips - 1))(lambda: out_right(p).wait_send())


def total_call(n, x, pieces, lag):
    rows, width = x.shape
    return pl.pallas_call(
        functools.partial(total_kernel, n, pieces, lag),
        in_specs=[WHOLE],
        out_specs=WHOLE,
        out_shape=jax.ShapeDtypeStruct(x.shape, x.dtype),
        scratch_shapes=[pltpu.VMEM((rows // 2, width), BF)] * 4 + sems(6 * pieces),
        compiler_params=remote_params(3),
    )(x)


def final_kernel(n, target_sum, source_sum, grad_one, w1, nodes, out, dw1, pair_buf, send_buf, far_buf, send, recv):
    place = Place(n)
    D = grad_one.shape[1]
    greet([place.sibling] + place.mates)
    total = scatter_sum(place, target_sum, pair_buf, send_buf, far_buf, send, recv)
    source = dot_nt(source_sum[...].astype(BF), w1[:D, :])
    total = total.astype(BF)
    out[...] = grad_one[...] + source + dot_nt(total, w1[D : 2 * D, :])
    dw1[...] = dot_tn(nodes[...], total).astype(BF)


def final_call(n, target_sum, source_sum, grad_one, w1, nodes):
    rows, D = grad_one.shape
    return pl.pallas_call(
        functools.partial(final_kernel, n),
        in_specs=[WHOLE] * 5,
        out_specs=[WHOLE] * 2,
        out_shape=[jax.ShapeDtypeStruct((rows, D), F32), jax.ShapeDtypeStruct((D, D), BF)],
        scratch_shapes=[*comm_scratch(n, rows, D), *sems(n)],
        compiler_params=remote_params(4),
    )(target_sum, source_sum, grad_one, w1, nodes)


def body(
    nodes, edges, nbr_owner, nbr_slot, edge_mask, w_msg1, w_msg2, w_msg3, gain_one, offset_one,
    w_ffn1, w_ffn2, gain_two, offset_two, w_edge1, w_edge2, w_edge3, gain_three, offset_three,
    node_cotangent, edge_cotangent,
):
    n = lax.axis_size("edge")
    rows, D = nodes.shape
    C = w_edge2.shape[0]
    K = nbr_slot.shape[1]
    g1, o1, g2, o2 = (v.reshape(1, D) for v in (gain_one, offset_one, gain_two, offset_two))
    nodes_all, tcol, lcol, trow, count = start_call(
        n, nodes, nbr_owner.reshape(rows, K), nbr_slot, edge_mask
    )
    act1, slope1, slope2, summed = message_call(
        C, tcol, lcol, trow, nodes_all, nodes, w_msg1, w_msg2, edges
    )
    node_out, far_all, near, low, n1, n2, inv, act, slope, own_sum = node_call(
        n, C, summed, count, nodes, w_msg3, g1, o1, w_ffn1, w_ffn2, g2, o2, w_edge1
    )
    edge_out, partial, far_sum, near_sum, dwe1, dwe2, dwe3, dg3 = edge_call(
        C, tcol, trow, far_all, near, w_edge1, w_edge2, w_edge3,
        gain_three.reshape(1, C), offset_three.reshape(1, C), edges, edge_cotangent,
    )
    grad_one, vw_all, resid, dgain, dw3, dwe_near, dwe_far = node_back_call(
        n, C, far_sum, near_sum, node_cotangent, node_out, n1, n2, inv, act, slope, low, own_sum,
        w_msg3, g1, w_ffn1, w_ffn2, g2, w_edge1,
    )
    both = lax.all_gather(jnp.concatenate([low, resid], axis=1), "edge", axis=0, tiled=True)
    small = jnp.concatenate(
        [dgain[0::8], jnp.concatenate([dg3[0::8], jnp.zeros((2, D - 256), F32)], axis=1)], axis=0
    )
    small = lax.psum(small, "edge")
    grad_edges, dw1, dw2, target_sum, source_sum = message_back_call(
        C, tcol, trow, nodes, vw_all, w_msg1, w_msg2, act1, slope1, slope2, edges, partial,
    )
    dwf1, dwf2 = feed_call(both, w_ffn1, w_ffn2)
    grad_nodes, dw1t = final_call(n, target_sum, source_sum, grad_one, w_msg1, nodes)
    wide = lambda v: jnp.pad(v, ((0, 0), (0, 256 - v.shape[1])))
    edge1 = jnp.concatenate([wide(dwe_near), wide(dwe_far), dwe1], axis=0).astype(BF)
    split = edge1.shape[0] // 2
    edge1 = jnp.concatenate([edge1[:split], edge1[split:]], axis=1)
    edge23 = jnp.concatenate([dwe2[:C], dwe3[:C]], axis=1).astype(BF)
    packed = jnp.concatenate([dw1[:D], dw1t, dw1[D:], dw2, dw3.astype(BF), edge1, edge23], axis=0)
    packed = total_call(n, packed, 5, 4).astype(F32)
    at = 0
    pieces = []
    for size in (2 * D + C, D, D, split, C):
        pieces.append(packed[at : at + size])
        at += size
    tot1, tot2, tot3, tot_e1, tot_e23 = pieces
    grad_we1 = jnp.concatenate([tot_e1[:, :C], tot_e1[:, 256 : 256 + C]], axis=0)
    return (
        node_out, edge_out, grad_nodes, grad_edges,
        tot1, tot2, tot3, small[0], small[1], dwf1, dwf2, small[2], small[3],
        grad_we1, tot_e23[:, :C], tot_e23[:, 256 : 256 + C], small[4, :C], small[5, :C],
    )


def solution(mesh):
    rows = P(("dp", "edge"), None)
    return jax.shard_map(
        body,
        mesh=mesh,
        in_specs=(rows, rows, P(("dp", "edge"), None, None), rows, rows)
        + (P(),) * 14
        + (rows, rows),
        out_specs=(rows,) * 4
        + (P("dp", None),) * 3
        + (P("dp"),) * 2
        + (P("dp", None),) * 2
        + (P("dp"),) * 2
        + (P("dp", None),) * 3
        + (P("dp"),) * 2,
        check_vma=False,
    )
```

time: 2760 us -> 384 us (0.14)
  local copies, waits for them, and re-layouts: 849 us -> 25.2 us
  waiting for transfers between devices: 755 us -> 0.02 us
  other arithmetic: 427 us -> 5.71 us
  matrix products: 340 us -> 0 us
  Pallas kernels: 0 us -> 312 us
  blocking collectives: 326 us -> 26.4 us
  starting transfers between devices: 39 us -> 0.04 us
    all_to_all x7 -> x0, waiting for transfers between devices: 755 us -> none  [the longest x1 258 us: body(): lax.all_to_all(back_rows.reshape(peer_count, capacity, node_width), 'edge...]
    gather x11 -> x0, local copies, waits for them, and re-layouts: 478 us -> none  [the longest x1 73.7 us: body(): slot_code = jnp.where(filled, code_flat[slot_safe], -1)]
    dot_general x27 -> x0, matrix products: 340 us -> none  [the longest x8 123 us: product_nt(): lax.dot_general(left, right, (((1,), (1,)), ((), ())), preferred_element_...]
    all_to_all x3 -> x0, other arithmetic: 330 us -> none  [the longest x2 220 us: body(): lax.all_to_all(edge_grads, 'edge', split_axis=0, concat_axis=0, tiled=True)]
    pallas_call x0 -> x9, Pallas kernels: none -> 312 us  [the longest x1 71 us: total_call(): pl.pallas_call(functools.partial(total_kernel, n, pieces, lag), in_specs=...]
    psum x1, blocking collectives: 326 us -> 26.4 us  [body(): small = lax.psum(small, 'edge')]
    unnamed x223 -> x35, local copies, waits for them, and re-layouts: 123 us -> 13.6 us
    reshape x9 -> x0, local copies, waits for them, and re-layouts: 78.8 us -> none  [the longest x1 15.3 us: body(): grad_edge_join[:, :node_width].reshape(row_count, fanout, node_width)]
  transfers between devices with their start and end apart: 8 -> 1, of which waited for: 5 -> 0; matrix products, arithmetic and copies ran while one was open for 31% -> 5% of each run, Pallas kernels for 0% -> 33%
where the time goes in v1:
time: 384 us; the launch traced here: 383 us
  Pallas kernels  312 us (81%)
  blocking collectives  26.4 us (7%)
  local copies, waits for them, and re-layouts  25.2 us (7%)
  between operations  14.3 us (4%)
  other arithmetic  5.71 us (1%)
    pallas_call x1, Pallas kernels, total_call(): pl.pallas_call(functools.partial(total_kernel, n, pieces, lag), in_specs=...  71 us
    pallas_call x1, Pallas kernels, edge_call(): pl.pallas_call(functools.partial(edge_kernel, tiles, C), grid=(tiles,), i...  43.7 us
    pallas_call x1, Pallas kernels, message_call(): pl.pallas_call(functools.partial(message_kernel, tiles, C), grid=(tiles +...  43.1 us
    pallas_call x1, Pallas kernels, message_back_call(): pl.pallas_call(functools.partial(message_back_kernel, tiles, C), grid=(ti...  37.5 us
    pallas_call x1, Pallas kernels, node_back_call(): pl.pallas_call(functools.partial(node_back_kernel, n, C), in_specs=[WHOLE...  30.3 us
    pallas_call x1, Pallas kernels, node_call(): pl.pallas_call(functools.partial(node_kernel, n, C), in_specs=[WHOLE] * 1...  29.9 us
    psum x1, blocking collectives, body(): small = lax.psum(small, 'edge')  26.4 us
    pallas_call x1, Pallas kernels, start_call(): pl.pallas_call(functools.partial(start_kernel, n, K), in_specs=[WHOLE] *...  22 us
  transfers between devices with their start and end apart: 1, of which 0 were waited for; matrix products, arithmetic and copies ran while one was open for 5% of the time, Pallas kernels for 33%

profile of v1, /device:TPU:0, one launch (start us, length us, event | category | flops | bytes accessed | tf_op | source)
XLA Modules:
  0.0 383.4 jit_solution(2498783389481068905)
XLA Ops:
  7.2 1.5 copy.39
  8.7 1.5 copy.40.slot
  10.2 1.5 copy.41.live
  11.7 2.1 copy.42.we1
  13.8 22.0 %shard_map.340 = (bf16[1024,512]{1,0:T(8,128)(2,1)}, s32[128,128]{1,0:T(8,128)}, f32[128,128]{1,0:T(8,128)}, s32[128,128]{1,0:T(8,128)}, f32[8,128]{1,0:T(8,128)}) custom-call(bf16[128,512]{1,0:T(8,128)(2,1)} %nodes.9, s32[128,52]{1,0:T(8,128)} %bitcast.13, s32[128,52]{1,0:T(8,128)} %copy.40.slot, s32[128,52]{1,0:T(8,128)} %copy.41.live), custom_call_target="tpu_custom_call" | custom-call | tf_op jit(solution)/shard_map/pallas_call | solution.py:286
  35.7 43.1 %shard_map.341 = (bf16[6656,512]{1,0:T(8,128)(2,1)}, bf16[6656,512]{1,0:T(8,128)(2,1)}, bf16[6656,512]{1,0:T(8,128)(2,1)}, bf16[1024,512]{1,0:T(8,128)(2,1)}) custom-call(s32[128,128]{1,0:T(8,128)} %get-tuple-element.61.tcol, f32[128,128]{1,0:T(8,128)} %get-tuple-element.62.lcol, s32[128,128]{1,0:T(8,128)} %get-tuple-element.63.trow, ...), custom_call_target="tpu_custom_call" | custom-call | tf_op jit(solution)/shard_map/pallas_call | solution.py:408
  78.8 29.9 %shard_map.342 = (bf16[128,512]{1,0:T(8,128)(2,1)}, bf16[1024,256]{1,0:T(8,128)(2,1)}, f32[128,256]{1,0:T(8,128)}, bf16[128,512]{1,0:T(8,128)(2,1)}, f32[128,512...) custom-call(bf16[1024,512]{1,0:T(8,128)(2,1)} %get-tuple-element.65., ...), custom_call_target="tpu_custom_call" | custom-call | tf_op jit(solution)/shard_map/pallas_call | solution.py:484
  108.7 43.7 %shard_map.343 = (bf16[128,9984]{1,0:T(8,128)(2,1)}, f32[128,9984]{1,0:T(8,128)}, bf16[1024,256]{1,0:T(8,128)(2,1)}, f32[128,256]{1,0:T(8,128)}, f32[192,256]{1,...) custom-call(s32[128,128]{1,0:T(8,128)} %get-tuple-element.61.tcol, ...), custom_call_target="tpu_custom_call" | custom-call | tf_op jit(solution)/shard_map/pallas_call | solution.py:618
  152.5 30.3 %shard_map.344 = (f32[128,512]{1,0:T(8,128)}, bf16[1024,512]{1,0:T(8,128)(2,1)}, bf16[128,512]{1,0:T(8,128)(2,1)}, f32[32,512]{1,0:T(8,128)}, f32[512,512]{1,0:T...) custom-call(bf16[1024,256]{1,0:T(8,128)(2,1)} %get-tuple-element.71.far_sum, f32[128,256]{1,0:T(8,128)} %get-tuple-element.72.near_sum, ...), custom_call_target="tpu_custom_call" | custom-call | tf_op jit(solution)/shard_map/pallas_call | solution.py:700
  182.8 1.6 pad_maximum_fusion.2
  185.5 1.1 convert.21
  187.3 1.6 slice.113
  188.9 1.6 slice.114
  190.5 37.5 %shard_map.345 = (f32[128,9984]{1,0:T(8,128)}, bf16[704,512]{1,0:T(8,128)(2,1)}, bf16[512,512]{1,0:T(8,128)(2,1)}, bf16[1024,512]{1,0:T(8,128)(2,1)}, f32[128,512]{1,0:T(8,128)}) custom-call(s32[128,128]{1,0:T(8,128)} %get-tuple-element.61.tcol, s32[128,128]{1,0:T(8,128)} %get-tuple-element.63.trow, bf16[128,512]{1,0:T(8,128)(2,1)} %nodes.9, ...), custom_call_target="tpu_custom_call" | custom-call | tf_op jit(solution)/shard_map/pallas_call | solution.py:784
  228.0 19.8 %shard_map.346 = (f32[128,512]{1,0:T(8,128)}, bf16[512,512]{1,0:T(8,128)(2,1)}) custom-call(bf16[1024,512]{1,0:T(8,128)(2,1)} %get-tuple-element.85.target_sum, f32[128,512]{1,0:T(8,128)} %get-tuple-element.86.source_sum, f32[128,512]{1,0:T(8,128)} %get-tuple-element.87.grad_one, bf16[1216,512]{1,0:T(8,128)(2,1)} %w1.5, bf16[128,512]{1,0:T(8,128)(2,1)} %nodes.9), custom_call_target="tpu_custom_call" | custom-call | tf_op jit(solution)/shard_map/pallas_call | solution.py:990
  247.9 1.2 constant_dynamic-update-slice_fusion.1
  249.5 1.6 copy-done.1
  251.1 71.0 %shard_map.347 = bf16[3040,512]{1,0:T(8,128)(2,1)} custom-call(bf16[3040,512]{1,0:T(8,128)(2,1)} %copy-done.1), custom_call_target="tpu_custom_call" | custom-call | tf_op jit(solution)/shard_map/pallas_call | solution.py:967
  322.1 3.2 slice.96
  325.5 1.1 pad_maximum_fusion
  326.6 2.6 copy.45
  330.8 26.4 %psum.7 = f32[6,512]{1,0:T(8,128)S(1)} all-reduce(f32[6,512]{1,0:T(8,128)S(1)} %select_maximum_fusion), channel_id=1, replica_groups=mesh['dp'=4,'edge'=8] {'edge'}, use_global_device_ids=true, to_apply=%region_0.0 | all-reduce | flops 3072 | bytes 24576 | tf_op jit(solution)/shard_map/psum | solution.py:1031
  359.2 1.6 fusion.6
  360.8 14.4 %shard_map.348 = (f32[512,2048]{1,0:T(8,128)}, f32[2048,512]{1,0:T(8,128)}) custom-call(bf16[1024,1024]{1,0:T(8,128)(2,1)} %all-gather.2.cloned.1.call-done.low.resid, bf16[1024,1024]{1,0:T(8,128)(2,1)} %all-gather.2.cloned.1.call-done.low.resid, bf16[512,2048]{1,0:T(8,128)(2,1)} %wf1.5, bf16[2048,512]{1,0:T(8,128)(2,1)} %wf2.5), custom_call_target="tpu_custom_call" | custom-call | tf_op jit(solution)/shard_map/pallas_call | solution.py:826
  (45 shorter events, 7.2 us)
Async XLA Ops:
  7.2 353.6 %all-gather.2.cloned.1.call-start = ((), (), s32[]{:S(2)}) async-start(), calls=%async_computation | async-start | bytes 2359296 | tf_op jit(solution)/shard_map/all_gather | solution.py:1027
  152.5 30.4 %copy-start.5 = (bf16[128,512]{1,0:T(8,128)(2,1)S(1)}, bf16[128,512]{1,0:T(8,128)(2,1)}, u32[]{:S(2)}) copy-start(bf16[128,512]{1,0:T(8,128)(2,1)} %get-tuple-element.78.low) | copy-start | bytes 393220
  152.5 34.2 %copy-start.11 = (f32[192,256]{1,0:T(8,128)S(1)}, f32[192,256]{1,0:T(8,128)}, u32[]{:S(2)}) copy-start(f32[192,256]{1,0:T(8,128)} %get-tuple-element.96) | copy-start | bytes 589828
  227.9 19.9 %copy-start.3 = (bf16[704,512]{1,0:T(8,128)(2,1)S(1)}, bf16[704,512]{1,0:T(8,128)(2,1)}, u32[]{:S(2)}) copy-start(bf16[704,512]{1,0:T(8,128)(2,1)} %get-tuple-element.90) | copy-start | bytes 2162692
  247.8 1.4 copy-start.6
  247.8 1.5 copy-start.2
  247.8 1.6 copy-start.7
  247.8 1.6 copy-start.8
  247.9 1.6 copy-start.9
  249.5 1.7 copy-start.1
  322.1 3.3 copy-start
  360.8 14.4 %copy-start.4 = (bf16[128,512]{1,0:T(8,128)(2,1)S(1)}, bf16[128,512]{1,0:T(8,128)(2,1)}, u32[]{:S(2)}) copy-start(bf16[128,512]{1,0:T(8,128)(2,1)} %get-tuple-element.152.node_low) | copy-start | bytes 393220
  360.8 15.1 %copy-start.10 = (f32[128,512]{1,0:T(8,128)S(1)}, f32[128,512]{1,0:T(8,128)}, u32[]{:S(2)}) copy-start(f32[128,512]{1,0:T(8,128)} %get-tuple-element.154) | copy-start | bytes 786436
Sparse Core Ops, SparseCore 0:
  184.6 31.8 all-gather.1

commit v2 on v1

--- a/solution.py
+++ b/solution.py
@@ -234,17 +234,17 @@
     handles = gather_start(place, nodes, nodes_all, send, recv)
     own = pltpu.make_async_copy(nodes, block(nodes_all, place.me, rows), own_sem.at[0])
     own.start()
-    spare = jnp.zeros((rows, LANES - K), I32)
-    own_wide = jnp.concatenate([owner[...], spare], axis=1)
-    slot_wide = jnp.concatenate([slot[...], spare], axis=1)
-    live_wide = jnp.concatenate([live[...], spare], axis=1).astype(F32)
+    spare = jnp.zeros((LANES - K, rows), I32)
+    own_wide = jnp.concatenate([owner[...], spare], axis=0)
+    slot_wide = jnp.concatenate([slot[...], spare], axis=0)
+    live_wide = jnp.concatenate([live[...], spare], axis=0).astype(F32)
     target = own_wide * rows + slot_wide
-    tcol[...] = target
-    lcol[...] = live_wide
-    scol[...] = slot_wide
-    trow[...] = jnp.transpose(target)
-    orow[...] = jnp.transpose(own_wide)
-    lrow[...] = jnp.transpose(live_wide)
+    trow[...] = target
+    orow[...] = own_wide
+    lrow[...] = live_wide
+    tcol[...] = jnp.transpose(target)
+    lcol[...] = jnp.transpose(live_wide)
+    scol[...] = jnp.transpose(slot_wide)
 
     def tally(g, total):
         ks = [g * GROUP + j for j in range(GROUP)]
@@ -281,7 +281,7 @@
 
 def start_call(n, nodes, owner, slot, live):
     rows, D = nodes.shape
-    K = slot.shape[1]
+    K = slot.shape[0]
     shape = jax.ShapeDtypeStruct
     return pl.pallas_call(
         functools.partial(start_kernel, n, K),
@@ -467,12 +467,12 @@
     node_low = (n2 * g2[...] + o2[...]).astype(BF)
     node_out[...] = node_low
     pad = jnp.zeros((rows, 256 - C), F32)
-    far = dot(node_low, we1[D : 2 * D, :])
+    far = dot_nt(node_low, we1[:, D : 2 * D])
     q_own[...] = jnp.concatenate([far, pad], axis=1).astype(BF)
     handles = gather_start(place, q_own, far_all, gsend, grecv)
     own = pltpu.make_async_copy(q_own, block(far_all, place.me, rows), own_sem.at[0])
     own.start()
-    near[...] = jnp.concatenate([dot(node_low, we1[:D, :]), pad], axis=1)
+    near[...] = jnp.concatenate([dot_nt(node_low, we1[:, :D]), pad], axis=1)
     own.wait()
     gather_finish(place, handles, q_own, far_all, gsend, grecv)
 
@@ -515,14 +515,14 @@
 ):
     g = pl.program_id(0)
     rows = near.shape[0]
-    D2 = we1.shape[0] - C
+    D2 = we1.shape[1] - C
     gap = 256 - C
 
     @pl.when(g == 0)
     def _():
         for ref in (w1o, w2p, w3o, w1t, w2t, w3t, gains, total, a1, a2, a3, ag, near_sum):
             ref[...] = jnp.zeros_like(ref)
-        own = we1[D2:, :]
+        own = jnp.transpose(we1[:, D2:].astype(F32)).astype(BF)
         w1o[0, :C, :C] = own
         w1o[1, gap:, :C] = own
         w2p[:C, :C] = we2[...]
@@ -660,7 +660,7 @@
 def node_back_kernel(
     n, C, far_sum, near_sum, cot, node_low, n1, n2, inv, act, slope, low, summed,
     w3, g1, wf1, wf2, g2, we1,
-    grad_one, vw_all, resid_out, dgain, dw3, dwe_near, dwe_far,
+    grad_one, vw_all, both, dgain, dw3, dwe_near, dwe_far,
     pair_buf, send_buf, far_buf, v_own, send, recv, gsend, grecv, own_sem,
 ):
     place = Place(n)
@@ -669,12 +669,13 @@
     far = scatter_sum(place, far_sum, pair_buf, send_buf, far_buf, send, recv)
     far = far.astype(BF)[:, :C]
     near = near_sum[...].astype(BF)[:, :C]
-    grad = cot[...].astype(F32) + dot_nt(near, we1[:D, :]) + dot_nt(far, we1[D : 2 * D, :])
+    grad = cot[...].astype(F32) + dot(near, we1[:, :D]) + dot(far, we1[:, D : 2 * D])
     two = norm_back(grad, n2[...], inv[1][:, 0:1], g2[...])
     dgain[16:24, :] = jnp.broadcast_to(jnp.sum(grad * n2[...], axis=0, keepdims=True), (8, D))
     dgain[24:32, :] = jnp.broadcast_to(jnp.sum(grad, axis=0, keepdims=True), (8, D))
     resid = two.astype(BF)
-    resid_out[...] = resid
+    both[:, :D] = low[...]
+    both[:, D:] = resid
     inner = (dot_nt(resid, wf2[...]) * slope[...].astype(F32)).astype(BF)
     grad = two + dot_nt(inner, wf1[...])
     one = norm_back(grad, n1[...], inv[0][:, 0:1], g1[...])
@@ -704,7 +705,7 @@
         out_shape=[
             shape((rows, D), F32),
             shape((n * rows, D), BF),
-            shape((rows, D), BF),
+            shape((rows, 2 * D), BF),
             shape((32, D), F32),
             shape((D, D), F32),
             shape((D, C), F32),
@@ -722,7 +723,7 @@
 
 
 def message_back_kernel(
-    tiles, C, tcol, trow, nodes, vw, w1, w2,
+    tiles, C, tcol, trow, nodes_all, nodes, vw, w1, w2,
     act1, slope1, slope2, edges, partial,
     grad_edges, dw1, dw2, target_sum, source_sum,
     w2t, w_own, w_own_t, total, a2, ae,
@@ -766,10 +767,17 @@
         target_sum[...] = total[...].astype(BF)
         dw2[...] = a2[...].astype(BF)
         dw1[:D, :] = dot_tn(nodes[...], source_sum[...].astype(BF)).astype(BF)
-        dw1[D:, :] = (ae[0][:C, :] + ae[1][gap:, :]).astype(BF)
-
-
-def message_back_call(C, tcol, trow, nodes, vw, w1, w2, act1, slope1, slope2, edges, partial):
+        dw1[2 * D :, :] = (ae[0][:C, :] + ae[1][gap:, :]).astype(BF)
+        a2[...] = jnp.zeros_like(a2)
+
+        def weigh(part):
+            a2[...] += dot_tn(nodes_all[part, :], total[part, :].astype(BF))
+
+        by_chunks(vw.shape[0], weigh)
+        dw1[D : 2 * D, :] = a2[...].astype(BF)
+
+
+def message_back_call(C, tcol, trow, nodes_all, nodes, vw, w1, w2, act1, slope1, slope2, edges, partial):
     rows, D = nodes.shape
     count = vw.shape[0]
     K = edges.shape[1] // C
@@ -784,12 +792,12 @@
     return pl.pallas_call(
         functools.partial(message_back_kernel, tiles, C),
         grid=(tiles,),
-        in_specs=[full(x) for x in (tcol, trow, nodes, vw, w1, w2)]
+        in_specs=[full(x) for x in (tcol, trow, nodes_all, nodes, vw, w1, w2)]
         + [tile, tile, tile, slab, slab],
-        out_specs=[slab, fixed(D + C, D), fixed(D, D), fixed(count, D), fixed(rows, D)],
+        out_specs=[slab, fixed(2 * D + C, D), fixed(D, D), fixed(count, D), fixed(rows, D)],
         out_shape=[
             shape((rows, K * C), F32),
-            shape((D + C, D), BF),
+            shape((2 * D + C, D), BF),
             shape((D, D), BF),
             shape((count, D), BF),
             shape((rows, D), F32),
@@ -803,7 +811,7 @@
             pltpu.VMEM((2, 256, D), F32),
         ],
         compiler_params=LOCAL,
-    )(tcol, trow, nodes, vw, w1, w2, act1, slope1, slope2, edges, partial)
+    )(tcol, trow, nodes_all, nodes, vw, w1, w2, act1, slope1, slope2, edges, partial)
 
 
 def feed_kernel(low, resid, wf1, wf2, dwf1, dwf2):
@@ -841,160 +849,288 @@
     )(both, both, wf1, wf2)
 
 
-def total_kernel(n, pieces, lag, x, out, pair_buf, low_buf, high_buf, send_buf, send, recv):
-    place = Place(n)
-    chips, c, q = place.chips, place.chip, place.core
-    root = chips // 2 - 1 + q
-    right = jnp.minimum(c + 1, chips - 1) * 2 + q
-    left = jnp.maximum(c - 1, 0) * 2 + q
-    half = x.shape[0] // 2
-    rows = half // pieces
-    barrier = pltpu.get_barrier_semaphore()
-
-    def hello(peer):
-        pl.semaphore_signal(barrier, inc=1, device_id={"edge": peer}, device_id_type=MESH)
-
-    hello(place.sibling)
-    pl.when(c > 0)(lambda: hello(left))
-    pl.when(c < chips - 1)(lambda: hello(right))
-    inner = jnp.where((c > 0) & (c < chips - 1), 1, 0)
-    pl.semaphore_wait(barrier, 2 + inner)
-
-    def part(which, p):
-        return pl.ds(pl.multiple_of(which * half + p * rows, rows), rows)
-
-    def local(p):
-        return pl.ds(p * rows, rows)
-
-    def link(src, dst, p, sent, got, peer):
-        return remote(src, dst, send.at[sent * pieces + p], recv.at[got * pieces + p], peer)
-
-    def pair(p):
-        return link(x.at[part(1 - q, p)], pair_buf.at[local(p)], p, 0, 0, place.sibling)
-
-    def up(p):
-        return link(send_buf.at[local(p)], low_buf.at[local(p)], p, 1, 1, right)
-
-    def down(p):
-        return link(send_buf.at[local(p)], high_buf.at[local(p)], p, 2, 2, left)
-
-    def out_left(p):
-        return link(out.at[part(q, p)], out.at[part(q, p)], p, 3, 3, left)
-
-    def out_right(p):
-        return link(out.at[part(q, p)], out.at[part(q, p)], p, 5, 3, right)
-
-    def across(p):
-        return link(out.at[part(q, p)], out.at[part(q, p)], p, 4, 4, place.sibling)
-
-    for p in range(pieces):
-        pair(p).start()
-
-    def reduce(p):
-        pair(p).wait_recv()
-        here = local(p)
-        mine = lambda: x[part(q, p), :].astype(F32) + pair_buf[here, :].astype(F32)
-
-        def from_left():
-            def first():
-                send_buf[here, :] = mine().astype(BF)
-
-            def inner():
-                up(p).wait_recv()
-                send_buf[here, :] = (mine() + low_buf[here, :].astype(F32)).astype(BF)
-
-            pl.when(c == 0)(first)
-            pl.when(c > 0)(inner)
-            up(p).start()
-
-        def from_right():
-            def first():
-                send_buf[here, :] = mine().astype(BF)
-
-            def inner():
-                down(p).wait_recv()
-                send_buf[here, :] = (mine() + high_buf[here, :].astype(F32)).astype(BF)
-
-            pl.when(c == chips - 1)(first)
-            pl.when(c < chips - 1)(inner)
-            down(p).start()
+class Line:
+    def __init__(self, place, pieces, x, out, pair_buf, low_buf, high_buf, send_buf, send, recv):
+        self.place, self.pieces, self.x, self.out = place, pieces, x, out
+        self.pair_buf, self.low_buf, self.high_buf = pair_buf, low_buf, high_buf
+        self.send_buf, self.send, self.recv = send_buf, send, recv
+        c, q, chips = place.chip, place.core, place.chips
+        self.root = chips // 2 - 1 + q
+        self.away = jnp.abs(c - self.root)
+        self.right = jnp.minimum(c + 1, chips - 1) * 2 + q
+        self.left = jnp.maximum(c - 1, 0) * 2 + q
+        self.half = x.shape[0] // 2
+        self.rows = self.half // pieces
+
+    def part(self, which, p):
+        return pl.ds(pl.multiple_of(which * self.half + p * self.rows, self.rows), self.rows)
+
+    def here(self, p):
+        return pl.ds(pl.multiple_of(p * self.rows, self.rows), self.rows)
+
+    def link(self, src, dst, p, sent, got, peer):
+        n = self.pieces
+        return remote(src, dst, self.send.at[sent * n + p], self.recv.at[got * n + p], peer)
+
+    def pair(self, p):
+        src = self.x.at[self.part(1 - self.place.core, p)]
+        return self.link(src, self.pair_buf.at[self.here(p)], p, 0, 0, self.place.sibling)
+
+    def up(self, p):
+        here = self.here(p)
+        return self.link(self.send_buf.at[here], self.low_buf.at[here], p, 1, 1, self.right)
+
+    def down(self, p):
+        here = self.here(p)
+        return self.link(self.send_buf.at[here], self.high_buf.at[here], p, 2, 2, self.left)
+
+    def outward(self, p, sent, got, peer):
+        mine = self.out.at[self.part(self.place.core, p)]
+        return self.link(mine, mine, p, sent, got, peer)
+
+    def out_left(self, p):
+        return self.outward(p, 3, 3, self.left)
+
+    def out_right(self, p):
+        return self.outward(p, 5, 3, self.right)
+
+    def across(self, p):
+        return self.outward(p, 4, 4, self.place.sibling)
+
+    def each(self, step):
+        lax.fori_loop(0, self.pieces, lambda p, z: (step(p), z)[1], 0)
+
+    def start(self):
+        self.each(lambda p: self.pair(p).start())
+
+    def reduce(self, p):
+        c, root, last = self.place.chip, self.root, self.place.chips - 1
+        here, mine_at = self.here(p), self.part(self.place.core, p)
+        self.pair(p).wait_recv()
+        mine = lambda: self.x[mine_at, :].astype(F32) + self.pair_buf[here, :].astype(F32)
+
+        def end():
+            self.send_buf[here, :] = mine().astype(BF)
+
+        def from_low():
+            self.up(p).wait_recv()
+            self.send_buf[here, :] = (mine() + self.low_buf[here, :].astype(F32)).astype(BF)
+
+        def from_high():
+            self.down(p).wait_recv()
+            self.send_buf[here, :] = (mine() + self.high_buf[here, :].astype(F32)).astype(BF)
 
         def at_root():
-            up(p).wait_recv()
-            down(p).wait_recv()
-            total = mine() + low_buf[here, :].astype(F32) + high_buf[here, :].astype(F32)
-            out[part(q, p), :] = total.astype(BF)
-            out_left(p).start()
-            out_right(p).start()
-            across(p).start()
-
-        pl.when(c < root)(from_left)
-        pl.when(c > root)(from_right)
+            self.up(p).wait_recv()
+            self.down(p).wait_recv()
+            total = mine() + self.low_buf[here, :].astype(F32) + self.high_buf[here, :].astype(F32)
+            self.out[mine_at, :] = total.astype(BF)
+            self.out_left(p).start()
+            self.out_right(p).start()
+            self.across(p).start()
+
+        pl.when((c == 0) | (c == last))(end)
+        pl.when((c > 0) & (c < root))(from_low)
+        pl.when((c > root) & (c < last))(from_high)
+        pl.when(c < root)(lambda: self.up(p).start())
+        pl.when(c > root)(lambda: self.down(p).start())
         pl.when(c == root)(at_root)
 
-    def spread_out(p):
+    def spread(self, p):
+        c, root, last = self.place.chip, self.root, self.place.chips - 1
+
         def leftward():
-            out_left(p).wait_recv()
-            pl.when(c > 0)(lambda: out_left(p).start())
-            across(p).start()
+            self.out_left(p).wait_recv()
+            pl.when(c > 0)(lambda: self.out_left(p).start())
+            self.across(p).start()
 
         def rightward():
-            out_right(p).wait_recv()
-            pl.when(c < chips - 1)(lambda: out_right(p).start())
-            across(p).start()
+            self.out_right(p).wait_recv()
+            pl.when(c < last)(lambda: self.out_right(p).start())
+            self.across(p).start()
 
         pl.when(c < root)(leftward)
         pl.when(c > root)(rightward)
 
-    for s in range(pieces + lag):
-        if s < pieces:
-            reduce(s)
-        if s >= lag:
-            spread_out(s - lag)
-    for p in range(pieces):
-        across(p).wait_recv()
-    for p in range(pieces):
-        pair(p).wait_send()
-        across(p).wait_send()
-        pl.when(c < root)(lambda: up(p).wait_send())
-        pl.when(c > root)(lambda: down(p).wait_send())
-        pl.when((c <= root) & (c > 0))(lambda: out_left(p).wait_send())
-        pl.when((c >= root) & (c < chips - 1))(lambda: out_right(p).wait_send())
-
-
-def total_call(n, x, pieces, lag):
-    rows, width = x.shape
-    return pl.pallas_call(
-        functools.partial(total_kernel, n, pieces, lag),
-        in_specs=[WHOLE],
-        out_specs=WHOLE,
-        out_shape=jax.ShapeDtypeStruct(x.shape, x.dtype),
-        scratch_shapes=[pltpu.VMEM((rows // 2, width), BF)] * 4 + sems(6 * pieces),
-        compiler_params=remote_params(3),
-    )(x)
-
-
-def final_kernel(n, target_sum, source_sum, grad_one, w1, nodes, out, dw1, pair_buf, send_buf, far_buf, send, recv):
+    def slots(self, lag):
+        return self.pieces + lag * (self.place.chips // 2)
+
+    def slot(self, s, lag):
+        pl.when(s < self.pieces)(lambda: self.reduce(s))
+        p = s - lag * self.away
+        pl.when((p >= 0) & (p < self.pieces) & (self.away > 0))(lambda: self.spread(p))
+
+    def finish(self):
+        c, root, last = self.place.chip, self.root, self.place.chips - 1
+
+        def end(p):
+            self.pair(p).wait_send()
+            self.across(p).wait_send()
+            pl.when(c < root)(lambda: self.up(p).wait_send())
+            pl.when(c > root)(lambda: self.down(p).wait_send())
+            pl.when((c <= root) & (c > 0))(lambda: self.out_left(p).wait_send())
+            pl.when((c >= root) & (c < last))(lambda: self.out_right(p).wait_send())
+
+        self.each(lambda p: self.across(p).wait_recv())
+        self.each(end)
+
+
+def line_scratch(rows, width, pieces):
+    return [pltpu.VMEM((rows // 2, width), BF)] * 4 + sems(6 * pieces)
+
+
+PIECES = 19
+LAG = 4
+
+
+def final_kernel(
+    n, C, feed, target_sum, source_sum, grad_one, w1, dw1, dw2, dw3, dwe_near, dwe_far, dwe1, dwe2,
+    dwe3, dgain, dg3, *rest,
+):
+    if feed:
+        both, wf1, wf2, grad_nodes, out, small, dwf1, dwf2, *rest = rest
+    else:
+        grad_nodes, out, small, *rest = rest
+    x, gains, others_gains, pair_buf, send_buf, far_buf, send, recv, gsend, grecv, *line_refs = rest
     place = Place(n)
-    D = grad_one.shape[1]
-    greet([place.sibling] + place.mates)
+    rows, D = grad_one.shape
+    others = [lax.rem(place.me + d, n) for d in range(1, n)]
+    greet(others)
+    at = 2 * D + C
+    x[:at, :] = dw1[...]
+    x[at : at + D, :] = dw2[...]
+    x[at + D : at + 2 * D, :] = dw3[...].astype(BF)
+    at += 2 * D
+    spare = jnp.zeros((D, 256 - C), F32)
+    edge1 = jnp.concatenate(
+        [
+            jnp.concatenate([dwe_near[...], spare], axis=1),
+            jnp.concatenate([dwe_far[...], spare], axis=1),
+            dwe1[...],
+        ],
+        axis=0,
+    ).astype(BF)
+    half = edge1.shape[0] // 2
+    x[at : at + half, :256] = edge1[:half]
+    x[at : at + half, 256:] = edge1[half:]
+    at += half
+    x[at : at + C, :256] = dwe2[:C, :].astype(BF)
+    x[at : at + C, 256:] = dwe3[:C, :].astype(BF)
+    line = Line(place, PIECES, x, out, *line_refs)
+    line.start()
+    gains[...] = jnp.zeros_like(gains)
+    for r in range(4):
+        gains[r : r + 1, :] = dgain[8 * r : 8 * r + 1, :]
+    for r in range(2):
+        gains[4 + r : 5 + r, :256] = dg3[8 * r : 8 * r + 1, :]
+    copies = []
+    for d in range(1, n):
+        copy = remote(gains, others_gains.at[place.me], gsend.at[d], grecv.at[d], others[d - 1])
+        copy.start()
+        copies.append(copy)
+    others_gains[place.me] = gains[...]
+
+    def feed_part(f):
+        step = 256
+        cols = pl.ds(pl.multiple_of(f * step, step), step)
+        low, resid = both[:, :D], both[:, D:]
+        act, slope = gelu_pair(dot(low, wf1[:, cols]))
+        dwf2[cols, :] = dot_tn(act.astype(BF), resid).astype(BF)
+        inner = (dot_nt(resid, wf2[cols, :]) * slope).astype(BF)
+        dwf1[:, cols] = dot_tn(low, inner).astype(BF)
+
+    parts = wf1.shape[1] // 256 if feed else 0
+
+    def slot(s, carry):
+        line.slot(s, LAG)
+        if feed:
+            pl.when((s % 2 == 1) & (s // 2 < parts))(lambda: feed_part(s // 2))
+        return carry
+
+    lax.fori_loop(0, line.slots(LAG), slot, 0)
     total = scatter_sum(place, target_sum, pair_buf, send_buf, far_buf, send, recv)
     source = dot_nt(source_sum[...].astype(BF), w1[:D, :])
-    total = total.astype(BF)
-    out[...] = grad_one[...] + source + dot_nt(total, w1[D : 2 * D, :])
-    dw1[...] = dot_tn(nodes[...], total).astype(BF)
-
-
-def final_call(n, target_sum, source_sum, grad_one, w1, nodes):
-    rows, D = grad_one.shape
+    grad_nodes[...] = grad_one[...] + source + dot_nt(total.astype(BF), w1[D : 2 * D, :])
+    for copy in copies:
+        copy.wait_recv()
+    total = others_gains[0]
+    for e in range(1, n):
+        total = total + others_gains[e]
+    small[...] = total
+    line.finish()
+    for copy in copies:
+        copy.wait_send()
+
+
+def final_call(n, C, feed, args, both, wf1, wf2):
+    rows, D = args[2].shape
+    FF = wf1.shape[1]
+    size = 4 * D + C + (2 * D + C) // 2 + C
+    shape = jax.ShapeDtypeStruct
+    outs = [shape((rows, D), F32), shape((size, D), BF), shape((8, D), F32)]
+    if feed:
+        args = [*args, both, wf1, wf2]
+        outs += [shape((D, FF), BF), shape((FF, D), BF)]
     return pl.pallas_call(
-        functools.partial(final_kernel, n),
-        in_specs=[WHOLE] * 5,
-        out_specs=[WHOLE] * 2,
-        out_shape=[jax.ShapeDtypeStruct((rows, D), F32), jax.ShapeDtypeStruct((D, D), BF)],
-        scratch_shapes=[*comm_scratch(n, rows, D), *sems(n)],
-        compiler_params=remote_params(4),
-    )(target_sum, source_sum, grad_one, w1, nodes)
+        functools.partial(final_kernel, n, C, feed),
+        in_specs=[WHOLE] * len(args),
+        out_specs=[WHOLE] * len(outs),
+        out_shape=outs,
+        scratch_shapes=[
+            pltpu.VMEM((size, D), BF),
+            pltpu.VMEM((8, D), F32),
+            pltpu.VMEM((n, 8, D), F32),
+            *comm_scratch(n, rows, D),
+            *sems(n),
+            *sems(n),
+            *line_scratch(size, D, PIECES),
+        ],
+        compiler_params=remote_params(3),
+    )(*args)
+
+
+def unpack_kernel(C, steps, sizes, packed, *refs):
+    g = pl.program_id(0)
+    count = len(sizes)
+    plain = refs[: (len(refs) - 3 - count) // 2]
+    outs = refs[len(plain) :]
+    at = 0
+    for size, b in zip(sizes, outs):
+        step = size // steps
+        b[...] = packed[pl.ds(pl.multiple_of(at + g * step, 16), step), :].astype(F32)
+        at += size
+    for a, b in zip(plain, outs[count:]):
+        b[...] = a[...].astype(F32)
+    one, two, three = outs[-3:]
+
+    @pl.when(g == steps - 1)
+    def _():
+        half = packed.shape[0] - at - C
+        for r in range(2):
+            left = 256 * r
+            flipped = jnp.transpose(packed[at : at + half, left : left + 256].astype(F32))
+            one[:, half * r : half * r + half] = flipped[:C, :]
+        two[...] = packed[at + half :, :C].astype(F32)
+        three[...] = packed[at + half :, 256 : 256 + C].astype(F32)
+
+
+def unpack_call(C, sizes, packed, arrays):
+    steps = 4
+    D = packed.shape[1]
+    shape = jax.ShapeDtypeStruct
+    cut = lambda r, c: pl.BlockSpec((r // steps, c), lambda g: (g, 0))
+    fixed = lambda *s: pl.BlockSpec(s, lambda g: (0,) * len(s))
+    half = packed.shape[0] - sum(sizes) - C
+    last = [(C, 2 * half), (C, C), (C, C)]
+    first = [(size, D) for size in sizes] + [v.shape for v in arrays]
+    return pl.pallas_call(
+        functools.partial(unpack_kernel, C, steps, sizes),
+        grid=(steps,),
+        in_specs=[full(packed)] + [cut(*v.shape) for v in arrays],
+        out_specs=[cut(*v) for v in first] + [fixed(*s) for s in last],
+        out_shape=[shape(v, F32) for v in first + last],
+        compiler_params=LOCAL,
+    )(packed, *arrays)
 
 
 def body(
@@ -1005,53 +1141,45 @@
     n = lax.axis_size("edge")
     rows, D = nodes.shape
     C = w_edge2.shape[0]
-    K = nbr_slot.shape[1]
+    we1 = w_edge1.T
     g1, o1, g2, o2 = (v.reshape(1, D) for v in (gain_one, offset_one, gain_two, offset_two))
     nodes_all, tcol, lcol, trow, count = start_call(
-        n, nodes, nbr_owner.reshape(rows, K), nbr_slot, edge_mask
+        n, nodes, nbr_owner[:, :, 0].T, nbr_slot.T, edge_mask.T
     )
     act1, slope1, slope2, summed = message_call(
         C, tcol, lcol, trow, nodes_all, nodes, w_msg1, w_msg2, edges
     )
     node_out, far_all, near, low, n1, n2, inv, act, slope, own_sum = node_call(
-        n, C, summed, count, nodes, w_msg3, g1, o1, w_ffn1, w_ffn2, g2, o2, w_edge1
+        n, C, summed, count, nodes, w_msg3, g1, o1, w_ffn1, w_ffn2, g2, o2, we1
     )
     edge_out, partial, far_sum, near_sum, dwe1, dwe2, dwe3, dg3 = edge_call(
-        C, tcol, trow, far_all, near, w_edge1, w_edge2, w_edge3,
+        C, tcol, trow, far_all, near, we1, w_edge2, w_edge3,
         gain_three.reshape(1, C), offset_three.reshape(1, C), edges, edge_cotangent,
     )
-    grad_one, vw_all, resid, dgain, dw3, dwe_near, dwe_far = node_back_call(
+    grad_one, vw_all, both, dgain, dw3, dwe_near, dwe_far = node_back_call(
         n, C, far_sum, near_sum, node_cotangent, node_out, n1, n2, inv, act, slope, low, own_sum,
-        w_msg3, g1, w_ffn1, w_ffn2, g2, w_edge1,
-    )
-    both = lax.all_gather(jnp.concatenate([low, resid], axis=1), "edge", axis=0, tiled=True)
-    small = jnp.concatenate(
-        [dgain[0::8], jnp.concatenate([dg3[0::8], jnp.zeros((2, D - 256), F32)], axis=1)], axis=0
-    )
-    small = lax.psum(small, "edge")
+        w_msg3, g1, w_ffn1, w_ffn2, g2, we1,
+    )
+    both = lax.all_gather(both, "edge", axis=0, tiled=True)
     grad_edges, dw1, dw2, target_sum, source_sum = message_back_call(
-        C, tcol, trow, nodes, vw_all, w_msg1, w_msg2, act1, slope1, slope2, edges, partial,
-    )
-    dwf1, dwf2 = feed_call(both, w_ffn1, w_ffn2)
-    grad_nodes, dw1t = final_call(n, target_sum, source_sum, grad_one, w_msg1, nodes)
-    wide = lambda v: jnp.pad(v, ((0, 0), (0, 256 - v.shape[1])))
-    edge1 = jnp.concatenate([wide(dwe_near), wide(dwe_far), dwe1], axis=0).astype(BF)
-    split = edge1.shape[0] // 2
-    edge1 = jnp.concatenate([edge1[:split], edge1[split:]], axis=1)
-    edge23 = jnp.concatenate([dwe2[:C], dwe3[:C]], axis=1).astype(BF)
-    packed = jnp.concatenate([dw1[:D], dw1t, dw1[D:], dw2, dw3.astype(BF), edge1, edge23], axis=0)
-    packed = total_call(n, packed, 5, 4).astype(F32)
-    at = 0
-    pieces = []
-    for size in (2 * D + C, D, D, split, C):
-        pieces.append(packed[at : at + size])
-        at += size
-    tot1, tot2, tot3, tot_e1, tot_e23 = pieces
-    grad_we1 = jnp.concatenate([tot_e1[:, :C], tot_e1[:, 256 : 256 + C]], axis=0)
+        C, tcol, trow, nodes_all, nodes, vw_all, w_msg1, w_msg2, act1, slope1, slope2, edges, partial,
+    )
+    feed = both.shape[0] <= TABLE
+    grad_nodes, packed, small, *dwf = final_call(
+        n, C, feed,
+        [target_sum, source_sum, grad_one, w_msg1, dw1, dw2, dw3, dwe_near, dwe_far, dwe1, dwe2, dwe3, dgain, dg3],
+        both, w_ffn1, w_ffn2,
+    )
+    if not feed:
+        dwf = feed_call(both, w_ffn1, w_ffn2)
+    tot1, tot2, tot3, *dwf_out, we1_t, tot_e2, tot_e3 = unpack_call(
+        C, [2 * D + C, D, D], packed, dwf if feed else []
+    )
+    dwf1, dwf2 = dwf_out if feed else dwf
     return (
         node_out, edge_out, grad_nodes, grad_edges,
         tot1, tot2, tot3, small[0], small[1], dwf1, dwf2, small[2], small[3],
-        grad_we1, tot_e23[:, :C], tot_e23[:, 256 : 256 + C], small[4, :C], small[5, :C],
+        we1_t.T, tot_e2, tot_e3, small[4, :C], small[5, :C],
     )
 
 

time: 384 us -> 312 us (0.81)
  blocking collectives: 26.4 us -> 0 us
  Pallas kernels: 312 us -> 291 us
  local copies, waits for them, and re-layouts: 25.2 us -> 5.52 us
  other arithmetic: 5.71 us -> 0 us
    psum x1 -> x0, blocking collectives: 26.4 us -> none  [body(): small = lax.psum(small, 'edge')]
    pallas_call x3 -> x2, Pallas kernels: 105 us -> 83.7 us  [the longest x1 74.8 us: final_call(): pl.pallas_call(functools.partial(final_kernel, n, C, feed), in_specs=[WHO...]
    unnamed x35 -> x7, local copies, waits for them, and re-layouts: 13.6 us -> 2.72 us
    slice x8 -> x0, local copies, waits for them, and re-layouts: 10.4 us -> none  [the longest x2 4.85 us: body(): pieces.append(packed[at:at + size])]
  transfers between devices with their start and end apart: 1 -> 1, of which waited for: 0 -> 0; matrix products, arithmetic and copies ran while one was open for 5% -> 0% of each run, Pallas kernels for 33% -> 12%
where the time goes in v2:
time: 312 us; the launch traced here: 311 us
  Pallas kernels  291 us (93%)
  between operations  14.1 us (5%)
  local copies, waits for them, and re-layouts  5.52 us (2%)
    pallas_call x1, Pallas kernels, final_call(): pl.pallas_call(functools.partial(final_kernel, n, C, feed), in_specs=[WHO...  74.8 us
    pallas_call x1, Pallas kernels, edge_call(): pl.pallas_call(functools.partial(edge_kernel, tiles, C), grid=(tiles,), i...  43.8 us
    pallas_call x1, Pallas kernels, message_call(): pl.pallas_call(functools.partial(message_kernel, tiles, C), grid=(tiles +...  43.1 us
    pallas_call x1, Pallas kernels, message_back_call(): pl.pallas_call(functools.partial(message_back_kernel, tiles, C), grid=(ti...  38.5 us
    pallas_call x1, Pallas kernels, node_back_call(): pl.pallas_call(functools.partial(node_back_kernel, n, C), in_specs=[WHOLE...  30.4 us
    pallas_call x1, Pallas kernels, node_call(): pl.pallas_call(functools.partial(node_kernel, n, C), in_specs=[WHOLE] * 1...  29.7 us
    pallas_call x1, Pallas kernels, start_call(): pl.pallas_call(functools.partial(start_kernel, n, K), in_specs=[WHOLE] *...  21.9 us
    pallas_call x1, Pallas kernels, unpack_call(): pl.pallas_call(functools.partial(unpack_kernel, C, steps, sizes), grid=(s...  8.91 us
  transfers between devices with their start and end apart: 1, of which 0 were waited for; matrix products, arithmetic and copies ran while one was open for 0% of the time, Pallas kernels for 12%

profile of v2, /device:TPU:0, one launch (start us, length us, event | category | flops | bytes accessed | tf_op | source)
XLA Modules:
  0.0 310.9 jit_solution(16942943862944571537)
XLA Ops:
  7.2 0.0 all-gather.2.cloned.1.call-start
  7.2 1.4 copy.41
  8.6 21.9 %shard_map.340 = (bf16[1024,512]{1,0:T(8,128)(2,1)}, s32[128,128]{1,0:T(8,128)}, f32[128,128]{1,0:T(8,128)}, s32[128,128]{1,0:T(8,128)}, f32[8,128]{1,0:T(8,128)}) custom-call(bf16[128,512]{1,0:T(8,128)(2,1)} %nodes.7, s32[52,128]{1,0:T(8,128)} %bitcast.24, s32[52,128]{1,0:T(8,128)} %bitcast.25, s32[52,128]{1,0:T(8,128)} %bitcast.26), custom_call_target="tpu_custom_call" | custom-call | tf_op jit(solution)/shard_map/pallas_call | solution.py:286
  30.5 43.1 %shard_map.341 = (bf16[6656,512]{1,0:T(8,128)(2,1)}, bf16[6656,512]{1,0:T(8,128)(2,1)}, bf16[6656,512]{1,0:T(8,128)(2,1)}, bf16[1024,512]{1,0:T(8,128)(2,1)}) custom-call(s32[128,128]{1,0:T(8,128)} %get-tuple-element.70.tcol, f32[128,128]{1,0:T(8,128)} %get-tuple-element.71.lcol, s32[128,128]{1,0:T(8,128)} %get-tuple-element.72.trow, ...), custom_call_target="tpu_custom_call" | custom-call | tf_op jit(solution)/shard_map/pallas_call | solution.py:408
  73.6 29.7 %shard_map.342 = (bf16[128,512]{1,0:T(8,128)(2,1)}, bf16[1024,256]{1,0:T(8,128)(2,1)}, f32[128,256]{1,0:T(8,128)}, bf16[128,512]{1,0:T(8,128)(2,1)}, f32[128,512...) custom-call(bf16[1024,512]{1,0:T(8,128)(2,1)} %get-tuple-element.74., ...), custom_call_target="tpu_custom_call" | custom-call | tf_op jit(solution)/shard_map/pallas_call | solution.py:484
  103.3 43.8 %shard_map.343 = (bf16[128,9984]{1,0:T(8,128)(2,1)}, f32[128,9984]{1,0:T(8,128)}, bf16[1024,256]{1,0:T(8,128)(2,1)}, f32[128,256]{1,0:T(8,128)}, f32[192,256]{1,...) custom-call(s32[128,128]{1,0:T(8,128)} %get-tuple-element.70.tcol, ...), custom_call_target="tpu_custom_call" | custom-call | tf_op jit(solution)/shard_map/pallas_call | solution.py:618
  147.1 30.4 %shard_map.344 = (f32[128,512]{1,0:T(8,128)}, bf16[1024,512]{1,0:T(8,128)(2,1)}, bf16[128,1024]{1,0:T(8,128)(2,1)}, f32[32,512]{1,0:T(8,128)}, f32[512,512]{1,0:...) custom-call(bf16[1024,256]{1,0:T(8,128)(2,1)} %get-tuple-element.80.far_sum, f32[128,256]{1,0:T(8,128)} %get-tuple-element.81.near_sum, ...), custom_call_target="tpu_custom_call" | custom-call | tf_op jit(solution)/shard_map/pallas_call | solution.py:701
  177.5 0.0 all-gather.2.cloned.1.call-update
  177.5 38.5 %shard_map.345 = (f32[128,9984]{1,0:T(8,128)}, bf16[1216,512]{1,0:T(8,128)(2,1)}, bf16[512,512]{1,0:T(8,128)(2,1)}, bf16[1024,512]{1,0:T(8,128)(2,1)}, f32[128,512]{1,0:T(8,128)}) custom-call(s32[128,128]{1,0:T(8,128)} %get-tuple-element.70.tcol, s32[128,128]{1,0:T(8,128)} %get-tuple-element.72.trow, bf16[1024,512]{1,0:T(8,128)(2,1)} %get-tuple-element.73.nodes_all, ...), custom_call_target="tpu_custom_call" | custom-call | tf_op jit(solution)/shard_map/pallas_call | solution.py:792
  216.1 0.0 all-gather.2.cloned.1.call-done.rest_0_
  216.1 74.8 %shard_map.346 = (f32[128,512]{1,0:T(8,128)}, bf16[3040,512]{1,0:T(8,128)(2,1)}, f32[8,512]{1,0:T(8,128)}, bf16[512,2048]{1,0:T(8,128)(2,1)}, bf16[2048,512]{1,0:T(8,128)(2,1)}) custom-call(bf16[1024,512]{1,0:T(8,128)(2,1)} %get-tuple-element.94.target_sum, f32[128,512]{1,0:T(8,128)} %get-tuple-element.95.source_sum, f32[128,512]{1,0:T(8,128)} %get-tuple-element.96.grad_one, ...), custom_call_target="tpu_custom_call" | custom-call | tf_op jit(solution)/shard_map/pallas_call | solution.py:1074
  290.9 1.3 fusion
  292.3 1.5 fusion.1
  293.7 0.0 copy-start
  293.7 0.0 copy-start.1
  293.7 8.9 %shard_map.347 = (f32[1216,512]{1,0:T(8,128)}, f32[512,512]{1,0:T(8,128)}, f32[512,512]{1,0:T(8,128)}, f32[512,2048]{1,0:T(8,128)}, f32[2048,512]{1,0:T(8,128)},...) custom-call(bf16[3040,512]{1,0:T(8,128)(2,1)} %get-tuple-element.110.packed, ...), custom_call_target="tpu_custom_call" | custom-call | tf_op jit(solution)/shard_map/pallas_call | solution.py:1126
  302.7 0.0 copy-done
  302.7 0.7 copy.44
  303.3 0.0 copy-done.1
  303.3 0.7 copy.45
Async XLA Ops:
  7.2 208.9 %all-gather.2.cloned.1.call-start = ((), (), s32[]{:S(2)}) async-start(), calls=%async_computation | async-start | bytes 2359296 | tf_op jit(solution)/shard_map/all_gather | solution.py:1163
  293.7 8.9 %copy-start = (bf16[128,512]{1,0:T(8,128)(2,1)S(1)}, bf16[128,512]{1,0:T(8,128)(2,1)}, u32[]{:S(2)}) copy-start(bf16[128,512]{1,0:T(8,128)(2,1)} %get-tuple-element.146.node_low) | copy-start | bytes 393220
  293.7 9.6 %copy-start.1 = (f32[128,512]{1,0:T(8,128)S(1)}, f32[128,512]{1,0:T(8,128)}, u32[]{:S(2)}) copy-start(f32[128,512]{1,0:T(8,128)} %get-tuple-element.148) | copy-start | bytes 786436
Sparse Core Ops, SparseCore 0:
  177.7 31.8 all-gather.1

commit v3 on v2

v3 whole, which is shorter than its diff:
```python
import functools

import jax
import jax.numpy as jnp
from jax import lax
from jax.experimental import pallas as pl
from jax.experimental.pallas import tpu as pltpu
from jax.sharding import PartitionSpec as P

BF = jnp.bfloat16
F32 = jnp.float32
I32 = jnp.int32
MESH = pl.DeviceIdType.MESH
MIB = 1024 * 1024
LANES = 128
GROUP = 4
ORDER = (0, 2, 1, 3)
TABLE = 1024
EPS = 1e-05
ROOT = 0.7978845608028654
CUBE = 0.044715 * ROOT


def dot(a, b):
    return jnp.dot(a, b, preferred_element_type=F32)


def dot_tn(a, b):
    return lax.dot_general(a, b, (((0,), (0,)), ((), ())), preferred_element_type=F32)


def dot_nt(a, b):
    return lax.dot_general(a, b, (((1,), (1,)), ((), ())), preferred_element_type=F32)


def gelu_pair(v):
    v = v.astype(BF)
    c = lambda x: jnp.asarray(x, BF)
    z = v * v
    q = c(0.5) + c(0.5) * jnp.tanh(v * (c(ROOT) + c(CUBE) * z))
    act = v * q
    slope = q + (act - act * q) * (c(2.0 * ROOT) + c(6.0 * CUBE) * z)
    return act, slope


def gelu_full(v):
    z = v * v
    q = 0.5 + 0.5 * jnp.tanh(v * (ROOT + CUBE * z))
    act = v * q
    slope = q + (act - act * q) * (2.0 * ROOT + 6.0 * CUBE * z)
    return act.astype(BF), slope.astype(BF)


def row_mean(v):
    return jnp.mean(v, axis=-1, keepdims=True)


def lane_column(ref, k):
    rows = ref.shape[0]
    return jnp.broadcast_to(pltpu.roll(ref[...], LANES - k, axis=1)[:, 0:1], (rows, LANES))


def pick_rows(target, width):
    lane = lax.broadcasted_iota(I32, target.shape, 1)
    one, nil = jnp.ones((), BF), jnp.zeros((), BF)
    t16, l16 = target.astype(jnp.int16), lane.astype(jnp.int16)
    return jnp.concatenate(
        [jnp.where(t16 == l16 + jnp.int16(LANES * c), one, nil) for c in range(width // LANES)], axis=1)


def pick_cols(target, width):
    edges = target.shape[1]
    sub = lax.broadcasted_iota(I32, (width, edges), 0)
    return jnp.where(jnp.broadcast_to(target, (width, edges)).astype(jnp.int16) == sub.astype(jnp.int16), jnp.ones((), BF), jnp.zeros((), BF))


def gather_table(targets, table):
    count = table.shape[0]
    if count <= TABLE:
        hot = jnp.concatenate([pick_rows(t, count) for t in targets], axis=0)
        return dot(hot, table[...])

    def step(c, total):
        base = c * TABLE
        hot = jnp.concatenate([pick_rows(t - base, TABLE) for t in targets], axis=0)
        return total + dot(hot, table[pl.ds(pl.multiple_of(base, TABLE), TABLE), :])

    rows = sum(t.shape[0] for t in targets)
    return lax.fori_loop(0, count // TABLE, step, jnp.zeros((rows, table.shape[1]), F32))


def add_by_target(target, values, total):
    count = total.shape[0]
    if count <= TABLE:
        total[...] += dot(pick_cols(target, count), values)
        return

    def step(c, carry):
        base = c * TABLE
        part = pl.ds(pl.multiple_of(base, TABLE), TABLE)
        total[part, :] += dot(pick_cols(target - base, TABLE), values)
        return carry

    lax.fori_loop(0, count // TABLE, step, 0)


def by_chunks(count, step):
    if count <= TABLE:
        step(pl.ds(0, count))
        return

    def one(c, carry):
        step(pl.ds(pl.multiple_of(c * TABLE, TABLE), TABLE))
        return carry

    lax.fori_loop(0, count // TABLE, one, 0)


def remote(src, dst, send, recv, peer):
    return pltpu.make_async_remote_copy(
        src_ref=src,
        dst_ref=dst,
        send_sem=send,
        recv_sem=recv,
        device_id={"edge": peer},
        device_id_type=MESH,
    )


def greet(peers):
    barrier = pltpu.get_barrier_semaphore()
    for peer in peers:
        pl.semaphore_signal(barrier, inc=1, device_id={"edge": peer}, device_id_type=MESH)
    pl.semaphore_wait(barrier, len(peers))


def block(ref, index, rows):
    return ref.at[pl.ds(pl.multiple_of(index * rows, rows), rows)]


class Place:
    def __init__(self, n):
        self.me = lax.axis_index("edge")
        self.chips = n // 2
        self.chip = self.me // 2
        self.core = lax.rem(self.me, 2)
        self.sibling = self.chip * 2 + 1 - self.core
        self.mates = [self.at(d) for d in range(1, self.chips)]

    def at(self, d):
        return lax.rem(self.chip + d + self.chips, self.chips) * 2 + self.core


class Gather:
    def __init__(self, place, x, out, send, recv):
        rows, chips = x.shape[0], place.chips
        mine = block(out, place.me, rows)
        self.near = remote(x, mine, send.at[0], recv.at[0], place.sibling)
        self.far, self.passed = [], []
        for d in range(1, chips):
            self.far.append(remote(x, mine, send.at[d], recv.at[d], place.mates[d - 1]))
            got = block(out, place.at(-d), rows)
            at = chips + d
            self.passed.append(remote(got, got, send.at[at], recv.at[at], place.sibling))

    def start(self):
        for copy in self.far:
            copy.start()
        self.near.start()

    def finish(self):
        for far, passed in zip(self.far, self.passed):
            far.wait_recv()
            passed.start()
        self.near.wait()
        for copy in self.passed:
            copy.wait()
        for copy in self.far:
            copy.wait_send()


class Scatter:
    def __init__(self, place, x, pair_buf, far_buf, send, recv):
        self.place, self.x = place, x
        self.pair_buf, self.far_buf = pair_buf, far_buf
        chips, self.rows = place.chips, pair_buf.shape[1]
        self.pairs, self.far = [], []
        for d in range(chips):
            theirs = lax.rem(place.chip + d, chips) * 2 + 1 - place.core
            src = block(x, theirs, self.rows)
            self.pairs.append(remote(src, pair_buf.at[d], send.at[d], recv.at[d], place.sibling))
        for d in range(1, chips):
            at = chips + d
            self.far.append(
                remote(pair_buf.at[d], far_buf.at[d], send.at[at], recv.at[at], place.at(d))
            )

    def start(self):
        for copy in self.pairs[1:]:
            copy.start()
        self.pairs[0].start()

    def pass_on(self):
        for d in range(1, self.place.chips):
            self.pairs[d].wait_recv()
            at = pl.ds(pl.multiple_of(self.place.at(d) * self.rows, self.rows), self.rows)
            mine = self.x[at, :].astype(F32) + self.pair_buf[d].astype(F32)
            self.pair_buf[d] = mine.astype(BF)
            self.far[d - 1].start()

    def finish(self):
        self.pairs[0].wait_recv()
        at = pl.ds(pl.multiple_of(self.place.me * self.rows, self.rows), self.rows)
        total = self.x[at, :].astype(F32) + self.pair_buf[0].astype(F32)
        for d in range(1, self.place.chips):
            self.far[d - 1].wait_recv()
            total = total + self.far_buf[d].astype(F32)
        for copy in self.pairs + self.far:
            copy.wait_send()
        return total


def scatter_sum(*refs):
    scatter = Scatter(*refs)
    scatter.start()
    scatter.pass_on()
    return scatter.finish()


def comm_scratch(n, rows, width):
    return [pltpu.VMEM((n // 2, rows, width), BF)] * 2


def sems(count):
    return [pltpu.SemaphoreType.DMA((count,))] * 2


def remote_params(cid):
    return pltpu.CompilerParams(
        collective_id=cid, has_side_effects=True, vmem_limit_bytes=62 * MIB
    )


LOCAL = pltpu.CompilerParams(vmem_limit_bytes=62 * MIB)
WHOLE = pl.BlockSpec(memory_space=pltpu.VMEM)


def slab_pairs(slab, C):
    pairs = slab.shape[1] // (2 * C)
    even = [slab[:, 2 * C * m : 2 * C * m + 256] for m in range(pairs)]
    odd = [slab[:, 2 * C * m + 2 * C - 256 : 2 * C * m + 2 * C] for m in range(pairs)]
    return jnp.concatenate(even, axis=0), jnp.concatenate(odd, axis=0)


def interleave(even, odd, rows):
    parts = []
    for m in range(even.shape[0] // rows):
        parts += [even[m * rows : (m + 1) * rows], odd[m * rows : (m + 1) * rows]]
    return jnp.concatenate(parts, axis=0)


def split_tiles(values, rows):
    count = values.shape[0] // rows
    pick = lambda first: jnp.concatenate(
        [values[k * rows : (k + 1) * rows] for k in range(first, count, 2)], axis=0
    )
    return pick(0), pick(1)


def join_slab(even, odd, rows, C):
    parts = []
    for m in range(even.shape[0] // rows):
        a = even[m * rows : (m + 1) * rows]
        b = odd[m * rows : (m + 1) * rows]
        parts += [a[:, :LANES], a[:, LANES:] + b[:, :LANES], b[:, LANES:]]
    return jnp.concatenate(parts, axis=1)


class Loads:
    def __init__(self, pairs, sem):
        self.copies = [
            pltpu.make_async_copy(src, dst, sem.at[j]) for j, (src, dst) in enumerate(pairs)
        ]

    def start(self):
        for copy in self.copies:
            copy.start()

    def wait(self, first=0, last=None):
        for copy in self.copies[first:last]:
            copy.wait()


def column_of(row):
    return jnp.transpose(jnp.broadcast_to(row, (LANES, row.shape[1])))


def spread(column, width):
    return jnp.concatenate([column] * (width // LANES), axis=1)


def norm_parts(values):
    centred = values - row_mean(values)
    inverse = lax.rsqrt(row_mean(centred * centred) + EPS)
    return centred * inverse, inverse


def forward_kernel(
    n, K, C, nodes, owner, slot, live, g1, o1, g2, o2, w1_h, w2_h, w3_h, wf1_h, wf2_h, we1_h, edges,
    act1, slope1, slope2, tcol, trow, node_out, near, low_out, n1_out, n2_out, inv_out, act_out,
    slope_out, sum_out, nodes_h, far_h,
    w1, w2, w3, wf1, wf2, we1, load_sem,
    nodes_all, far_all, lcol, orow, lrow, scol, hist, hist_got, count,
    p_all, p_own, w_own, pre2, total, summed, q_own, pair_buf, far_buf,
    send, recv, hsend, hrecv, rsend, rrecv, qsend, qrecv, own_sem,
):
    i = pl.program_id(0)
    rows, D = nodes.shape
    tiles = K // GROUP
    size = GROUP * rows
    if n * rows > TABLE:
        p_all = summed = nodes_all
    place = Place(n)
    others = [lax.rem(place.me + d, n) for d in range(1, n)]
    loads = Loads(
        [(w1_h, w1), (w2_h, w2), (w3_h, w3), (wf1_h, wf1), (wf2_h, wf2), (we1_h, we1)], load_sem
    )
    keep_nodes = pltpu.make_async_copy(nodes_all, nodes_h, own_sem.at[1])

    @pl.when(i == 0)
    def _():
        loads.start()
        spare = jnp.zeros((LANES - K, rows), I32)
        own_wide = jnp.concatenate([owner[...], spare], axis=0)
        slot_wide = jnp.concatenate([slot[...], spare], axis=0)
        live_wide = jnp.concatenate([live[...], spare], axis=0).astype(F32)
        target = own_wide * rows + slot_wide
        trow[...] = target
        orow[...] = own_wide
        lrow[...] = live_wide
        tcol[...] = jnp.transpose(target)
        lcol[...] = jnp.transpose(live_wide)
        scol[...] = jnp.transpose(slot_wide)
        pre2[...] = jnp.zeros_like(pre2)
        total[...] = jnp.zeros_like(total)
        w_own[...] = jnp.zeros_like(w_own)
        greet(others)
        gather = Gather(place, nodes, nodes_all, send, recv)
        gather.start()
        own = pltpu.make_async_copy(nodes, block(nodes_all, place.me, rows), own_sem.at[0])
        own.start()

        def tally(g, total):
            ks = [g * GROUP + j for j in range(GROUP)]
            hot = jnp.concatenate([pick_rows(lane_column(scol, k), LANES) for k in ks], axis=0)
            owners = jnp.concatenate([orow[pl.ds(k, 1), :] for k in ks], axis=1)
            lives = jnp.concatenate([lrow[pl.ds(k, 1), :] for k in ks], axis=1)
            sub = lax.broadcasted_iota(I32, (n, size), 0)
            who = jnp.where(
                jnp.broadcast_to(owners, sub.shape) == sub, jnp.broadcast_to(lives, sub.shape), 0.0
            )
            return total + dot(who.astype(BF), hot)

        totals = lax.fori_loop(0, tiles, tally, jnp.zeros((n, LANES), F32))
        for e in range(n):
            hist[e] = jnp.broadcast_to(totals[e : e + 1, :], (8, LANES))
        copies = []
        for d in range(1, n):
            peer = others[d - 1]
            copy = remote(hist.at[peer], hist_got.at[d], hsend.at[d], hrecv.at[d], peer)
            copy.start()
            copies.append(copy)
        loads.wait(0, 2)
        p_own[...] = dot(nodes[...], w1[:D, :])
        w_own[0, :C, :] = w1[2 * D :, :]
        w_own[1, 256 - C :, :] = w1[2 * D :, :]
        tallied = hist[place.me]
        for copy in copies:
            copy.wait_recv()
        for d in range(1, n):
            tallied = tallied + hist_got[d]
        count[...] = tallied
        own.wait()
        gather.finish()
        for copy in copies:
            copy.wait_send()
        keep_nodes.start()
        if n * rows > TABLE:
            keep_nodes.wait()

        def project(part):
            p_all[part, :] = dot(nodes_all[part, :], w1[D : 2 * D, :]).astype(BF)

        by_chunks(n * rows, project)

    last = jnp.clip(i - 1, 0, tiles - 1)
    ks = [last * GROUP + j for j in ORDER]
    act, slope = gelu_pair(pre2[...])
    alive = jnp.concatenate(
        [jnp.concatenate([lane_column(lcol, k)] * (D // LANES), axis=1) for k in ks], axis=0
    ).astype(BF)
    slope2[...] = slope * alive
    act = act * (alive * jnp.where(i >= 1, 1.0, 0.0).astype(BF))
    target = jnp.concatenate([trow[pl.ds(k, 1), :] for k in ks], axis=1)
    add_by_target(target, act, total)

    now = jnp.minimum(i, tiles - 1)
    targets = [lane_column(tcol, now * GROUP + j) for j in ORDER]
    even, odd = slab_pairs(edges[...], C)
    own = jnp.concatenate([dot(even, w_own[0]), dot(odd, w_own[1])], axis=0)
    act, slope = gelu_pair(
        gather_table(targets, p_all) + own + jnp.concatenate([p_own[...]] * GROUP, axis=0)
    )
    act1[...] = act
    slope1[...] = slope
    pre2[...] = dot(act, w2[...])

    @pl.when(i == tiles)
    def _():
        summed[...] = total[...].astype(BF)
        scatter = Scatter(place, summed, pair_buf, far_buf, rsend, rrecv)
        scatter.start()
        scatter.pass_on()
        if n * rows <= TABLE:
            keep_nodes.wait()
        loads.wait(2)
        divisor = 1.0 + column_of(count[0:1, :])
        inv_out[2] = divisor
        mine = scatter.finish().astype(BF)
        sum_out[...] = mine
        resid = nodes[...].astype(F32) + dot(mine, w3[...]) / spread(divisor, D)
        n1, inv1 = norm_parts(resid)
        n1_out[...] = n1
        inv_out[0] = jnp.broadcast_to(inv1, (rows, LANES))
        normed = n1 * g1[...] + o1[...]
        low = normed.astype(BF)
        low_out[...] = low
        act, slope = gelu_full(dot(low, wf1[...]))
        act_out[...] = act
        slope_out[...] = slope
        n2, inv2 = norm_parts(normed + dot(act, wf2[...]))
        n2_out[...] = n2
        inv_out[1] = jnp.broadcast_to(inv2, (rows, LANES))
        node_low = (n2 * g2[...] + o2[...]).astype(BF)
        node_out[...] = node_low
        pad = jnp.zeros((rows, 256 - C), F32)
        far = dot_nt(node_low, we1[:, D : 2 * D])
        q_own[...] = jnp.concatenate([far, pad], axis=1).astype(BF)
        gather = Gather(place, q_own, far_all, qsend, qrecv)
        gather.start()
        own = pltpu.make_async_copy(q_own, block(far_all, place.me, rows), own_sem.at[0])
        own.start()
        near[...] = jnp.concatenate([dot_nt(node_low, we1[:, :D]), pad], axis=1)
        own.wait()
        gather.finish()
        keep_far = pltpu.make_async_copy(far_all, far_h, own_sem.at[2])
        keep_far.start()
        keep_far.wait()


def full(x):
    return pl.BlockSpec(
        x.shape, lambda g: (0,) * x.ndim, pipeline_mode=pl.Buffered(buffer_count=1)
    )


def fixed(*s):
    return pl.BlockSpec(s, lambda g: (0,) * len(s), pipeline_mode=pl.Buffered(buffer_count=1))


HBM = pl.BlockSpec(memory_space=pl.ANY)


def forward_call(n, C, nodes, owner, slot, live, g1, o1, g2, o2, weights, edges):
    rows, D = nodes.shape
    K = slot.shape[0]
    FF = weights[3].shape[1]
    tiles = K // GROUP
    size = GROUP * rows
    count = n * rows
    other = count if count <= TABLE else 16
    shape = jax.ShapeDtypeStruct
    lag = lambda d: pl.BlockSpec((size, D), lambda g: (jnp.clip(g - d, 0, tiles - 1), 0))
    small = [nodes, owner, slot, live, g1, o1, g2, o2]
    outs = [
        shape((LANES, rows), I32),
        shape((LANES, rows), I32),
        shape((rows, D), BF),
        shape((rows, 256), F32),
        shape((rows, D), BF),
        shape((rows, D), F32),
        shape((rows, D), F32),
        shape((3, rows, LANES), F32),
        shape((rows, FF), BF),
        shape((rows, FF), BF),
        shape((rows, D), BF),
    ]
    outs[0] = shape((rows, LANES), I32)
    return pl.pallas_call(
        functools.partial(forward_kernel, n, K, C),
        grid=(tiles + 1,),
        in_specs=[full(v) for v in small]
        + [HBM] * 6
        + [pl.BlockSpec((rows, GROUP * C), lambda g: (0, jnp.minimum(g, tiles - 1)))],
        out_specs=[lag(0), lag(0), lag(1)] + [fixed(*v.shape) for v in outs] + [HBM] * 2,
        out_shape=[shape((K * rows, D), BF)] * 3
        + outs
        + [shape((count, D), BF), shape((count, 256), BF)],
        scratch_shapes=[pltpu.VMEM(v.shape, BF) for v in weights]
        + [
            pltpu.SemaphoreType.DMA((6,)),
            pltpu.VMEM((count, D), BF),
            pltpu.VMEM((count, 256), BF),
            pltpu.VMEM((rows, LANES), F32),
            pltpu.VMEM((LANES, rows), I32),
            pltpu.VMEM((LANES, rows), F32),
            pltpu.VMEM((rows, LANES), I32),
            pltpu.VMEM((n, 8, LANES), F32),
            pltpu.VMEM((n, 8, LANES), F32),
            pltpu.VMEM((8, LANES), F32),
            pltpu.VMEM((other, D), BF),
            pltpu.VMEM((rows, D), F32),
            pltpu.VMEM((2, 256, D), BF),
            pltpu.VMEM((size, D), F32),
            pltpu.VMEM((count, D), F32),
            pltpu.VMEM((other, D), BF),
            pltpu.VMEM((rows, 256), BF),
            *comm_scratch(n, rows, D),
            *sems(n),
            *sems(n),
            *sems(n),
            *sems(n),
            pltpu.SemaphoreType.DMA((3,)),
        ],
        compiler_params=remote_params(0),
    )(*small, *weights, edges)


def edge_kernel(
    tiles, C, tcol, trow, far_all, near, we1, we2, we3, gain, offset, edges1, edges4, edges6, cot,
    edge_out, partial, far_sum, near_sum, dw1, dw2, dw3, dgain,
    w1o, w2p, w3o, w1t, w2t, w3t, gains, total, a1, a2, a3, ag,
    pre1, hid1, slope1, pre2, hid2, slope2, res3, third, up2, up1,
):
    i = pl.program_id(0)
    rows = near.shape[0]
    D2 = we1.shape[1] - C
    gap = 256 - C
    half = GROUP // 2 * rows

    @pl.when(i == 0)
    def _():
        for ref in (w1o, w2p, w3o, w1t, w2t, w3t, gains, total, a1, a2, a3, ag, near_sum,
                    pre1, hid1, slope1, pre2, hid2, slope2, res3, third, up2, up1):
            ref[...] = jnp.zeros_like(ref)
        own = jnp.transpose(we1[:, D2:].astype(F32)).astype(BF)
        w1o[0, :C, :C] = own
        w1o[1, gap:, :C] = own
        w2p[:C, :C] = we2[...]
        w3o[0, :C, :C] = we3[...]
        w3o[1, :C, :] = jnp.concatenate([jnp.zeros((C, gap), F32), we3[...].astype(F32)], axis=1).astype(BF)
        for s in range(2):
            w1t[s] = jnp.transpose(w1o[s].astype(F32)).astype(BF)
            w3t[s] = jnp.transpose(w3o[s].astype(F32)).astype(BF)
        w2t[...] = jnp.transpose(w2p[...].astype(F32)).astype(BF)
        zero = jnp.zeros((1, gap), F32)
        gains[0, 0:1] = jnp.concatenate([gain[...], zero], axis=1)
        gains[0, 1:2] = jnp.concatenate([offset[...], zero], axis=1)
        gains[1, 0:1] = jnp.concatenate([zero, gain[...]], axis=1)
        gains[1, 1:2] = jnp.concatenate([zero, offset[...]], axis=1)

    tile = lambda d: jnp.clip(i - d, 0, tiles - 1)
    sides = [slice(0, half), slice(half, 2 * half)]

    t4 = tile(1)
    valid = jnp.where(i >= 1, 1.0, 0.0)
    slabs = slab_pairs(edges4[...], C)
    cots = slab_pairs(cot[...], C)
    lane = lax.broadcasted_iota(I32, (half, 256), 1)
    outs, grads, ups = [], [], []
    for s in range(2):
        inside = (lane < C) if s == 0 else (lane >= gap)
        keep = lambda v: jnp.where(inside, v, 0.0)
        mean = lambda v: jnp.sum(v, axis=-1, keepdims=True) * (1.0 / C)
        value = keep(slabs[s].astype(F32)) + res3[sides[s], :]
        centred = keep(value - mean(value))
        inverse = lax.rsqrt(mean(centred * centred) + EPS)
        normal = centred * inverse
        outs.append(normal * gains[s, 0:1] + gains[s, 1:2])
        upstream = keep(cots[s].astype(F32)) * valid
        moved = upstream * normal
        for r in range(half // rows):
            part = slice(r * rows, (r + 1) * rows)
            ag[s, 0] += moved[part]
            ag[s, 1] += upstream[part]
        scaled = upstream * gains[s, 0:1]
        grad = inverse * (scaled - mean(scaled) - normal * mean(scaled * normal))
        grad = keep(grad)
        grads.append(grad)
        low3 = grad.astype(BF)
        a3[s] += dot_tn(hid2[sides[s], :], low3)
        ups.append(dot(low3, w3t[s]))
    edge_out[...] = join_slab(outs[0], outs[1], rows, C).astype(BF)

    t5 = tile(1)
    low2 = (jnp.concatenate(ups, axis=0) * slope2[0].astype(F32)).astype(BF)
    a2[...] += dot_tn(hid1[0], low2)
    up1v = dot(low2, w2t[...])

    t6 = tile(1)
    low1 = (up1v * slope1[0].astype(F32)).astype(BF)
    slabs = slab_pairs(edges4[...], C)
    outs = []
    for s in range(2):
        a1[s] += dot_tn(low1[sides[s]], slabs[s])
        outs.append(grads[s] + dot(low1[sides[s]], w1t[s]))
    partial[...] = join_slab(outs[0], outs[1], rows, C).astype(BF)
    wide = low1.astype(F32)
    acc = wide[:rows]
    for j in range(1, GROUP):
        acc = acc + wide[j * rows : (j + 1) * rows]
    near_sum[...] += acc
    target = jnp.concatenate([trow[pl.ds(t6 * GROUP + j, 1), :] for j in ORDER], axis=1)
    add_by_target(target, low1, total)

    t1 = tile(0)
    slabs = slab_pairs(edges1[...], C)
    own = jnp.concatenate([dot(slabs[0], w1o[0]), dot(slabs[1], w1o[1])], axis=0)
    got = gather_table([lane_column(tcol, t1 * GROUP + j) for j in ORDER], far_all)
    pre1v = got + own + jnp.concatenate([near[...]] * GROUP, axis=0)

    t2 = tile(0)
    act, slope = gelu_pair(pre1v)
    hid1[0] = act
    slope1[0] = slope
    pre2v = dot(act, w2p[...])

    t3 = tile(0)
    act, slope = gelu_pair(pre2v)
    hid2[...] = act
    slope2[0] = slope
    for s in range(2):
        res3[sides[s], :] = dot(act[sides[s]], w3o[s])

    @pl.when(i == tiles)
    def _():
        far_sum[...] = total[...].astype(BF)
        dw1[...] = jnp.transpose(a1[0])[:C, :] + jnp.transpose(a1[1])[gap:, :]
        dw2[...] = a2[...]
        shifted = a3[1][:, gap:]
        dw3[...] = a3[0] + jnp.concatenate([shifted, jnp.zeros((256, gap), F32)], axis=1)
        for r in range(2):
            even = jnp.sum(ag[0, r], axis=0, keepdims=True)
            odd = jnp.sum(ag[1, r], axis=0, keepdims=True)
            row = even + jnp.concatenate([odd[:, gap:], jnp.zeros((1, gap), F32)], axis=1)
            dgain[r * 8 : r * 8 + 8, :] = jnp.broadcast_to(row, (8, 256))


def edge_call(C, tcol, trow, far_all, near, we1, we2, we3, gain, offset, edges, cot):
    rows = near.shape[0]
    count = far_all.shape[0]
    K = edges.shape[1] // C
    tiles = K // GROUP
    size = GROUP * rows
    shape = jax.ShapeDtypeStruct
    slab = lambda d: pl.BlockSpec(
        (rows, GROUP * C), lambda g: (0, jnp.clip(g - d, 0, tiles - 1))
    )
    fixed = lambda *s: pl.BlockSpec(
        s, lambda g: (0,) * len(s), pipeline_mode=pl.Buffered(buffer_count=1)
    )
    return pl.pallas_call(
        functools.partial(edge_kernel, tiles, C),
        grid=(tiles + 1,),
        in_specs=[full(x) for x in (tcol, trow, far_all, near, we1, we2, we3, gain, offset)]
        + [slab(0), slab(1), slab(99), slab(1)],
        out_specs=[
            slab(1), slab(1), fixed(count, 256), fixed(rows, 256),
            fixed(C, 256), fixed(256, 256), fixed(256, 256), fixed(16, 256),
        ],
        out_shape=[
            shape((rows, K * C), BF),
            shape((rows, K * C), BF),
            shape((count, 256), BF),
            shape((rows, 256), F32),
            shape((C, 256), F32),
            shape((256, 256), F32),
            shape((256, 256), F32),
            shape((16, 256), F32),
        ],
        scratch_shapes=[
            pltpu.VMEM((2, 256, 256), BF),
            pltpu.VMEM((256, 256), BF),
            pltpu.VMEM((2, 256, 256), BF),
            pltpu.VMEM((2, 256, 256), BF),
            pltpu.VMEM((256, 256), BF),
            pltpu.VMEM((2, 256, 256), BF),
            pltpu.VMEM((2, 8, 256), F32),
            pltpu.VMEM((count, 256), F32),
            pltpu.VMEM((2, 256, 256), F32),
            pltpu.VMEM((256, 256), F32),
            pltpu.VMEM((2, 256, 256), F32),
            pltpu.VMEM((2, 2, rows, 256), F32),
            pltpu.VMEM((size, 256), F32),
            pltpu.VMEM((3, size, 256), BF),
            pltpu.VMEM((4, size, 256), BF),
            pltpu.VMEM((size, 256), F32),
            pltpu.VMEM((size, 256), BF),
            pltpu.VMEM((2, size, 256), BF),
            pltpu.VMEM((size, 256), F32),
            pltpu.VMEM((2, size, 256), F32),
            pltpu.VMEM((size, 256), F32),
            pltpu.VMEM((size, 256), F32),
        ],
        compiler_params=LOCAL,
    )(tcol, trow, far_all, near, we1, we2, we3, gain, offset, edges, edges, edges, cot)


def norm_back(upstream, normal, inverse, gain):
    scaled = upstream * gain
    return inverse * (scaled - row_mean(scaled) - normal * row_mean(scaled * normal))


def node_back_kernel(
    n, C, far_sum, near_sum, cot, node_low, n1, n2, inv, act, slope, low, summed,
    w3, g1, wf1, wf2, g2, we1,
    grad_one, vw_all, both, dgain, dw3, dwe_near, dwe_far,
    pair_buf, far_buf, v_own, send, recv, gsend, grecv, own_sem,
):
    place = Place(n)
    rows, D = cot.shape
    greet([place.sibling] + place.mates)
    far = scatter_sum(place, far_sum, pair_buf, far_buf, send, recv)
    far = far.astype(BF)[:, :C]
    near = near_sum[...].astype(BF)[:, :C]
    grad = cot[...].astype(F32) + dot(near, we1[:, :D]) + dot(far, we1[:, D : 2 * D])
    two = norm_back(grad, n2[...], inv[1][:, 0:1], g2[...])
    dgain[16:24, :] = jnp.broadcast_to(jnp.sum(grad * n2[...], axis=0, keepdims=True), (8, D))
    dgain[24:32, :] = jnp.broadcast_to(jnp.sum(grad, axis=0, keepdims=True), (8, D))
    resid = two.astype(BF)
    both[:, :D] = low[...]
    both[:, D:] = resid
    inner = (dot_nt(resid, wf2[...]) * slope[...].astype(F32)).astype(BF)
    grad = two + dot_nt(inner, wf1[...])
    one = norm_back(grad, n1[...], inv[0][:, 0:1], g1[...])
    dgain[0:8, :] = jnp.broadcast_to(jnp.sum(grad * n1[...], axis=0, keepdims=True), (8, D))
    dgain[8:16, :] = jnp.broadcast_to(jnp.sum(grad, axis=0, keepdims=True), (8, D))
    grad_one[...] = one
    upper = (one / spread(inv[2], D)).astype(BF)
    v_own[...] = dot_nt(upper, w3[...]).astype(BF)
    gather = Gather(place, v_own, vw_all, gsend, grecv)
    gather.start()
    own = pltpu.make_async_copy(v_own, block(vw_all, place.me, rows), own_sem.at[0])
    own.start()
    dw3[...] = dot_tn(summed[...], upper)
    dwe_near[...] = dot_tn(node_low[...], near)
    dwe_far[...] = dot_tn(node_low[...], far)
    own.wait()
    gather.finish()


def node_back_call(n, C, *args):
    cot, wf1 = args[2], args[13]
    rows, D = cot.shape
    shape = jax.ShapeDtypeStruct
    return pl.pallas_call(
        functools.partial(node_back_kernel, n, C),
        in_specs=[WHOLE] * len(args),
        out_specs=[WHOLE] * 7,
        out_shape=[
            shape((rows, D), F32),
            shape((n * rows, D), BF),
            shape((rows, 2 * D), BF),
            shape((32, D), F32),
            shape((D, D), F32),
            shape((D, C), F32),
            shape((D, C), F32),
        ],
        scratch_shapes=[
            *comm_scratch(n, rows, 256),
            pltpu.VMEM((rows, D), BF),
            *sems(n),
            *sems(n),
            pltpu.SemaphoreType.DMA((1,)),
        ],
        compiler_params=remote_params(2),
    )(*args)


class Line:
    def __init__(self, place, pieces, x, out, pair_buf, low_buf, high_buf, send_buf, send, recv):
        self.place, self.pieces, self.x, self.out = place, pieces, x, out
        self.pair_buf, self.low_buf, self.high_buf = pair_buf, low_buf, high_buf
        self.send_buf, self.send, self.recv = send_buf, send, recv
        c, q, chips = place.chip, place.core, place.chips
        self.root = chips // 2 - 1 + q
        self.away = jnp.abs(c - self.root)
        self.right = jnp.minimum(c + 1, chips - 1) * 2 + q
        self.left = jnp.maximum(c - 1, 0) * 2 + q
        self.half = x.shape[0] // 2
        self.rows = self.half // pieces

    def part(self, which, p):
        return pl.ds(pl.multiple_of(which * self.half + p * self.rows, self.rows), self.rows)

    def here(self, p):
        return pl.ds(pl.multiple_of(p * self.rows, self.rows), self.rows)

    def link(self, src, dst, p, sent, got, peer):
        n = self.pieces
        return remote(src, dst, self.send.at[sent * n + p], self.recv.at[got * n + p], peer)

    def pair(self, p):
        src = self.x.at[self.part(1 - self.place.core, p)]
        return self.link(src, self.pair_buf.at[self.here(p)], p, 0, 0, self.place.sibling)

    def up(self, p):
        here = self.here(p)
        return self.link(self.send_buf.at[here], self.low_buf.at[here], p, 1, 1, self.right)

    def down(self, p):
        here = self.here(p)
        return self.link(self.send_buf.at[here], self.high_buf.at[here], p, 2, 2, self.left)

    def outward(self, p, sent, got, peer):
        mine = self.out.at[self.part(self.place.core, p)]
        return self.link(mine, mine, p, sent, got, peer)

    def out_left(self, p):
        return self.outward(p, 3, 3, self.left)

    def out_right(self, p):
        return self.outward(p, 5, 3, self.right)

    def across(self, p):
        return self.outward(p, 4, 4, self.place.sibling)

    def each(self, step):
        lax.fori_loop(0, self.pieces, lambda p, z: (step(p), z)[1], 0)

    def start(self):
        self.each(lambda p: self.pair(p).start())

    def reduce(self, p):
        c, root, last = self.place.chip, self.root, self.place.chips - 1
        here, mine_at = self.here(p), self.part(self.place.core, p)
        self.pair(p).wait_recv()
        mine = lambda: self.x[mine_at, :].astype(F32) + self.pair_buf[here, :].astype(F32)

        def end():
            self.send_buf[here, :] = mine().astype(BF)

        def from_low():
            self.up(p).wait_recv()
            self.send_buf[here, :] = (mine() + self.low_buf[here, :].astype(F32)).astype(BF)

        def from_high():
            self.down(p).wait_recv()
            self.send_buf[here, :] = (mine() + self.high_buf[here, :].astype(F32)).astype(BF)

        def at_root():
            self.up(p).wait_recv()
            self.down(p).wait_recv()
            total = mine() + self.low_buf[here, :].astype(F32) + self.high_buf[here, :].astype(F32)
            self.out[mine_at, :] = total.astype(BF)
            self.out_left(p).start()
            self.out_right(p).start()
            self.across(p).start()

        pl.when((c == 0) | (c == last))(end)
        pl.when((c > 0) & (c < root))(from_low)
        pl.when((c > root) & (c < last))(from_high)
        pl.when(c < root)(lambda: self.up(p).start())
        pl.when(c > root)(lambda: self.down(p).start())
        pl.when(c == root)(at_root)

    def spread(self, p):
        c, root, last = self.place.chip, self.root, self.place.chips - 1

        def leftward():
            self.out_left(p).wait_recv()
            pl.when(c > 0)(lambda: self.out_left(p).start())
            self.across(p).start()

        def rightward():
            self.out_right(p).wait_recv()
            pl.when(c < last)(lambda: self.out_right(p).start())
            self.across(p).start()

        pl.when(c < root)(leftward)
        pl.when(c > root)(rightward)

    def slots(self, lag):
        return self.pieces + 2 * lag * (self.place.chips // 2)

    def slot(self, s, lag):
        deep = self.place.chips // 2
        p = s - lag * (deep - self.away)
        pl.when((p >= 0) & (p < self.pieces))(lambda: self.reduce(p))
        o = s - lag * (deep + self.away)
        pl.when((o >= 0) & (o < self.pieces) & (self.away > 0))(lambda: self.spread(o))

    def finish(self):
        c, root, last = self.place.chip, self.root, self.place.chips - 1

        def end(p):
            self.pair(p).wait_send()
            self.across(p).wait_send()
            pl.when(c < root)(lambda: self.up(p).wait_send())
            pl.when(c > root)(lambda: self.down(p).wait_send())
            pl.when((c <= root) & (c > 0))(lambda: self.out_left(p).wait_send())
            pl.when((c >= root) & (c < last))(lambda: self.out_right(p).wait_send())

        self.each(lambda p: self.across(p).wait_recv())
        self.each(end)


def line_scratch(rows, width, pieces):
    return [pltpu.VMEM((rows // 2, width), BF)] * 4 + sems(6 * pieces)


class Exchange:
    def __init__(self, place, n, mine, got, send, recv):
        self.place, self.n, self.mine, self.got = place, n, mine, got
        self.copies = []
        for d in range(1, n):
            peer = lax.rem(place.me + d, n)
            self.copies.append(remote(mine, got.at[place.me], send.at[d], recv.at[d], peer))

    def start(self):
        for copy in self.copies:
            copy.start()
        self.got[self.place.me] = self.mine[...]

    def finish(self):
        for copy in self.copies:
            copy.wait_recv()
        total = self.got[0]
        for e in range(1, self.n):
            total = total + self.got[e]
        for copy in self.copies:
            copy.wait_send()
        return total


PIECES = 19
LAG = 4


def pack_sums(C, x, gains, dw1, dw2, dw3, dwe_near, dwe_far, dwe1, dwe2, dwe3, dgain, dg3):
    D = dw3.shape[0]
    at = 2 * D + C
    if dw1 is not x:
        x[:at, :] = dw1[...]
        x[at : at + D, :] = dw2[...]
    at += D
    x[at : at + D, :] = dw3[...].astype(BF)
    at += D
    spare = jnp.zeros((D, 256 - C), F32)
    edge1 = jnp.concatenate(
        [
            jnp.concatenate([dwe_near[...], spare], axis=1),
            jnp.concatenate([dwe_far[...], spare], axis=1),
            dwe1[...],
        ],
        axis=0,
    ).astype(BF)
    half = edge1.shape[0] // 2
    x[at : at + half, :256] = edge1[:half]
    x[at : at + half, 256:] = edge1[half:]
    at += half
    x[at : at + C, :256] = dwe2[:C, :].astype(BF)
    x[at : at + C, 256:] = dwe3[:C, :].astype(BF)
    gains[...] = jnp.zeros_like(gains)
    for r in range(4):
        gains[r : r + 1, :] = dgain[8 * r : 8 * r + 1, :]
    for r in range(2):
        gains[4 + r : 5 + r, :256] = dg3[8 * r : 8 * r + 1, :]


def back_start(C, w1, w2, w2t, w_own, w_own_t, zeroed):
    D = w2.shape[0]
    gap = 256 - C
    for ref in (w_own, *zeroed):
        ref[...] = jnp.zeros_like(ref)
    w_own[0, :C, :] = w1[2 * D :, :]
    w_own[1, gap:, :] = w1[2 * D :, :]
    for s in range(2):
        w_own_t[s] = jnp.transpose(w_own[s].astype(F32)).astype(BF)
    w2t[...] = jnp.transpose(w2[...].astype(F32)).astype(BF)


def back_tile(
    g, rows, C, tcol, trow, vw, act1, slope1, slope2, edges, partial, grad_edges,
    w2t, w_own_t, total, a2, ae, source_sum,
):
    half = GROUP // 2 * rows
    ks = [g * GROUP + j for j in ORDER]
    up = gather_table([lane_column(tcol, k) for k in ks], vw)
    upper = up.astype(BF) * slope2[...]
    a2[...] += dot_tn(act1[...], upper)
    lower = dot(upper, w2t[...]).astype(BF) * slope1[...]
    wide = lower.astype(F32)
    acc = wide[:rows]
    for j in range(1, GROUP):
        acc = acc + wide[j * rows : (j + 1) * rows]
    source_sum[...] += acc
    target = jnp.concatenate([trow[pl.ds(k, 1), :] for k in ks], axis=1)
    add_by_target(target, lower, total)
    slabs = slab_pairs(edges[...], C)
    lowers = [lower[:half], lower[half:]]
    own = []
    for s in range(2):
        ae[s] += dot_tn(slabs[s], lowers[s])
        own.append(dot(lowers[s], w_own_t[s]))
    grad_edges[...] = (partial[...].astype(F32) + join_slab(own[0], own[1], rows, C)).astype(BF)


def back_weights(C, dw1, dw2, nodes_all, nodes, total, a2, ae, source_sum):
    D = nodes.shape[1]
    gap = 256 - C
    dw2[...] = a2[...].astype(BF)
    dw1[:D, :] = dot_tn(nodes[...], source_sum[...].astype(BF)).astype(BF)
    dw1[2 * D :, :] = (ae[0][:C, :] + ae[1][gap:, :]).astype(BF)
    a2[...] = jnp.zeros_like(a2)

    def weigh(part):
        a2[...] += dot_tn(nodes_all[part, :], total[part, :].astype(BF))

    by_chunks(total.shape[0], weigh)
    dw1[D : 2 * D, :] = a2[...].astype(BF)


def tail(
    place, n, line, scatter, exchange, source_sum, grad_one, w1, grad_nodes, small, feed,
):
    D = grad_one.shape[1]
    line.start()
    scatter.start()
    exchange.start()
    scatter.pass_on()

    def feed_part(f):
        both, wf1, wf2, dwf1, dwf2 = feed
        step = 256
        cols = pl.ds(pl.multiple_of(f * step, step), step)
        low, resid = both[:, :D], both[:, D:]
        act, slope = gelu_full(dot(low, wf1[:, cols]))
        dwf2[cols, :] = dot_tn(act, resid).astype(BF)
        inner = (dot_nt(resid, wf2[cols, :]) * slope.astype(F32)).astype(BF)
        dwf1[:, cols] = dot_tn(low, inner).astype(BF)

    parts = feed[1].shape[1] // 256 if feed else 0

    def slot(s, carry):
        line.slot(s, LAG)
        if feed:
            pl.when((s % 2 == 1) & (s // 2 < parts))(lambda: feed_part(s // 2))
        return carry

    lax.fori_loop(0, line.slots(LAG), slot, 0)
    source = dot_nt(source_sum[...].astype(BF), w1[:D, :])
    total = scatter.finish()
    grad_nodes[...] = grad_one[...] + source + dot_nt(total.astype(BF), w1[D : 2 * D, :])
    small[...] = exchange.finish()
    line.finish()


def back_kernel(
    n, tiles, C, tcol, trow, nodes, vw, w1, w2,
    dw3, dwe_near, dwe_far, dwe1, dwe2, dwe3, dgain, dg3, both_own,
    nodes_all_h, grad_one_h, wf1_h, wf2_h, act1, slope1, slope2, edges, partial,
    grad_edges, grad_nodes, small, dwf1, dwf2, out_h,
    nodes_all, grad_one, wf1, wf2, load_sem, both, bsend, brecv, out,
    w2t, w_own, w_own_t, total, a2, ae, source_sum, target_sum, x, gains, got, gsend, grecv,
    pair_buf, far_buf, send, recv, *line_refs,
):
    g = pl.program_id(0)
    rows, D = nodes.shape
    place = Place(n)
    loads = Loads(
        [(nodes_all_h, nodes_all), (grad_one_h, grad_one), (wf1_h, wf1), (wf2_h, wf2)], load_sem
    )
    gather = Gather(place, both_own, both, bsend, brecv)
    keep_own = pltpu.make_async_copy(both_own, block(both, place.me, rows), load_sem.at[4])

    @pl.when(g == 0)
    def _():
        loads.start()
        keep_own.start()
        greet([lax.rem(place.me + d, n) for d in range(1, n)])
        gather.start()
        back_start(C, w1, w2, w2t, w_own, w_own_t, (total, a2, ae, source_sum))

    back_tile(
        g, rows, C, tcol, trow, vw, act1, slope1, slope2, edges, partial, grad_edges,
        w2t, w_own_t, total, a2, ae, source_sum,
    )

    @pl.when(g == tiles - 1)
    def _():
        target_sum[...] = total[...].astype(BF)
        loads.wait()
        keep_own.wait()
        gather.finish()
        at = 2 * D + C
        back_weights(
            C, x.at[pl.ds(0, at)], x.at[pl.ds(at, D)], nodes_all, nodes, total, a2, ae, source_sum
        )
        pack_sums(C, x, gains, x, x, dw3, dwe_near, dwe_far, dwe1, dwe2, dwe3, dgain, dg3)
        tail(
            place, n, Line(place, PIECES, x, out, *line_refs),
            Scatter(place, target_sum, pair_buf, far_buf, send, recv),
            Exchange(place, n, gains, got, gsend, grecv),
            source_sum, grad_one, w1, grad_nodes, small, (both, wf1, wf2, dwf1, dwf2),
        )
        keep_out = pltpu.make_async_copy(out, out_h, load_sem.at[5])
        keep_out.start()
        keep_out.wait()


def sum_rows(D, C):
    return 4 * D + C + (2 * D + C) // 2 + C


def back_call(n, C, tcol, trow, nodes, vw, w1, w2, sums, both_own, loaded, act1, slope1, slope2, edges, partial):
    rows, D = nodes.shape
    count = vw.shape[0]
    K = edges.shape[1] // C
    tiles = K // GROUP
    size = GROUP * rows
    FF = loaded[2].shape[1]
    total = sum_rows(D, C)
    shape = jax.ShapeDtypeStruct
    slab = pl.BlockSpec((rows, GROUP * C), lambda g: (0, g))
    tile = pl.BlockSpec((size, D), lambda g: (g, 0))
    whole = [tcol, trow, nodes, vw, w1, w2, *sums, both_own]
    outs = [
        shape((rows, D), F32),
        shape((8, D), F32),
        shape((D, FF), BF),
        shape((FF, D), BF),
    ]
    return pl.pallas_call(
        functools.partial(back_kernel, n, tiles, C),
        grid=(tiles,),
        in_specs=[full(v) for v in whole] + [HBM] * 4 + [tile, tile, tile, slab, slab],
        out_specs=[slab] + [fixed(*v.shape) for v in outs] + [HBM],
        out_shape=[shape((rows, K * C), BF)] + outs + [shape((total, D), BF)],
        scratch_shapes=[pltpu.VMEM(v.shape, v.dtype) for v in loaded]
        + [
            pltpu.SemaphoreType.DMA((6,)),
            pltpu.VMEM((count, 2 * D), BF),
            *sems(n),
            pltpu.VMEM((total, D), BF),
            pltpu.VMEM((D, D), BF),
            pltpu.VMEM((2, 256, D), BF),
            pltpu.VMEM((2, D, 256), BF),
            pltpu.VMEM((count, D), F32),
            pltpu.VMEM((D, D), F32),
            pltpu.VMEM((2, 256, D), F32),
            pltpu.VMEM((rows, D), F32),
            pltpu.VMEM((count, D), BF),
            pltpu.VMEM((total, D), BF),
            pltpu.VMEM((8, D), F32),
            pltpu.VMEM((n, 8, D), F32),
            *sems(n),
            *comm_scratch(n, rows, D),
            *sems(n),
            *line_scratch(total, D, PIECES),
        ],
        compiler_params=remote_params(3),
    )(*whole, *loaded, act1, slope1, slope2, edges, partial)


def message_back_kernel(
    tiles, C, tcol, trow, nodes_all, nodes, vw, w1, w2, act1, slope1, slope2, edges, partial,
    grad_edges, dw1, dw2, target_sum, source_sum, w2t, w_own, w_own_t, total, a2, ae,
):
    g = pl.program_id(0)

    @pl.when(g == 0)
    def _():
        back_start(C, w1, w2, w2t, w_own, w_own_t, (total, a2, ae, source_sum))

    back_tile(
        g, nodes.shape[0], C, tcol, trow, vw, act1, slope1, slope2, edges, partial, grad_edges,
        w2t, w_own_t, total, a2, ae, source_sum,
    )

    @pl.when(g == tiles - 1)
    def _():
        target_sum[...] = total[...].astype(BF)
        back_weights(C, dw1, dw2, nodes_all, nodes, total, a2, ae, source_sum)


def message_back_call(C, tcol, trow, nodes_all, nodes, vw, w1, w2, act1, slope1, slope2, edges, partial):
    rows, D = nodes.shape
    count = vw.shape[0]
    K = edges.shape[1] // C
    tiles = K // GROUP
    size = GROUP * rows
    shape = jax.ShapeDtypeStruct
    slab = pl.BlockSpec((rows, GROUP * C), lambda g: (0, g))
    tile = pl.BlockSpec((size, D), lambda g: (g, 0))
    return pl.pallas_call(
        functools.partial(message_back_kernel, tiles, C),
        grid=(tiles,),
        in_specs=[full(x) for x in (tcol, trow, nodes_all, nodes, vw, w1, w2)]
        + [tile, tile, tile, slab, slab],
        out_specs=[slab, fixed(2 * D + C, D), fixed(D, D), fixed(count, D), fixed(rows, D)],
        out_shape=[
            shape((rows, K * C), BF),
            shape((2 * D + C, D), BF),
            shape((D, D), BF),
            shape((count, D), BF),
            shape((rows, D), F32),
        ],
        scratch_shapes=[
            pltpu.VMEM((D, D), BF),
            pltpu.VMEM((2, 256, D), BF),
            pltpu.VMEM((2, D, 256), BF),
            pltpu.VMEM((count, D), F32),
            pltpu.VMEM((D, D), F32),
            pltpu.VMEM((2, 256, D), F32),
        ],
        compiler_params=LOCAL,
    )(tcol, trow, nodes_all, nodes, vw, w1, w2, act1, slope1, slope2, edges, partial)


def final_kernel(
    n, C, target_sum, source_sum, grad_one, w1, dw1, dw2, dw3, dwe_near, dwe_far, dwe1, dwe2, dwe3,
    dgain, dg3, grad_nodes, out, small,
    x, gains, got, gsend, grecv, pair_buf, far_buf, send, recv, *line_refs,
):
    place = Place(n)
    greet([lax.rem(place.me + d, n) for d in range(1, n)])
    pack_sums(C, x, gains, dw1, dw2, dw3, dwe_near, dwe_far, dwe1, dwe2, dwe3, dgain, dg3)
    tail(
        place, n, Line(place, PIECES, x, out, *line_refs),
        Scatter(place, target_sum, pair_buf, far_buf, send, recv),
        Exchange(place, n, gains, got, gsend, grecv),
        source_sum, grad_one, w1, grad_nodes, small, None,
    )


def final_call(n, C, args):
    rows, D = args[2].shape
    size = sum_rows(D, C)
    shape = jax.ShapeDtypeStruct
    return pl.pallas_call(
        functools.partial(final_kernel, n, C),
        in_specs=[WHOLE] * len(args),
        out_specs=[WHOLE] * 3,
        out_shape=[shape((rows, D), F32), shape((size, D), BF), shape((8, D), F32)],
        scratch_shapes=[
            pltpu.VMEM((size, D), BF),
            pltpu.VMEM((8, D), F32),
            pltpu.VMEM((n, 8, D), F32),
            *sems(n),
            *comm_scratch(n, rows, D),
            *sems(n),
            *line_scratch(size, D, PIECES),
        ],
        compiler_params=remote_params(4),
    )(*args)


def feed_kernel(low, resid, wf1, wf2, dwf1, dwf2):
    @pl.when(pl.program_id(1) == 0)
    def _():
        dwf1[...] = jnp.zeros_like(dwf1)
        dwf2[...] = jnp.zeros_like(dwf2)

    act, slope = gelu_full(dot(low[...], wf1[...]))
    dwf2[...] += dot_tn(act, resid[...])
    inner = (dot_nt(resid[...], wf2[...]) * slope.astype(F32)).astype(BF)
    dwf1[...] += dot_tn(low[...], inner)


def feed_call(both, wf1, wf2):
    count = both.shape[0]
    D, FF = wf1.shape
    step, rows = min(FF, 512), min(count, TABLE)
    shape = jax.ShapeDtypeStruct
    return pl.pallas_call(
        feed_kernel,
        grid=(FF // step, count // rows),
        in_specs=[
            pl.BlockSpec((rows, D), lambda f, r: (r, 0)),
            pl.BlockSpec((rows, D), lambda f, r: (r, 1)),
            pl.BlockSpec((D, step), lambda f, r: (0, f)),
            pl.BlockSpec((step, D), lambda f, r: (f, 0)),
        ],
        out_specs=[
            pl.BlockSpec((D, step), lambda f, r: (0, f)),
            pl.BlockSpec((step, D), lambda f, r: (f, 0)),
        ],
        out_shape=[shape((D, FF), F32), shape((FF, D), F32)],
        compiler_params=LOCAL,
    )(both, both, wf1, wf2)


def unpack_kernel(C, steps, packed, small, edges, *refs):
    g = pl.program_id(0)
    D = packed.shape[1]
    plain = refs[: (len(refs) - 13) // 2]
    w1, w2, w3, grad_edges, one, two, three, *outs = refs[len(plain) :]
    gains = outs[len(plain) :]
    grad_edges[...] = edges[...].astype(F32)
    at = 0
    for ref, size in ((w1, 2 * D + C), (w2, D), (w3, D)):
        step = size // steps
        ref[...] = packed[pl.ds(pl.multiple_of(at + g * step, 16), step), :].astype(F32)
        at += size
    for a, b in zip(plain, outs):
        b[...] = a[...].astype(F32)

    @pl.when(g == steps - 1)
    def _():
        half = (2 * D + C) // 2
        for r in range(2):
            left = 256 * r
            flipped = jnp.transpose(packed[at : at + half, left : left + 256].astype(F32))
            one[:, half * r : half * r + half] = flipped[:C, :]
        end = at + half
        two[...] = packed[end : end + C, :C].astype(F32)
        three[...] = packed[end : end + C, 256 : 256 + C].astype(F32)
        for r in range(6):
            width = D if r < 4 else C
            gains[r][...] = small[r : r + 1, :width]


def unpack_call(C, packed, small, edges, arrays):
    steps = 4
    D = packed.shape[1]
    first = 2 * D + C
    shape = jax.ShapeDtypeStruct
    cut = lambda r, c: pl.BlockSpec((r // steps, c), lambda g: (g, 0))
    head = [(first, D), (D, D), (D, D), edges.shape]
    last = [(C, first), (C, C), (C, C)]
    plain = [v.shape for v in arrays]
    gains = [(1, D)] * 4 + [(1, C)] * 2
    return pl.pallas_call(
        functools.partial(unpack_kernel, C, steps),
        grid=(steps,),
        in_specs=[full(packed), full(small)] + [cut(*v.shape) for v in (edges, *arrays)],
        out_specs=[cut(*v) for v in head]
        + [fixed(*v) for v in last]
        + [cut(*v) for v in plain]
        + [fixed(*v) for v in gains],
        out_shape=[shape(v, F32) for v in head + last + plain + gains],
        compiler_params=LOCAL,
    )(packed, small, edges, *arrays)


def body(
    nodes, edges, nbr_owner, nbr_slot, edge_mask, w_msg1, w_msg2, w_msg3, gain_one, offset_one,
    w_ffn1, w_ffn2, gain_two, offset_two, w_edge1, w_edge2, w_edge3, gain_three, offset_three,
    node_cotangent, edge_cotangent,
):
    n = lax.axis_size("edge")
    rows, D = nodes.shape
    C = w_edge2.shape[0]
    we1 = w_edge1.T
    g1, o1, g2, o2 = (v.reshape(1, D) for v in (gain_one, offset_one, gain_two, offset_two))
    (
        act1, slope1, slope2, tcol, trow, node_out, near, low, n1, n2, inv, act, slope, own_sum,
        nodes_all, far_all,
    ) = forward_call(
        n, C, nodes, nbr_owner[:, :, 0].T, nbr_slot.T, edge_mask.T, g1, o1, g2, o2,
        [w_msg1, w_msg2, w_msg3, w_ffn1, w_ffn2, we1], edges,
    )
    edge_out, partial, far_sum, near_sum, dwe1, dwe2, dwe3, dg3 = edge_call(
        C, tcol, trow, far_all, near, we1, w_edge2, w_edge3,
        gain_three.reshape(1, C), offset_three.reshape(1, C), edges, edge_cotangent,
    )
    grad_one, vw_all, both, dgain, dw3, dwe_near, dwe_far = node_back_call(
        n, C, far_sum, near_sum, node_cotangent, node_out, n1, n2, inv, act, slope, low, own_sum,
        w_msg3, g1, w_ffn1, w_ffn2, g2, we1,
    )
    sums = [dw3, dwe_near, dwe_far, dwe1, dwe2, dwe3, dgain, dg3]
    kept = [act1, slope1, slope2, edges, partial]
    if n * rows <= TABLE:
        grad_edges, grad_nodes, small, *dwf, packed = back_call(
            n, C, tcol, trow, nodes, vw_all, w_msg1, w_msg2, sums, both,
            [nodes_all, grad_one, w_ffn1, w_ffn2], *kept,
        )
        tot1, tot2, tot3, grad_edges, we1_t, tot_e2, tot_e3, dwf1, dwf2, *gains = unpack_call(
            C, packed, small, grad_edges, dwf
        )
    else:
        grad_edges, dw1, dw2, target_sum, source_sum = message_back_call(
            C, tcol, trow, nodes_all, nodes, vw_all, w_msg1, w_msg2, *kept
        )
        grad_nodes, packed, small = final_call(
            n, C, [target_sum, source_sum, grad_one, w_msg1, dw1, dw2, *sums]
        )
        tot1, tot2, tot3, grad_edges, we1_t, tot_e2, tot_e3, *gains = unpack_call(
            C, packed, small, grad_edges, []
        )
        both = lax.all_gather(both, "edge", axis=0, tiled=True)
        dwf1, dwf2 = feed_call(both, w_ffn1, w_ffn2)
    gains = [v.reshape(v.shape[1]) for v in gains]
    return (
        node_out, edge_out, grad_nodes, grad_edges,
        tot1, tot2, tot3, gains[0], gains[1], dwf1, dwf2, gains[2], gains[3],
        we1_t.T, tot_e2, tot_e3, gains[4], gains[5],
    )


def solution(mesh):
    rows = P(("dp", "edge"), None)
    return jax.shard_map(
        body,
        mesh=mesh,
        in_specs=(rows, rows, P(("dp", "edge"), None, None), rows, rows)
        + (P(),) * 14
        + (rows, rows),
        out_specs=(rows,) * 4
        + (P("dp", None),) * 3
        + (P("dp"),) * 2
        + (P("dp", None),) * 2
        + (P("dp"),) * 2
        + (P("dp", None),) * 3
        + (P("dp"),) * 2,
        check_vma=False,
    )
```

time: 312 us -> 271 us (0.87)
  Pallas kernels: 291 us -> 268 us
  between operations: 14.1 us -> 0.71 us
    pallas_call x7 -> x4, Pallas kernels: 261 us -> 237 us  [the longest x1 112 us: back_call(): pl.pallas_call(functools.partial(back_kernel, n, tiles, C), grid=(tiles,)...]
  transfers between devices with their start and end apart: 1 -> 0, of which waited for: 0 -> 0; matrix products, arithmetic and copies ran while one was open for 0% -> 0% of each run, Pallas kernels for 12% -> 0%
where the time goes in v3:
time: 271 us
  Pallas kernels  268 us (99%)
  local copies, waits for them, and re-layouts  2.72 us (1%)
    pallas_call x1, Pallas kernels, back_call(): pl.pallas_call(functools.partial(back_kernel, n, tiles, C), grid=(tiles,)...  112 us
    pallas_call x1, Pallas kernels, forward_call(): pl.pallas_call(functools.partial(forward_kernel, n, K, C), grid=(tiles +...  79.9 us
    pallas_call x1, Pallas kernels, edge_call(): pl.pallas_call(functools.partial(edge_kernel, tiles, C), grid=(tiles + 1,...  34.3 us
    pallas_call x1, Pallas kernels, node_back_call(): pl.pallas_call(functools.partial(node_back_kernel, n, C), in_specs=[WHOLE...  30.5 us
    pallas_call x1, Pallas kernels, unpack_call(): pl.pallas_call(functools.partial(unpack_kernel, C, steps), grid=(steps,),...  10.9 us

profile of v3, /device:TPU:0, one launch (start us, length us, event | category | flops | bytes accessed | tf_op | source)
XLA Modules:
  0.0 271.0 jit_solution(8325504876083814622)
XLA Ops:
  0.7 1.4 copy.41
  2.0 79.9 %shard_map.340 = (bf16[6656,512]{1,0:T(8,128)(2,1)}, bf16[6656,512]{1,0:T(8,128)(2,1)}, bf16[6656,512]{1,0:T(8,128)(2,1)}, s32[128,128]{1,0:T(8,128)}, s32[128,1...) custom-call(bf16[128,512]{1,0:T(8,128)(2,1)} %nodes.3, ...), custom_call_target="tpu_custom_call" | custom-call | tf_op jit(solution)/shard_map/pallas_call | solution.py:499
  81.9 34.3 %shard_map.341 = (bf16[128,9984]{1,0:T(8,128)(2,1)}, bf16[128,9984]{1,0:T(8,128)(2,1)}, bf16[1024,256]{1,0:T(8,128)(2,1)}, f32[128,256]{1,0:T(8,128)}, f32[192,2...) custom-call(s32[128,128]{1,0:T(8,128)} %get-tuple-element.71.tcol, ...), custom_call_target="tpu_custom_call" | custom-call | tf_op jit(solution)/shard_map/pallas_call | solution.py:672
  116.3 30.5 %shard_map.342 = (f32[128,512]{1,0:T(8,128)}, bf16[1024,512]{1,0:T(8,128)(2,1)}, bf16[128,1024]{1,0:T(8,128)(2,1)}, f32[32,512]{1,0:T(8,128)}, f32[512,512]{1,0:...) custom-call(bf16[1024,256]{1,0:T(8,128)(2,1)} %get-tuple-element.76.far_sum, f32[128,256]{1,0:T(8,128)} %get-tuple-element.77.near_sum, ...), custom_call_target="tpu_custom_call" | custom-call | tf_op jit(solution)/shard_map/pallas_call | solution.py:766
  146.7 111.9 %shard_map.343 = (bf16[128,9984]{1,0:T(8,128)(2,1)}, f32[128,512]{1,0:T(8,128)}, f32[8,512]{1,0:T(8,128)}, bf16[512,2048]{1,0:T(8,128)(2,1)}, bf16[2048,512]{1,0:T(8,128)(2,1)}, /*index=5*/bf16[3040,512]{1,0:T(8,128)(2,1)}) custom-call(s32[128,128]{1,0:T(8,128)} %get-tuple-element.71.tcol, s32[128,128]{1,0:T(8,128)} %get-tuple-element.72.trow, ...), custom_call_target="tpu_custom_call" | custom-call | tf_op jit(solution)/shard_map/pallas_call | solution.py:1144
  258.6 0.0 copy-start
  258.6 0.0 copy-start.1
  258.6 10.9 %shard_map.344 = (f32[1216,512]{1,0:T(8,128)}, f32[512,512]{1,0:T(8,128)}, f32[512,512]{1,0:T(8,128)}, f32[128,9984]{1,0:T(8,128)}, f32[192,1216]{1,0:T(8,128)},...) custom-call(bf16[3040,512]{1,0:T(8,128)(2,1)} %get-tuple-element.102, ...), custom_call_target="tpu_custom_call" | custom-call | tf_op jit(solution)/shard_map/pallas_call | solution.py:1344
  269.6 0.0 copy-done
  269.6 0.7 copy.44
  270.3 0.0 copy-done.1
  270.3 0.7 copy.45
Async XLA Ops:
  258.6 11.0 %copy-start = (bf16[128,512]{1,0:T(8,128)(2,1)S(1)}, bf16[128,512]{1,0:T(8,128)(2,1)}, u32[]{:S(2)}) copy-start(bf16[128,512]{1,0:T(8,128)(2,1)} %get-tuple-element.140.node_low) | copy-start | bytes 393220
  258.6 11.6 %copy-start.1 = (f32[128,512]{1,0:T(8,128)S(1)}, f32[128,512]{1,0:T(8,128)}, u32[]{:S(2)}) copy-start(f32[128,512]{1,0:T(8,128)} %get-tuple-element.142) | copy-start | bytes 786436

commit v4 on v3

--- a/solution.py
+++ b/solution.py
@@ -307,7 +307,7 @@
 
 def forward_kernel(
     n, K, C, nodes, owner, slot, live, g1, o1, g2, o2, w1_h, w2_h, w3_h, wf1_h, wf2_h, we1_h, edges,
-    act1, slope1, slope2, tcol, trow, node_out, near, low_out, n1_out, n2_out, inv_out, act_out,
+    act1, slope1, slope2, tcol, trow, node_out, near, low_out, n1_out, n2_out, inv_out,
     slope_out, sum_out, nodes_h, far_h,
     w1, w2, w3, wf1, wf2, we1, load_sem,
     nodes_all, far_all, lcol, orow, lrow, scol, hist, hist_got, count,
@@ -331,7 +331,8 @@
     def _():
         loads.start()
         spare = jnp.zeros((LANES - K, rows), I32)
-        own_wide = jnp.concatenate([owner[...], spare], axis=0)
+        own_rows = jnp.concatenate([owner[...], jnp.zeros((rows, LANES - K), I32)], axis=1)
+        own_wide = jnp.transpose(own_rows)
         slot_wide = jnp.concatenate([slot[...], spare], axis=0)
         live_wide = jnp.concatenate([live[...], spare], axis=0).astype(F32)
         target = own_wide * rows + slot_wide
@@ -436,7 +437,6 @@
         low = normed.astype(BF)
         low_out[...] = low
         act, slope = gelu_full(dot(low, wf1[...]))
-        act_out[...] = act
         slope_out[...] = slope
         n2, inv2 = norm_parts(normed + dot(act, wf2[...]))
         n2_out[...] = n2
@@ -491,7 +491,6 @@
         shape((rows, D), F32),
         shape((rows, D), F32),
         shape((3, rows, LANES), F32),
-        shape((rows, FF), BF),
         shape((rows, FF), BF),
         shape((rows, D), BF),
     ]
@@ -721,16 +720,10 @@
     return inverse * (scaled - row_mean(scaled) - normal * row_mean(scaled * normal))
 
 
-def node_back_kernel(
-    n, C, far_sum, near_sum, cot, node_low, n1, n2, inv, act, slope, low, summed,
-    w3, g1, wf1, wf2, g2, we1,
-    grad_one, vw_all, both, dgain, dw3, dwe_near, dwe_far,
-    pair_buf, far_buf, v_own, send, recv, gsend, grecv, own_sem,
+def node_back(
+    C, far, near_sum, cot, n1, n2, inv, slope, w3, g1, wf1, wf2, g2, we1, grad_one, resid_out, dgain, v_own
 ):
-    place = Place(n)
     rows, D = cot.shape
-    greet([place.sibling] + place.mates)
-    far = scatter_sum(place, far_sum, pair_buf, far_buf, send, recv)
     far = far.astype(BF)[:, :C]
     near = near_sum[...].astype(BF)[:, :C]
     grad = cot[...].astype(F32) + dot(near, we1[:, :D]) + dot(far, we1[:, D : 2 * D])
@@ -738,8 +731,7 @@
     dgain[16:24, :] = jnp.broadcast_to(jnp.sum(grad * n2[...], axis=0, keepdims=True), (8, D))
     dgain[24:32, :] = jnp.broadcast_to(jnp.sum(grad, axis=0, keepdims=True), (8, D))
     resid = two.astype(BF)
-    both[:, :D] = low[...]
-    both[:, D:] = resid
+    resid_out[...] = resid
     inner = (dot_nt(resid, wf2[...]) * slope[...].astype(F32)).astype(BF)
     grad = two + dot_nt(inner, wf1[...])
     one = norm_back(grad, n1[...], inv[0][:, 0:1], g1[...])
@@ -748,6 +740,23 @@
     grad_one[...] = one
     upper = (one / spread(inv[2], D)).astype(BF)
     v_own[...] = dot_nt(upper, w3[...]).astype(BF)
+    return far, near, upper
+
+
+def node_back_kernel(
+    n, C, far_sum, near_sum, cot, node_low, n1, n2, inv, slope, summed,
+    w3, g1, wf1, wf2, g2, we1,
+    grad_one, vw_all, resid_out, dgain, dw3, dwe_near, dwe_far,
+    pair_buf, far_buf, v_own, send, recv, gsend, grecv, own_sem,
+):
+    place = Place(n)
+    rows = cot.shape[0]
+    greet([place.sibling] + place.mates)
+    far = scatter_sum(place, far_sum, pair_buf, far_buf, send, recv)
+    far, near, upper = node_back(
+        C, far, near_sum, cot, n1, n2, inv, slope, w3, g1, wf1, wf2, g2, we1,
+        grad_one, resid_out, dgain, v_own,
+    )
     gather = Gather(place, v_own, vw_all, gsend, grecv)
     gather.start()
     own = pltpu.make_async_copy(v_own, block(vw_all, place.me, rows), own_sem.at[0])
@@ -760,7 +769,7 @@
 
 
 def node_back_call(n, C, *args):
-    cot, wf1 = args[2], args[13]
+    cot = args[2]
     rows, D = cot.shape
     shape = jax.ShapeDtypeStruct
     return pl.pallas_call(
@@ -770,7 +779,7 @@
         out_shape=[
             shape((rows, D), F32),
             shape((n * rows, D), BF),
-            shape((rows, 2 * D), BF),
+            shape((rows, D), BF),
             shape((32, D), F32),
             shape((D, D), F32),
             shape((D, C), F32),
@@ -943,19 +952,19 @@
         return total
 
 
-PIECES = 19
-LAG = 4
-
-
-def pack_sums(C, x, gains, dw1, dw2, dw3, dwe_near, dwe_far, dwe1, dwe2, dwe3, dgain, dg3):
+EARLY, LATE, LAG = 7, 9, 2
+SPREAD_AT = 0
+
+
+def early_rows(D, C):
+    used = D + (2 * D + C) // 2 + C
+    unit = 2 * EARLY * 16
+    return -(-used // unit) * unit
+
+
+def pack_early(C, x, gains, dw3, dwe_near, dwe_far, dwe1, dwe2, dwe3, dgain, dg3):
     D = dw3.shape[0]
-    at = 2 * D + C
-    if dw1 is not x:
-        x[:at, :] = dw1[...]
-        x[at : at + D, :] = dw2[...]
-    at += D
-    x[at : at + D, :] = dw3[...].astype(BF)
-    at += D
+    x[:D, :] = dw3[...].astype(BF)
     spare = jnp.zeros((D, 256 - C), F32)
     edge1 = jnp.concatenate(
         [
@@ -966,11 +975,13 @@
         axis=0,
     ).astype(BF)
     half = edge1.shape[0] // 2
-    x[at : at + half, :256] = edge1[:half]
-    x[at : at + half, 256:] = edge1[half:]
-    at += half
+    x[D : D + half, :256] = edge1[:half]
+    x[D : D + half, 256:] = edge1[half:]
+    at = D + half
     x[at : at + C, :256] = dwe2[:C, :].astype(BF)
     x[at : at + C, 256:] = dwe3[:C, :].astype(BF)
+    if at + C < x.shape[0]:
+        x[at + C :, :] = jnp.zeros((x.shape[0] - at - C, D), BF)
     gains[...] = jnp.zeros_like(gains)
     for r in range(4):
         gains[r : r + 1, :] = dgain[8 * r : 8 * r + 1, :]
@@ -1031,67 +1042,94 @@
     dw1[D : 2 * D, :] = a2[...].astype(BF)
 
 
-def tail(
-    place, n, line, scatter, exchange, source_sum, grad_one, w1, grad_nodes, small, feed,
-):
+def tail(early, late, scatter, source_sum, grad_one, w1, grad_nodes, feed):
     D = grad_one.shape[1]
-    line.start()
+    early.start()
+    late.start()
     scatter.start()
-    exchange.start()
-    scatter.pass_on()
 
     def feed_part(f):
-        both, wf1, wf2, dwf1, dwf2 = feed
+        low, resid, wf1, wf2, dwf1, dwf2 = feed
         step = 256
         cols = pl.ds(pl.multiple_of(f * step, step), step)
-        low, resid = both[:, :D], both[:, D:]
-        act, slope = gelu_full(dot(low, wf1[:, cols]))
-        dwf2[cols, :] = dot_tn(act, resid).astype(BF)
-        inner = (dot_nt(resid, wf2[cols, :]) * slope.astype(F32)).astype(BF)
-        dwf1[:, cols] = dot_tn(low, inner).astype(BF)
-
-    parts = feed[1].shape[1] // 256 if feed else 0
+        act, slope = gelu_full(dot(low[...], wf1[:, cols]))
+        dwf2[cols, :] = dot_tn(act, resid[...]).astype(BF)
+        inner = (dot_nt(resid[...], wf2[cols, :]) * slope.astype(F32)).astype(BF)
+        dwf1[:, cols] = dot_tn(low[...], inner).astype(BF)
+
+    parts = feed[2].shape[1] // 256 if feed else 0
 
     def slot(s, carry):
-        line.slot(s, LAG)
+        early.slot(s, LAG)
+        late.slot(s - EARLY, LAG)
         if feed:
             pl.when((s % 2 == 1) & (s // 2 < parts))(lambda: feed_part(s // 2))
         return carry
 
-    lax.fori_loop(0, line.slots(LAG), slot, 0)
+    first = SPREAD_AT
+    lax.fori_loop(0, first, slot, 0)
+    scatter.pass_on()
+    lax.fori_loop(first, EARLY + late.slots(LAG), slot, 0)
     source = dot_nt(source_sum[...].astype(BF), w1[:D, :])
     total = scatter.finish()
     grad_nodes[...] = grad_one[...] + source + dot_nt(total.astype(BF), w1[D : 2 * D, :])
-    small[...] = exchange.finish()
-    line.finish()
-
-
-def back_kernel(
-    n, tiles, C, tcol, trow, nodes, vw, w1, w2,
-    dw3, dwe_near, dwe_far, dwe1, dwe2, dwe3, dgain, dg3, both_own,
-    nodes_all_h, grad_one_h, wf1_h, wf2_h, act1, slope1, slope2, edges, partial,
-    grad_edges, grad_nodes, small, dwf1, dwf2, out_h,
-    nodes_all, grad_one, wf1, wf2, load_sem, both, bsend, brecv, out,
-    w2t, w_own, w_own_t, total, a2, ae, source_sum, target_sum, x, gains, got, gsend, grecv,
-    pair_buf, far_buf, send, recv, *line_refs,
-):
+    early.finish()
+    late.finish()
+
+
+def back_kernel(n, tiles, C, tcol, trow, nodes, near_sum, g1, g2, dwe1, dwe2, dwe3, dg3, *refs):
+    sources, refs = refs[:16], refs[16:]
+    act1, slope1, slope2, edges, partial, *refs = refs
+    grad_edges, grad_nodes, small, dwf1, dwf2, early_h, late_h, *refs = refs
+    held, refs = refs[:16], refs[16:]
+    (
+        far_sum, low_own, cot, we1, n2, inv, wf2, slope, wf1, n1, w3, w1, w2, summed, node_low, nodes_all
+    ) = held
+    (
+        load_sem, low, lsend, lrecv, vw, v_own, grad_one, resid_own, dgain, dw3, dwe_near, dwe_far,
+        resid, bsend, brecv, vsend, vrecv, hsend, hrecv, pair_h, far_h,
+        w2t, w_own, w_own_t, total, a2, ae, source_sum, target_sum, gains, got, gsend, grecv,
+        pair_buf, far_buf, send, recv, x1, out1, x2, out2, *line_refs,
+    ) = refs
     g = pl.program_id(0)
     rows, D = nodes.shape
     place = Place(n)
-    loads = Loads(
-        [(nodes_all_h, nodes_all), (grad_one_h, grad_one), (wf1_h, wf1), (wf2_h, wf2)], load_sem
-    )
-    gather = Gather(place, both_own, both, bsend, brecv)
-    keep_own = pltpu.make_async_copy(both_own, block(both, place.me, rows), load_sem.at[4])
+    loads = Loads(list(zip(sources, held)), load_sem)
+    gather = Gather(place, resid_own, resid, bsend, brecv)
+    gather_low = Gather(place, low_own, low, lsend, lrecv)
+    early = Line(place, EARLY, x1, out1, *line_refs[: len(line_refs) // 2])
+    late = Line(place, LATE, x2, out2, *line_refs[len(line_refs) // 2 :])
+    exchange = Exchange(place, n, gains, got, gsend, grecv)
 
     @pl.when(g == 0)
     def _():
         loads.start()
-        keep_own.start()
         greet([lax.rem(place.me + d, n) for d in range(1, n)])
-        gather.start()
+        loads.wait(0, 2)
+        scatter = Scatter(place, far_sum, pair_h, far_h, hsend, hrecv)
+        scatter.start()
+        scatter.pass_on()
+        mine = pl.ds(pl.multiple_of(place.me * rows, rows), rows)
+        low[mine, :] = low_own[...]
+        loads.wait(2, 15)
         back_start(C, w1, w2, w2t, w_own, w_own_t, (total, a2, ae, source_sum))
-
+        far, near, upper = node_back(
+            C, scatter.finish(), near_sum, cot, n1, n2, inv, slope, w3, g1, wf1, wf2, g2, we1,
+            grad_one, resid_own, dgain, v_own,
+        )
+        spread_v = Gather(place, v_own, vw, vsend, vrecv)
+        spread_v.start()
+        dw3[...] = dot_tn(summed[...], upper)
+        dwe_near[...] = dot_tn(node_low[...], near)
+        dwe_far[...] = dot_tn(node_low[...], far)
+        pack_early(C, x1, gains, dw3, dwe_near, dwe_far, dwe1, dwe2, dwe3, dgain, dg3)
+        vw[mine, :] = v_own[...]
+        resid[mine, :] = resid_own[...]
+        spread_v.finish()
+        exchange.start()
+
+    pl.when(g == 1)(gather_low.start)
+    pl.when(g == tiles // 2)(gather.start)
     back_tile(
         g, rows, C, tcol, trow, vw, act1, slope1, slope2, edges, partial, grad_edges,
         w2t, w_own_t, total, a2, ae, source_sum,
@@ -1100,41 +1138,37 @@
     @pl.when(g == tiles - 1)
     def _():
         target_sum[...] = total[...].astype(BF)
-        loads.wait()
-        keep_own.wait()
-        gather.finish()
+        loads.wait(15)
         at = 2 * D + C
         back_weights(
-            C, x.at[pl.ds(0, at)], x.at[pl.ds(at, D)], nodes_all, nodes, total, a2, ae, source_sum
+            C, x2.at[pl.ds(0, at)], x2.at[pl.ds(at, D)], nodes_all, nodes, total, a2, ae, source_sum
         )
-        pack_sums(C, x, gains, x, x, dw3, dwe_near, dwe_far, dwe1, dwe2, dwe3, dgain, dg3)
+        small[...] = exchange.finish()
+        gather_low.finish()
+        gather.finish()
+        scatter = Scatter(place, target_sum, pair_buf, far_buf, send, recv)
         tail(
-            place, n, Line(place, PIECES, x, out, *line_refs),
-            Scatter(place, target_sum, pair_buf, far_buf, send, recv),
-            Exchange(place, n, gains, got, gsend, grecv),
-            source_sum, grad_one, w1, grad_nodes, small, (both, wf1, wf2, dwf1, dwf2),
+            early, late, scatter, source_sum, grad_one, w1, grad_nodes, (low, resid, wf1, wf2, dwf1, dwf2)
         )
-        keep_out = pltpu.make_async_copy(out, out_h, load_sem.at[5])
-        keep_out.start()
-        keep_out.wait()
-
-
-def sum_rows(D, C):
-    return 4 * D + C + (2 * D + C) // 2 + C
-
-
-def back_call(n, C, tcol, trow, nodes, vw, w1, w2, sums, both_own, loaded, act1, slope1, slope2, edges, partial):
-    rows, D = nodes.shape
-    count = vw.shape[0]
+        keep_early = pltpu.make_async_copy(out1, early_h, load_sem.at[16])
+        keep_early.start()
+        keep_late = pltpu.make_async_copy(out2, late_h, load_sem.at[17])
+        keep_late.start()
+        keep_early.wait()
+        keep_late.wait()
+
+
+def back_call(n, C, whole, loaded, act1, slope1, slope2, edges, partial):
+    rows, D = whole[2].shape
+    count = n * rows
     K = edges.shape[1] // C
     tiles = K // GROUP
     size = GROUP * rows
-    FF = loaded[2].shape[1]
-    total = sum_rows(D, C)
+    FF = loaded[8].shape[1]
+    early, late = early_rows(D, C), 3 * D + C
     shape = jax.ShapeDtypeStruct
     slab = pl.BlockSpec((rows, GROUP * C), lambda g: (0, g))
     tile = pl.BlockSpec((size, D), lambda g: (g, 0))
-    whole = [tcol, trow, nodes, vw, w1, w2, *sums, both_own]
     outs = [
         shape((rows, D), F32),
         shape((8, D), F32),
@@ -1144,15 +1178,29 @@
     return pl.pallas_call(
         functools.partial(back_kernel, n, tiles, C),
         grid=(tiles,),
-        in_specs=[full(v) for v in whole] + [HBM] * 4 + [tile, tile, tile, slab, slab],
-        out_specs=[slab] + [fixed(*v.shape) for v in outs] + [HBM],
-        out_shape=[shape((rows, K * C), BF)] + outs + [shape((total, D), BF)],
+        in_specs=[full(v) for v in whole] + [HBM] * len(loaded) + [tile, tile, tile, slab, slab],
+        out_specs=[slab] + [fixed(*v.shape) for v in outs] + [HBM] * 2,
+        out_shape=[shape((rows, K * C), BF)]
+        + outs
+        + [shape((early, D), BF), shape((late, D), BF)],
         scratch_shapes=[pltpu.VMEM(v.shape, v.dtype) for v in loaded]
         + [
-            pltpu.SemaphoreType.DMA((6,)),
-            pltpu.VMEM((count, 2 * D), BF),
+            pltpu.SemaphoreType.DMA((18,)),
+            pltpu.VMEM((count, D), BF),
             *sems(n),
-            pltpu.VMEM((total, D), BF),
+            pltpu.VMEM((count, D), BF),
+            pltpu.VMEM((rows, D), BF),
+            pltpu.VMEM((rows, D), F32),
+            pltpu.VMEM((rows, D), BF),
+            pltpu.VMEM((32, D), F32),
+            pltpu.VMEM((D, D), F32),
+            pltpu.VMEM((D, C), F32),
+            pltpu.VMEM((D, C), F32),
+            pltpu.VMEM((count, D), BF),
+            *sems(n),
+            *sems(n),
+            *sems(n),
+            *comm_scratch(n, rows, 256),
             pltpu.VMEM((D, D), BF),
             pltpu.VMEM((2, 256, D), BF),
             pltpu.VMEM((2, D, 256), BF),
@@ -1161,13 +1209,17 @@
             pltpu.VMEM((2, 256, D), F32),
             pltpu.VMEM((rows, D), F32),
             pltpu.VMEM((count, D), BF),
-            pltpu.VMEM((total, D), BF),
             pltpu.VMEM((8, D), F32),
             pltpu.VMEM((n, 8, D), F32),
             *sems(n),
             *comm_scratch(n, rows, D),
             *sems(n),
-            *line_scratch(total, D, PIECES),
+            pltpu.VMEM((early, D), BF),
+            pltpu.VMEM((early, D), BF),
+            pltpu.VMEM((late, D), BF),
+            pltpu.VMEM((late, D), BF),
+            *line_scratch(early, D, EARLY),
+            *line_scratch(late, D, LATE),
         ],
         compiler_params=remote_params(3),
     )(*whole, *loaded, act1, slope1, slope2, edges, partial)
@@ -1230,37 +1282,49 @@
 
 def final_kernel(
     n, C, target_sum, source_sum, grad_one, w1, dw1, dw2, dw3, dwe_near, dwe_far, dwe1, dwe2, dwe3,
-    dgain, dg3, grad_nodes, out, small,
-    x, gains, got, gsend, grecv, pair_buf, far_buf, send, recv, *line_refs,
+    dgain, dg3, grad_nodes, out1, out2, small,
+    x1, x2, gains, got, gsend, grecv, pair_buf, far_buf, send, recv, *line_refs,
 ):
     place = Place(n)
+    D = grad_one.shape[1]
+    pack_early(C, x1, gains, dw3, dwe_near, dwe_far, dwe1, dwe2, dwe3, dgain, dg3)
+    at = 2 * D + C
+    x2[:at, :] = dw1[...]
+    x2[at:, :] = dw2[...]
     greet([lax.rem(place.me + d, n) for d in range(1, n)])
-    pack_sums(C, x, gains, dw1, dw2, dw3, dwe_near, dwe_far, dwe1, dwe2, dwe3, dgain, dg3)
-    tail(
-        place, n, Line(place, PIECES, x, out, *line_refs),
-        Scatter(place, target_sum, pair_buf, far_buf, send, recv),
-        Exchange(place, n, gains, got, gsend, grecv),
-        source_sum, grad_one, w1, grad_nodes, small, None,
-    )
+    early = Line(place, EARLY, x1, out1, *line_refs[: len(line_refs) // 2])
+    late = Line(place, LATE, x2, out2, *line_refs[len(line_refs) // 2 :])
+    exchange = Exchange(place, n, gains, got, gsend, grecv)
+    exchange.start()
+    small[...] = exchange.finish()
+    scatter = Scatter(place, target_sum, pair_buf, far_buf, send, recv)
+    tail(early, late, scatter, source_sum, grad_one, w1, grad_nodes, None)
 
 
 def final_call(n, C, args):
     rows, D = args[2].shape
-    size = sum_rows(D, C)
+    early, late = early_rows(D, C), 3 * D + C
     shape = jax.ShapeDtypeStruct
     return pl.pallas_call(
         functools.partial(final_kernel, n, C),
         in_specs=[WHOLE] * len(args),
-        out_specs=[WHOLE] * 3,
-        out_shape=[shape((rows, D), F32), shape((size, D), BF), shape((8, D), F32)],
+        out_specs=[WHOLE] * 4,
+        out_shape=[
+            shape((rows, D), F32),
+            shape((early, D), BF),
+            shape((late, D), BF),
+            shape((8, D), F32),
+        ],
         scratch_shapes=[
-            pltpu.VMEM((size, D), BF),
+            pltpu.VMEM((early, D), BF),
+            pltpu.VMEM((late, D), BF),
             pltpu.VMEM((8, D), F32),
             pltpu.VMEM((n, 8, D), F32),
             *sems(n),
             *comm_scratch(n, rows, D),
             *sems(n),
-            *line_scratch(size, D, PIECES),
+            *line_scratch(early, D, EARLY),
+            *line_scratch(late, D, LATE),
         ],
         compiler_params=remote_params(4),
     )(*args)
@@ -1278,8 +1342,8 @@
     dwf1[...] += dot_tn(low[...], inner)
 
 
-def feed_call(both, wf1, wf2):
-    count = both.shape[0]
+def feed_call(low, resid, wf1, wf2):
+    count = low.shape[0]
     D, FF = wf1.shape
     step, rows = min(FF, 512), min(count, TABLE)
     shape = jax.ShapeDtypeStruct
@@ -1288,7 +1352,7 @@
         grid=(FF // step, count // rows),
         in_specs=[
             pl.BlockSpec((rows, D), lambda f, r: (r, 0)),
-            pl.BlockSpec((rows, D), lambda f, r: (r, 1)),
+            pl.BlockSpec((rows, D), lambda f, r: (r, 0)),
             pl.BlockSpec((D, step), lambda f, r: (0, f)),
             pl.BlockSpec((step, D), lambda f, r: (f, 0)),
         ],
@@ -1298,21 +1362,21 @@
         ],
         out_shape=[shape((D, FF), F32), shape((FF, D), F32)],
         compiler_params=LOCAL,
-    )(both, both, wf1, wf2)
-
-
-def unpack_kernel(C, steps, packed, small, edges, *refs):
+    )(low, resid, wf1, wf2)
+
+
+def unpack_kernel(C, steps, late, packed, small, node_in, grad_in, edges, *refs):
     g = pl.program_id(0)
-    D = packed.shape[1]
-    plain = refs[: (len(refs) - 13) // 2]
-    w1, w2, w3, grad_edges, one, two, three, *outs = refs[len(plain) :]
+    D = late.shape[1]
+    plain = refs[: (len(refs) - 15) // 2]
+    w1, w2, w3, grad_edges, one, two, three, node_out, grad_nodes, *outs = refs[len(plain) :]
     gains = outs[len(plain) :]
     grad_edges[...] = edges[...].astype(F32)
-    at = 0
-    for ref, size in ((w1, 2 * D + C), (w2, D), (w3, D)):
-        step = size // steps
-        ref[...] = packed[pl.ds(pl.multiple_of(at + g * step, 16), step), :].astype(F32)
-        at += size
+    first = 2 * D + C
+    for ref, src, base in ((w1, late, 0), (w2, late, first), (w3, packed, 0)):
+        step = ref.shape[0]
+        ref[...] = src[pl.ds(pl.multiple_of(base + g * step, 16), step), :].astype(F32)
+    at = D
     for a, b in zip(plain, outs):
         b[...] = a[...].astype(F32)
 
@@ -1326,12 +1390,14 @@
         end = at + half
         two[...] = packed[end : end + C, :C].astype(F32)
         three[...] = packed[end : end + C, 256 : 256 + C].astype(F32)
+        node_out[...] = node_in[...]
+        grad_nodes[...] = grad_in[...]
         for r in range(6):
             width = D if r < 4 else C
             gains[r][...] = small[r : r + 1, :width]
 
 
-def unpack_call(C, packed, small, edges, arrays):
+def unpack_call(C, late, packed, small, node_out, grad_nodes, edges, arrays):
     steps = 4
     D = packed.shape[1]
     first = 2 * D + C
@@ -1344,14 +1410,17 @@
     return pl.pallas_call(
         functools.partial(unpack_kernel, C, steps),
         grid=(steps,),
-        in_specs=[full(packed), full(small)] + [cut(*v.shape) for v in (edges, *arrays)],
+        in_specs=[full(v) for v in (late, packed, small, node_out, grad_nodes)] + [cut(*v.shape) for v in (edges, *arrays)],
         out_specs=[cut(*v) for v in head]
         + [fixed(*v) for v in last]
+        + [fixed(*node_out.shape)] * 2
         + [cut(*v) for v in plain]
         + [fixed(*v) for v in gains],
-        out_shape=[shape(v, F32) for v in head + last + plain + gains],
+        out_shape=[shape(v, F32) for v in head + last]
+        + [shape(node_out.shape, BF), shape(node_out.shape, F32)]
+        + [shape(v, F32) for v in plain + gains],
         compiler_params=LOCAL,
-    )(packed, small, edges, *arrays)
+    )(late, packed, small, node_out, grad_nodes, edges, *arrays)
 
 
 def body(
@@ -1365,42 +1434,46 @@
     we1 = w_edge1.T
     g1, o1, g2, o2 = (v.reshape(1, D) for v in (gain_one, offset_one, gain_two, offset_two))
     (
-        act1, slope1, slope2, tcol, trow, node_out, near, low, n1, n2, inv, act, slope, own_sum,
+        act1, slope1, slope2, tcol, trow, node_out, near, low, n1, n2, inv, slope, own_sum,
         nodes_all, far_all,
     ) = forward_call(
-        n, C, nodes, nbr_owner[:, :, 0].T, nbr_slot.T, edge_mask.T, g1, o1, g2, o2,
+        n, C, nodes, nbr_owner[:, :, 0], nbr_slot.T, edge_mask.T, g1, o1, g2, o2,
         [w_msg1, w_msg2, w_msg3, w_ffn1, w_ffn2, we1], edges,
     )
     edge_out, partial, far_sum, near_sum, dwe1, dwe2, dwe3, dg3 = edge_call(
         C, tcol, trow, far_all, near, we1, w_edge2, w_edge3,
         gain_three.reshape(1, C), offset_three.reshape(1, C), edges, edge_cotangent,
     )
-    grad_one, vw_all, both, dgain, dw3, dwe_near, dwe_far = node_back_call(
-        n, C, far_sum, near_sum, node_cotangent, node_out, n1, n2, inv, act, slope, low, own_sum,
-        w_msg3, g1, w_ffn1, w_ffn2, g2, we1,
-    )
-    sums = [dw3, dwe_near, dwe_far, dwe1, dwe2, dwe3, dgain, dg3]
     kept = [act1, slope1, slope2, edges, partial]
     if n * rows <= TABLE:
-        grad_edges, grad_nodes, small, *dwf, packed = back_call(
-            n, C, tcol, trow, nodes, vw_all, w_msg1, w_msg2, sums, both,
-            [nodes_all, grad_one, w_ffn1, w_ffn2], *kept,
-        )
-        tot1, tot2, tot3, grad_edges, we1_t, tot_e2, tot_e3, dwf1, dwf2, *gains = unpack_call(
-            C, packed, small, grad_edges, dwf
+        grad_edges, grad_nodes, small, *dwf, early, late = back_call(
+            n, C, [tcol, trow, nodes, near_sum, g1, g2, dwe1, dwe2, dwe3, dg3],
+            [
+                far_sum, low, node_cotangent, we1, n2, inv, w_ffn2, slope, w_ffn1, n1, w_msg3, w_msg1,
+                w_msg2, own_sum, node_out, nodes_all,
+            ],
+            *kept,
         )
     else:
+        grad_one, vw_all, resid, dgain, dw3, dwe_near, dwe_far = node_back_call(
+            n, C, far_sum, near_sum, node_cotangent, node_out, n1, n2, inv, slope, own_sum,
+            w_msg3, g1, w_ffn1, w_ffn2, g2, we1,
+        )
+        sums = [dw3, dwe_near, dwe_far, dwe1, dwe2, dwe3, dgain, dg3]
         grad_edges, dw1, dw2, target_sum, source_sum = message_back_call(
             C, tcol, trow, nodes_all, nodes, vw_all, w_msg1, w_msg2, *kept
         )
-        grad_nodes, packed, small = final_call(
+        grad_nodes, early, late, small = final_call(
             n, C, [target_sum, source_sum, grad_one, w_msg1, dw1, dw2, *sums]
         )
-        tot1, tot2, tot3, grad_edges, we1_t, tot_e2, tot_e3, *gains = unpack_call(
-            C, packed, small, grad_edges, []
-        )
-        both = lax.all_gather(both, "edge", axis=0, tiled=True)
-        dwf1, dwf2 = feed_call(both, w_ffn1, w_ffn2)
+        low, resid = (lax.all_gather(v, "edge", axis=0, tiled=True) for v in (low, resid))
+        tot_dwf = feed_call(low, resid, w_ffn1, w_ffn2)
+        dwf = []
+    (
+        tot1, tot2, tot3, grad_edges, we1_t, tot_e2, tot_e3, node_out, grad_nodes, *rest
+    ) = unpack_call(C, late, early, small, node_out, grad_nodes, grad_edges, dwf)
+    dwf1, dwf2 = rest[:2] if dwf else tot_dwf
+    gains = rest[-6:]
     gains = [v.reshape(v.shape[1]) for v in gains]
     return (
         node_out, edge_out, grad_nodes, grad_edges,

time: 271 us -> 259 us (0.956)
  Pallas kernels: 268 us -> 256 us
    pallas_call x1 -> x0, Pallas kernels: 30.5 us -> none  [node_back_call(): pl.pallas_call(functools.partial(node_back_kernel, n, C), in_specs=[WHOLE...]
    pallas_call x1, Pallas kernels: 112 us -> 131 us  [back_call(): pl.pallas_call(functools.partial(back_kernel, n, tiles, C), grid=(tiles,)...]
where the time goes in v4:
time: 259 us
  Pallas kernels  256 us (99%)
    pallas_call x1, Pallas kernels, back_call(): pl.pallas_call(functools.partial(back_kernel, n, tiles, C), grid=(tiles,)...  131 us
    pallas_call x1, Pallas kernels, forward_call(): pl.pallas_call(functools.partial(forward_kernel, n, K, C), grid=(tiles +...  79.7 us
    pallas_call x1, Pallas kernels, edge_call(): pl.pallas_call(functools.partial(edge_kernel, tiles, C), grid=(tiles + 1,...  34.4 us
    pallas_call x1, Pallas kernels, unpack_call(): pl.pallas_call(functools.partial(unpack_kernel, C, steps), grid=(steps,),...  10.9 us

profile of v4, /device:TPU:0, one launch (start us, length us, event | category | flops | bytes accessed | tf_op | source)
XLA Modules:
  0.0 258.7 jit_solution(5017140874983855525)
XLA Ops:
  0.7 1.5 copy.39
  2.1 79.7 %shard_map.340 = (bf16[6656,512]{1,0:T(8,128)(2,1)}, bf16[6656,512]{1,0:T(8,128)(2,1)}, bf16[6656,512]{1,0:T(8,128)(2,1)}, s32[128,128]{1,0:T(8,128)}, s32[128,1...) custom-call(bf16[128,512]{1,0:T(8,128)(2,1)} %nodes.3, ...), custom_call_target="tpu_custom_call" | custom-call | tf_op jit(solution)/shard_map/pallas_call | solution.py:498
  81.8 34.4 %shard_map.341 = (bf16[128,9984]{1,0:T(8,128)(2,1)}, bf16[128,9984]{1,0:T(8,128)(2,1)}, bf16[1024,256]{1,0:T(8,128)(2,1)}, f32[128,256]{1,0:T(8,128)}, f32[192,2...) custom-call(s32[128,128]{1,0:T(8,128)} %get-tuple-element.65.tcol, ...), custom_call_target="tpu_custom_call" | custom-call | tf_op jit(solution)/shard_map/pallas_call | solution.py:671
  116.2 131.4 %shard_map.342 = (bf16[128,9984]{1,0:T(8,128)(2,1)}, f32[128,512]{1,0:T(8,128)}, f32[8,512]{1,0:T(8,128)}, bf16[512,2048]{1,0:T(8,128)(2,1)}, bf16[2048,512]{1,0...) custom-call(s32[128,128]{1,0:T(8,128)} %get-tuple-element.65.tcol, ...), custom_call_target="tpu_custom_call" | custom-call | tf_op jit(solution)/shard_map/pallas_call | solution.py:1178
  247.6 10.9 %shard_map.343 = (f32[1216,512]{1,0:T(8,128)}, f32[512,512]{1,0:T(8,128)}, f32[512,512]{1,0:T(8,128)}, f32[128,9984]{1,0:T(8,128)}, f32[192,1216]{1,0:T(8,128)},...) custom-call(bf16[1728,512]{1,0:T(8,128)(2,1)} %get-tuple-element.87., ...), custom_call_target="tpu_custom_call" | custom-call | tf_op jit(solution)/shard_map/pallas_call | solution.py:1410

commit v5 on v4

--- a/solution.py
+++ b/solution.py
@@ -331,13 +331,14 @@
     def _():
         loads.start()
         spare = jnp.zeros((LANES - K, rows), I32)
-        own_rows = jnp.concatenate([owner[...], jnp.zeros((rows, LANES - K), I32)], axis=1)
-        own_wide = jnp.transpose(own_rows)
+        for k in range(K):
+            orow[k : k + 1, :] = owner[k]
+        orow[K:, :] = spare
+        own_wide = orow[...]
         slot_wide = jnp.concatenate([slot[...], spare], axis=0)
         live_wide = jnp.concatenate([live[...], spare], axis=0).astype(F32)
         target = own_wide * rows + slot_wide
         trow[...] = target
-        orow[...] = own_wide
         lrow[...] = live_wide
         tcol[...] = jnp.transpose(target)
         lcol[...] = jnp.transpose(live_wide)
@@ -952,8 +953,7 @@
         return total
 
 
-EARLY, LATE, LAG = 7, 9, 2
-SPREAD_AT = 0
+EARLY, LATE, LAG, AHEAD = 7, 9, 2, 7
 
 
 def early_rows(D, C):
@@ -1044,7 +1044,6 @@
 
 def tail(early, late, scatter, source_sum, grad_one, w1, grad_nodes, feed):
     D = grad_one.shape[1]
-    early.start()
     late.start()
     scatter.start()
 
@@ -1063,13 +1062,12 @@
         early.slot(s, LAG)
         late.slot(s - EARLY, LAG)
         if feed:
-            pl.when((s % 2 == 1) & (s // 2 < parts))(lambda: feed_part(s // 2))
+            f = s - AHEAD
+            pl.when((f % 2 == 1) & (f // 2 < parts))(lambda: feed_part(f // 2))
         return carry
 
-    first = SPREAD_AT
-    lax.fori_loop(0, first, slot, 0)
     scatter.pass_on()
-    lax.fori_loop(first, EARLY + late.slots(LAG), slot, 0)
+    lax.fori_loop(AHEAD, EARLY + late.slots(LAG), slot, 0)
     source = dot_nt(source_sum[...].astype(BF), w1[:D, :])
     total = scatter.finish()
     grad_nodes[...] = grad_one[...] + source + dot_nt(total.astype(BF), w1[D : 2 * D, :])
@@ -1127,9 +1125,12 @@
         resid[mine, :] = resid_own[...]
         spread_v.finish()
         exchange.start()
+        early.start()
 
     pl.when(g == 1)(gather_low.start)
-    pl.when(g == tiles // 2)(gather.start)
+    pl.when(g == 4)(gather.start)
+    ahead = g - (tiles - AHEAD)
+    pl.when(ahead >= 0)(lambda: early.slot(ahead, LAG))
     back_tile(
         g, rows, C, tcol, trow, vw, act1, slope1, slope2, edges, partial, grad_edges,
         w2t, w_own_t, total, a2, ae, source_sum,
@@ -1298,6 +1299,8 @@
     exchange.start()
     small[...] = exchange.finish()
     scatter = Scatter(place, target_sum, pair_buf, far_buf, send, recv)
+    early.start()
+    lax.fori_loop(0, AHEAD, lambda s, z: (early.slot(s, LAG), z)[1], 0)
     tail(early, late, scatter, source_sum, grad_one, w1, grad_nodes, None)
 
 
@@ -1437,7 +1440,7 @@
         act1, slope1, slope2, tcol, trow, node_out, near, low, n1, n2, inv, slope, own_sum,
         nodes_all, far_all,
     ) = forward_call(
-        n, C, nodes, nbr_owner[:, :, 0], nbr_slot.T, edge_mask.T, g1, o1, g2, o2,
+        n, C, nodes, nbr_owner.transpose(1, 2, 0), nbr_slot.T, edge_mask.T, g1, o1, g2, o2,
         [w_msg1, w_msg2, w_msg3, w_ffn1, w_ffn2, we1], edges,
     )
     edge_out, partial, far_sum, near_sum, dwe1, dwe2, dwe3, dg3 = edge_call(

time: 259 us -> 250 us (0.965)
  Pallas kernels: 256 us -> 249 us
    pallas_call x1, Pallas kernels: 131 us -> 124 us  [back_call(): pl.pallas_call(functools.partial(back_kernel, n, tiles, C), grid=(tiles,)...]
where the time goes in v5:
time: 250 us
  Pallas kernels  249 us (100%)
    pallas_call x1, Pallas kernels, back_call(): pl.pallas_call(functools.partial(back_kernel, n, tiles, C), grid=(tiles,)...  124 us
    pallas_call x1, Pallas kernels, forward_call(): pl.pallas_call(functools.partial(forward_kernel, n, K, C), grid=(tiles +...  79.9 us
    pallas_call x1, Pallas kernels, edge_call(): pl.pallas_call(functools.partial(edge_kernel, tiles, C), grid=(tiles + 1,...  34.4 us
    pallas_call x1, Pallas kernels, unpack_call(): pl.pallas_call(functools.partial(unpack_kernel, C, steps), grid=(steps,),...  10.9 us

profile of v5, /device:TPU:0, one launch (start us, length us, event | category | flops | bytes accessed | tf_op | source)
XLA Modules:
  0.0 249.7 jit_solution(3022555585588667649)
XLA Ops:
  0.7 79.9 %shard_map.340 = (bf16[6656,512]{1,0:T(8,128)(2,1)}, bf16[6656,512]{1,0:T(8,128)(2,1)}, bf16[6656,512]{1,0:T(8,128)(2,1)}, s32[128,128]{1,0:T(8,128)}, s32[128,1...) custom-call(bf16[128,512]{1,0:T(8,128)(2,1)} %nodes.3, ...), custom_call_target="tpu_custom_call" | custom-call | tf_op jit(solution)/shard_map/pallas_call | solution.py:499
  80.5 34.4 %shard_map.341 = (bf16[128,9984]{1,0:T(8,128)(2,1)}, bf16[128,9984]{1,0:T(8,128)(2,1)}, bf16[1024,256]{1,0:T(8,128)(2,1)}, f32[128,256]{1,0:T(8,128)}, f32[192,2...) custom-call(s32[128,128]{1,0:T(8,128)} %get-tuple-element.65.tcol, ...), custom_call_target="tpu_custom_call" | custom-call | tf_op jit(solution)/shard_map/pallas_call | solution.py:672
  114.9 123.7 %shard_map.342 = (bf16[128,9984]{1,0:T(8,128)(2,1)}, f32[128,512]{1,0:T(8,128)}, f32[8,512]{1,0:T(8,128)}, bf16[512,2048]{1,0:T(8,128)(2,1)}, bf16[2048,512]{1,0...) custom-call(s32[128,128]{1,0:T(8,128)} %get-tuple-element.65.tcol, ...), custom_call_target="tpu_custom_call" | custom-call | tf_op jit(solution)/shard_map/pallas_call | solution.py:1179
  238.6 10.9 %shard_map.343 = (f32[1216,512]{1,0:T(8,128)}, f32[512,512]{1,0:T(8,128)}, f32[512,512]{1,0:T(8,128)}, f32[128,9984]{1,0:T(8,128)}, f32[192,1216]{1,0:T(8,128)},...) custom-call(bf16[1728,512]{1,0:T(8,128)(2,1)} %get-tuple-element.87., ...), custom_call_target="tpu_custom_call" | custom-call | tf_op jit(solution)/shard_map/pallas_call | solution.py:1413

commit v6 on v5

--- a/solution.py
+++ b/solution.py
@@ -587,7 +587,7 @@
         inverse = lax.rsqrt(mean(centred * centred) + EPS)
         normal = centred * inverse
         outs.append(normal * gains[s, 0:1] + gains[s, 1:2])
-        upstream = keep(cots[s].astype(F32)) * valid
+        upstream = cots[s].astype(F32) * valid
         moved = upstream * normal
         for r in range(half // rows):
             part = slice(r * rows, (r + 1) * rows)
@@ -1066,8 +1066,9 @@
             pl.when((f % 2 == 1) & (f // 2 < parts))(lambda: feed_part(f // 2))
         return carry
 
+    lax.fori_loop(AHEAD, AHEAD + 14, slot, 0)
     scatter.pass_on()
-    lax.fori_loop(AHEAD, EARLY + late.slots(LAG), slot, 0)
+    lax.fori_loop(AHEAD + 14, EARLY + late.slots(LAG), slot, 0)
     source = dot_nt(source_sum[...].astype(BF), w1[:D, :])
     total = scatter.finish()
     grad_nodes[...] = grad_one[...] + source + dot_nt(total.astype(BF), w1[D : 2 * D, :])
@@ -1401,7 +1402,7 @@
 
 
 def unpack_call(C, late, packed, small, node_out, grad_nodes, edges, arrays):
-    steps = 4
+    steps = 2
     D = packed.shape[1]
     first = 2 * D + C
     shape = jax.ShapeDtypeStruct

time: 250 us -> 244 us (0.976)
  Pallas kernels: 249 us -> 243 us
    pallas_call x1, Pallas kernels: 124 us -> 118 us  [back_call(): pl.pallas_call(functools.partial(back_kernel, n, tiles, C), grid=(tiles,)...]
where the time goes in v6:
time: 244 us
  Pallas kernels  243 us (100%)
    pallas_call x1, Pallas kernels, back_call(): pl.pallas_call(functools.partial(back_kernel, n, tiles, C), grid=(tiles,)...  118 us
    pallas_call x1, Pallas kernels, forward_call(): pl.pallas_call(functools.partial(forward_kernel, n, K, C), grid=(tiles +...  79.9 us
    pallas_call x1, Pallas kernels, edge_call(): pl.pallas_call(functools.partial(edge_kernel, tiles, C), grid=(tiles + 1,...  34.3 us
    pallas_call x1, Pallas kernels, unpack_call(): pl.pallas_call(functools.partial(unpack_kernel, C, steps), grid=(steps,),...  11 us

profile of v6, /device:TPU:0, one launch (start us, length us, event | category | flops | bytes accessed | tf_op | source)
XLA Modules:
  0.0 243.9 jit_solution(7563112280861050578)
XLA Ops:
  0.7 79.9 %shard_map.340 = (bf16[6656,512]{1,0:T(8,128)(2,1)}, bf16[6656,512]{1,0:T(8,128)(2,1)}, bf16[6656,512]{1,0:T(8,128)(2,1)}, s32[128,128]{1,0:T(8,128)}, s32[128,1...) custom-call(bf16[128,512]{1,0:T(8,128)(2,1)} %nodes.3, ...), custom_call_target="tpu_custom_call" | custom-call | tf_op jit(solution)/shard_map/pallas_call | solution.py:499
  80.5 34.3 %shard_map.341 = (bf16[128,9984]{1,0:T(8,128)(2,1)}, bf16[128,9984]{1,0:T(8,128)(2,1)}, bf16[1024,256]{1,0:T(8,128)(2,1)}, f32[128,256]{1,0:T(8,128)}, f32[192,2...) custom-call(s32[128,128]{1,0:T(8,128)} %get-tuple-element.65.tcol, ...), custom_call_target="tpu_custom_call" | custom-call | tf_op jit(solution)/shard_map/pallas_call | solution.py:672
  114.8 118.0 %shard_map.342 = (bf16[128,9984]{1,0:T(8,128)(2,1)}, f32[128,512]{1,0:T(8,128)}, f32[8,512]{1,0:T(8,128)}, bf16[512,2048]{1,0:T(8,128)(2,1)}, bf16[2048,512]{1,0...) custom-call(s32[128,128]{1,0:T(8,128)} %get-tuple-element.65.tcol, ...), custom_call_target="tpu_custom_call" | custom-call | tf_op jit(solution)/shard_map/pallas_call | solution.py:1180
  232.8 11.0 %shard_map.343 = (f32[1216,512]{1,0:T(8,128)}, f32[512,512]{1,0:T(8,128)}, f32[512,512]{1,0:T(8,128)}, f32[128,9984]{1,0:T(8,128)}, f32[192,1216]{1,0:T(8,128)},...) custom-call(bf16[1728,512]{1,0:T(8,128)(2,1)} %get-tuple-element.87., ...), custom_call_target="tpu_custom_call" | custom-call | tf_op jit(solution)/shard_map/pallas_call | solution.py:1414

commit v7 on v6

--- a/solution.py
+++ b/solution.py
@@ -1042,10 +1042,12 @@
     dw1[D : 2 * D, :] = a2[...].astype(BF)
 
 
-def tail(early, late, scatter, source_sum, grad_one, w1, grad_nodes, feed):
+def tail(early, late, scatter, source_sum, grad_one, w1, grad_nodes, feed, ready=None):
     D = grad_one.shape[1]
     late.start()
     scatter.start()
+    if ready:
+        ready()
 
     def feed_part(f):
         low, resid, wf1, wf2, dwf1, dwf2 = feed
@@ -1145,12 +1147,16 @@
         back_weights(
             C, x2.at[pl.ds(0, at)], x2.at[pl.ds(at, D)], nodes_all, nodes, total, a2, ae, source_sum
         )
-        small[...] = exchange.finish()
-        gather_low.finish()
-        gather.finish()
+
+        def ready():
+            gather_low.finish()
+            gather.finish()
+            small[...] = exchange.finish()
+
         scatter = Scatter(place, target_sum, pair_buf, far_buf, send, recv)
         tail(
-            early, late, scatter, source_sum, grad_one, w1, grad_nodes, (low, resid, wf1, wf2, dwf1, dwf2)
+            early, late, scatter, source_sum, grad_one, w1, grad_nodes, (low, resid, wf1, wf2, dwf1, dwf2),
+            ready,
         )
         keep_early = pltpu.make_async_copy(out1, early_h, load_sem.at[16])
         keep_early.start()

time: 244 us -> 246 us (level)
  no operation moved by 1% of the time
where the time goes in v7:
time: 246 us
  Pallas kernels  245 us (100%)
    pallas_call x1, Pallas kernels, back_call(): pl.pallas_call(functools.partial(back_kernel, n, tiles, C), grid=(tiles,)...  120 us
    pallas_call x1, Pallas kernels, forward_call(): pl.pallas_call(functools.partial(forward_kernel, n, K, C), grid=(tiles +...  79.9 us
    pallas_call x1, Pallas kernels, edge_call(): pl.pallas_call(functools.partial(edge_kernel, tiles, C), grid=(tiles + 1,...  34.3 us
    pallas_call x1, Pallas kernels, unpack_call(): pl.pallas_call(functools.partial(unpack_kernel, C, steps), grid=(steps,),...  11 us

profile of v7, /device:TPU:0, one launch (start us, length us, event | category | flops | bytes accessed | tf_op | source)
XLA Modules:
  0.0 246.0 jit_solution(7128641308638468094)
XLA Ops:
  0.7 79.9 %shard_map.340 = (bf16[6656,512]{1,0:T(8,128)(2,1)}, bf16[6656,512]{1,0:T(8,128)(2,1)}, bf16[6656,512]{1,0:T(8,128)(2,1)}, s32[128,128]{1,0:T(8,128)}, s32[128,1...) custom-call(bf16[128,512]{1,0:T(8,128)(2,1)} %nodes.3, ...), custom_call_target="tpu_custom_call" | custom-call | tf_op jit(solution)/shard_map/pallas_call | solution.py:499
  80.5 34.3 %shard_map.341 = (bf16[128,9984]{1,0:T(8,128)(2,1)}, bf16[128,9984]{1,0:T(8,128)(2,1)}, bf16[1024,256]{1,0:T(8,128)(2,1)}, f32[128,256]{1,0:T(8,128)}, f32[192,2...) custom-call(s32[128,128]{1,0:T(8,128)} %get-tuple-element.65.tcol, ...), custom_call_target="tpu_custom_call" | custom-call | tf_op jit(solution)/shard_map/pallas_call | solution.py:672
  114.8 120.0 %shard_map.342 = (bf16[128,9984]{1,0:T(8,128)(2,1)}, f32[128,512]{1,0:T(8,128)}, f32[8,512]{1,0:T(8,128)}, bf16[512,2048]{1,0:T(8,128)(2,1)}, bf16[2048,512]{1,0...) custom-call(s32[128,128]{1,0:T(8,128)} %get-tuple-element.65.tcol, ...), custom_call_target="tpu_custom_call" | custom-call | tf_op jit(solution)/shard_map/pallas_call | solution.py:1186
  234.8 11.0 %shard_map.343 = (f32[1216,512]{1,0:T(8,128)}, f32[512,512]{1,0:T(8,128)}, f32[512,512]{1,0:T(8,128)}, f32[128,9984]{1,0:T(8,128)}, f32[192,1216]{1,0:T(8,128)},...) custom-call(bf16[1728,512]{1,0:T(8,128)(2,1)} %get-tuple-element.87., ...), custom_call_target="tpu_custom_call" | custom-call | tf_op jit(solution)/shard_map/pallas_call | solution.py:1420
